TPU v7x, 32 devices: a whole 2x2x4 slice. The times are simulated.
32 devices in a mesh: row: 4 (over y, x), col: 8 (over z, core).
Axes of the slice: x: 2, y: 2, z: 4, core: 2. Of those that a mesh axis runs over, the one named last changes fastest.
Arguments:
- amplitudes: bfloat16 [8000, 2800], P('row', 'col'), may hold values from -6 to 6
- values_stored: bfloat16 [2800, 11200], P('row', 'col'), may hold values from -0.109375 to 0.109375
- irrep_virtual: int32 [1400], replicated, may hold values from 0 to 7
- residual_in: float32 [8000, 11200], P('row', 'col'), may hold values from -6 to 6
Outputs:
- residual_out: float32 [8000, 11200], P('row', 'col')
Inputs may be any that keep to these rules, and one draw needn't show every extreme that they name: `irrep_virtual`: labels of the eight irreducible representations of D2h.
All inputs are finite; a program needn't handle non-finite values.
Results may differ from a plain program's by a relative error of at most 0.0003.
Values may be sent and summed in bfloat16 or wider, within the bound.
No kernel may reach another device: no remote copies, remote signals or barrier semaphores. Data moves between devices by JAX's collectives and lax.ppermute only.
A program may use at most 128 MiB of HBM per device.

v0:
```python
import jax
import jax.numpy as jnp
from jax import lax
from jax.sharding import PartitionSpec as P

C_SLAB = 2


def stored_order(irrep_virtual):
    pair_irrep = jnp.bitwise_xor(irrep_virtual[:C_SLAB][:, None], irrep_virtual[None, :]).reshape(
        -1
    )
    count_pairs = pair_irrep.shape[0]
    sort_key = pair_irrep * count_pairs + jnp.arange(count_pairs, dtype=jnp.int32)
    return jnp.argsort(sort_key)


def on_device(amplitudes, values_stored, irrep_virtual, residual_in):
    stored = stored_order(irrep_virtual)
    gathered = lax.all_gather(amplitudes, "col", axis=1, tiled=True)
    sorted_columns = jnp.take(gathered, stored, axis=1)
    return residual_in + jnp.dot(
        sorted_columns,
        lax.all_gather(values_stored, "row", axis=0, tiled=True),
        preferred_element_type=jnp.float32,
    )


def solution(mesh):
    in_specs = (P("row", "col"), P("row", "col"), P(), P("row", "col"))
    out_specs = P("row", "col")
    return jax.shard_map(
        on_device, mesh=mesh, in_specs=in_specs, out_specs=out_specs, check_vma=False
    )
```

profile of v0, /device:TPU:0, one launch (start us, length us, event | category | flops | bytes accessed | tf_op | source)
XLA Modules:
  0.0 281.4 jit_solution(5661429530017848441)
XLA Ops:
  6.5 0.0 all-gather.7.cloned.1.call-start
  6.5 0.7 all-gather.7.cloned.1.call-update
  7.3 0.0 all-gather.5.cloned.1.call-start
  7.3 0.7 all-gather.5.cloned.1.call-update
  8.0 0.7 slice.3
  8.7 0.8 xor_multiply_fusion
  9.5 0.1 mul.13
  9.6 5.8 %sort.17 = (s32[2800]{0:T(1024)}, s32[2800]{0:T(1024)S(1)}) sort(s32[2800]{0:T(1024)S(1)} %iota_add_fusion, s32[2800]{0:T(1024)S(1)} %iota.8), dimensions={0}, to_apply=%region_0.0 | sort | flops 33600 | bytes 44800 | tf_op jit(solution)/shard_map/jit(argsort)/sort | solution.py:15
  15.4 80.4 %all-gather.7.cloned.1.call-done = bf16[4,700,1400]{2,1,0:T(8,128)(2,1)} async-done(((bf16[1,700,1400]{2,1,0:T(8,128)(2,1)}), bf16[4,700,1400]{2,1,0:T(8,128)(2,1)}) %all-gather.7.cloned.1.call-update) | async-done | bytes 7840016 | tf_op jit(solution)/shard_map/all_gather | solution.py:24
  95.7 7.6 %reshape.25 = bf16[2800,1400]{1,0:T(8,128)(2,1)} reshape(bf16[4,700,1400]{2,1,0:T(8,128)(2,1)} %all-gather.7.cloned.1.call-done) | data formatting | bytes 15680000
  103.3 102.1 %all-gather.5.cloned.1.call-done = bf16[8,350,2000]{2,1,0:T(8,128)(2,1)} async-done(((bf16[1,350,2000]{2,1,0:T(8,128)(2,1)}), bf16[8,350,2000]{2,1,0:T(8,128)(2,1)}) %all-gather.5.cloned.1.call-update) | async-done | bytes 11200016 | tf_op jit(solution)/shard_map/all_gather | solution.py:20
  205.5 15.7 %reshape.23 = bf16[2800,2000]{1,0:T(8,128)(2,1)} reshape(bf16[8,350,2000]{2,1,0:T(8,128)(2,1)} %all-gather.5.cloned.1.call-done) | data formatting | bytes 22400000
  221.1 27.7 %gather_fusion = bf16[2800,2000]{1,0:T(8,128)(2,1)} fusion(bf16[2000,2800]{0,1:T(8,128)(2,1)} %bitcast.6, s32[3072]{0:T(1024)S(1)} %pad_clamp_fusion), kind=kCustom, calls=%fused_computation | custom fusion | bytes 22411200 | tf_op jit(solution)/shard_map/jit(_take)/gather | solution.py:21
  248.9 25.7 %fusion.3 = f32[2000,1400]{1,0:T(8,128)} fusion(f32[2000,1400]{1,0:T(8,128)} %param.7, bf16[2800,1400]{1,0:T(8,128)(2,1)} %reshape.25, bf16[2800,2000]{1,0:T(8,128)(2,1)} %gather_fusion, pred[2800]{0:T(1024)(128)(4,1)S(1)} %compare_and_fusion), kind=kOutput, calls=%fused_computation.4 | convolution fusion | flops 15688399872 | bytes 41442800 | tf_op jit(solution)/shard_map/dot_general | solution.py:22
  (5 shorter events, 0.0 us)
Async XLA Ops:
  6.5 89.2 %all-gather.7.cloned.1.call-start = ((), (), s32[]{:S(2)}) async-start(), calls=%async_computation.1 | async-start | bytes 9912320 | tf_op jit(solution)/shard_map/all_gather | solution.py:24
  7.3 198.2 %all-gather.5.cloned.1.call-start = ((), (), s32[]{:S(2)}) async-start(), calls=%async_computation | async-start | bytes 12976128 | tf_op jit(solution)/shard_map/all_gather | solution.py:20
Sparse Core Ops, SparseCore 0:
  9.2 86.4 all-gather.6
  97.4 108.0 all-gather.4
where the time goes:
time: 282 us; the launch traced here: 281 us
  waiting for transfers between devices  184 us (65%)
  local copies, waits for them, and re-layouts  51.8 us (18%)
  matrix products  25.7 us (9%)
  between operations  13.4 us (5%)
  other arithmetic  6.58 us (2%)
    all_gather x1, waiting for transfers between devices, on_device(): gathered = lax.all_gather(amplitudes, 'col', axis=1, tiled=True)  102 us
    all_gather x1, waiting for transfers between devices, on_device(): lax.all_gather(values_stored, 'row', axis=0, tiled=True)  80.4 us
    gather x1, local copies, waits for them, and re-layouts, on_device(): sorted_columns = jnp.take(gathered, stored, axis=1)  27.7 us
    dot_general x1, matrix products, on_device(): jnp.dot(sorted_columns, lax.all_gather(values_stored, 'row', axis=0, tile...  25.7 us
    unnamed x2, local copies, waits for them, and re-layouts  23.3 us
    sort x1, other arithmetic, stored_order(): return jnp.argsort(sort_key)  5.79 us
  transfers between devices with their start and end apart: 2, of which 2 were waited for; matrix products, arithmetic and copies ran while one was open for 5% of the time, Pallas kernels for 0%

commit v1 on v0

v1 whole, which is shorter than its diff:
```python
import functools

import jax
import jax.numpy as jnp
import numpy as np
from jax import lax
from jax.experimental import pallas as pl
from jax.experimental.pallas import tpu as pltpu
from jax.sharding import PartitionSpec as P

C_SLAB = 2
CORES = 2
TILE = 256
CHUNKS = (4, 4)
CONTRACT_FIRST = (((0,), (0,)), ((), ()))


def round_up(value, step):
    return -(-value // step) * step


def stored_positions(irrep_virtual, chips, depth, depth_padded):
    pair_irrep = jnp.bitwise_xor(irrep_virtual[:C_SLAB][:, None], irrep_virtual[None, :]).reshape(-1)
    count = pair_irrep.shape[0]
    key = pair_irrep * count + jnp.arange(count, dtype=jnp.int32)
    blocks = jnp.pad(
        key.reshape(chips * CORES, depth), ((0, 0), (0, depth_padded - depth)), constant_values=-1
    ).reshape(chips, CORES * depth_padded, 1)
    rank = jnp.sum((key[None, None, :] < blocks).astype(jnp.int32), axis=2, keepdims=True)
    return jnp.where(blocks < 0, -1, rank)


def permute_kernel(count, has_previous, base_ref, pos_ref, *refs):
    out_ref = refs[-1]
    total = refs[count][0].astype(jnp.float32) if has_previous else None
    pos = pos_ref[0]
    for s in range(count):
        rows = refs[s].shape[0]
        picks = pos - base_ref[s] == lax.broadcasted_iota(jnp.int32, (pos.shape[0], rows), 1)
        term = jnp.dot(picks.astype(jnp.bfloat16), refs[s][...], preferred_element_type=jnp.float32)
        total = term if total is None else total + term
    out_ref[0] = total.astype(out_ref.dtype)


def add_permuted(pos, parts, bases, previous):
    chips, rows, _ = pos.shape
    columns = parts[0].shape[1]
    block = pl.BlockSpec((1, rows, columns), lambda q, *_: (q, 0, 0))
    in_specs = [pl.BlockSpec((1, rows, 1), lambda q, *_: (q, 0, 0))]
    in_specs += [
        pl.BlockSpec(part.shape, lambda q, *_: (0, 0), pipeline_mode=pl.Buffered(1)) for part in parts
    ]
    operands = [jnp.stack(bases).astype(jnp.int32), pos, *parts]
    aliases = {}
    if previous is not None:
        in_specs.append(block)
        aliases = {len(operands): 0}
        operands.append(previous)
    return pl.pallas_call(
        functools.partial(permute_kernel, len(parts), previous is not None),
        grid_spec=pltpu.PrefetchScalarGridSpec(
            num_scalar_prefetch=1, grid=(chips,), in_specs=in_specs, out_specs=block
        ),
        out_shape=jax.ShapeDtypeStruct((chips, rows, columns), parts[0].dtype),
        input_output_aliases=aliases,
        compiler_params=pltpu.CompilerParams(vmem_limit_bytes=32 << 20),
        cost_estimate=pl.CostEstimate(
            flops=2 * chips * rows * columns * sum(part.shape[0] for part in parts),
            bytes_accessed=4 * chips * rows * columns,
            transcendentals=0,
        ),
    )(*operands)


def gather_integrals(values, size):
    half = round_up(values.shape[0] // 2, 16)

    def send(array, bit):
        return lax.ppermute(array, "row", [(i, i ^ bit) for i in range(size)])

    got = {0: [values]}
    order = sorted(range(1, size), key=lambda d: (bin(d).count("1"), d))
    for d in order:
        low, high = d & -d, 1 << (d.bit_length() - 1)
        if low == high:
            got[d] = [send(values, d)]
            continue
        parts = []
        for which, bit in ((0, low), (1, high)):
            source = got[d ^ bit]
            if len(source) == 2:
                piece = source[which]
            else:
                piece = source[0][:half] if which == 0 else source[0][half:]
            parts.append(send(piece, bit))
        got[d] = parts
    return got, order, half


def slot_table(chips):
    table = []
    for z in range(chips):
        line = []
        for s in range(1, chips):
            if z + s < chips:
                line.append((("L", s), z + s))
            if z - s >= 0:
                line.append((("R", s), z - s))
        table.append(line)
    return table


def spread_line(chunk, chips):
    got = {}
    swap_all = [(i, i ^ 1) for i in range(chips * CORES)]
    got["own", 0] = (chunk, lax.ppermute(chunk, "col", swap_all))
    held = {"L": chunk, "R": chunk}
    for s in range(1, chips):
        for way, step in (("L", -1), ("R", 1)):
            pairs = []
            ends = []
            for z in range(chips):
                source = z + s if step < 0 else z - s
                if 0 <= source < chips:
                    ends.append(z)
                    for core in range(CORES):
                        pairs.append(((z - step) * CORES + core, z * CORES + core))
            held[way] = lax.ppermute(held[way], "col", pairs)
            swap = [(z * CORES + core, z * CORES + 1 - core) for z in ends for core in range(CORES)]
            got[way, s] = (held[way], lax.ppermute(held[way], "col", swap))
    return got


def product_kernel(slots, chunk_tiles, depth, info_ref, *refs):
    count = len(slots)
    offsets = np.cumsum([0, *slots])
    n_arrays = int(offsets[-1]) * len(chunk_tiles) * CORES
    arrays = refs[:n_arrays]
    natural_ref, acc_ref = refs[n_arrays], refs[n_arrays + 1]
    out_ref, buffer, integrals, sems, sem_integrals = refs[n_arrays + 2 :]
    core = info_ref[0]
    tile = acc_ref.shape[0]
    i = pl.program_id(0)
    steps = sum(chunk_tiles)

    def fetch(step, slot_of_buffer):
        first = 0
        for h, tiles in enumerate(chunk_tiles):

            @pl.when(jnp.logical_and(step >= first, step < first + tiles))
            def _(h=h, first=first):
                lanes = pl.ds(pl.multiple_of((step - first) * tile, tile), tile)
                for s in range(count):
                    for k in range(slots[s]):
                        at = ((int(offsets[s]) + k) * len(chunk_tiles) + h) * CORES

                        def start(at=at, s=s):
                            for other in range(CORES):
                                place = jnp.where(core == other, 0, depth) + 2 * depth * s
                                pltpu.make_async_copy(
                                    arrays[at + other].at[:, lanes],
                                    buffer.at[slot_of_buffer, pl.ds(pl.multiple_of(place, 16), depth), :],
                                    sems.at[slot_of_buffer],
                                ).start()

                        if slots[s] == 1:
                            start()
                        else:
                            pl.when(info_ref[1 + s] == k)(start)

            first += tiles

    @pl.when(i == 0)
    def _():
        for s in range(count):
            pltpu.make_async_copy(
                natural_ref.at[info_ref[1 + count + s]],
                integrals.at[pl.ds(2 * depth * s, 2 * depth), :],
                sem_integrals,
            ).start()
        fetch(0, 0)

    @pl.when(i + 1 < steps)
    def _():
        fetch(i + 1, lax.rem(i + 1, 2))

    @pl.when(i == 0)
    def _():
        pltpu.make_async_copy(integrals, integrals, sem_integrals).wait()

    now = lax.rem(i, 2)
    pltpu.make_async_copy(buffer.at[now], buffer.at[now], sems.at[now]).wait()
    out_ref[...] = acc_ref[...] + lax.dot_general(
        buffer[now], integrals[...], CONTRACT_FIRST, preferred_element_type=jnp.float32
    )


def add_product(info, slots, natural, acc, first_tile, in_place):
    tile = TILE
    chunk_tiles = tuple(pair[0].shape[1] // tile for pair in slots[0][0])
    depth = slots[0][0][0][0].shape[0]
    columns = natural.shape[2]
    arrays = [a for slot in slots for candidate in slot for pair in candidate for a in pair]
    anywhere = pl.BlockSpec(memory_space=pl.ANY)
    block = pl.BlockSpec((tile, columns), lambda i, *_: (first_tile + i, 0))
    operands = [info, *arrays, natural, acc]
    rows = 2 * depth * len(slots)
    lanes = sum(chunk_tiles) * tile
    return pl.pallas_call(
        functools.partial(product_kernel, tuple(len(slot) for slot in slots), chunk_tiles, depth),
        grid_spec=pltpu.PrefetchScalarGridSpec(
            num_scalar_prefetch=1,
            grid=(sum(chunk_tiles),),
            in_specs=[anywhere] * (len(arrays) + 1) + [block],
            out_specs=block,
            scratch_shapes=[
                pltpu.VMEM((2, rows, tile), natural.dtype),
                pltpu.VMEM((rows, columns), natural.dtype),
                pltpu.SemaphoreType.DMA((2,)),
                pltpu.SemaphoreType.DMA,
            ],
        ),
        out_shape=jax.ShapeDtypeStruct(acc.shape, acc.dtype),
        input_output_aliases={len(operands) - 1: 0} if in_place else {},
        compiler_params=pltpu.CompilerParams(vmem_limit_bytes=32 << 20),
        cost_estimate=pl.CostEstimate(
            flops=2 * lanes * rows * columns,
            bytes_accessed=8 * lanes * columns + 2 * rows * (lanes + columns),
            transcendentals=0,
        ),
    )(*operands)


def on_device(chips, row_size, amplitudes, values_stored, irrep_virtual, residual_in):
    occ, depth = amplitudes.shape
    depth_padded = round_up(depth, 16)
    chip = lax.axis_index("col") // CORES
    core = lax.axis_index("col") % CORES
    row = lax.axis_index("row")

    lanes = sum(CHUNKS) * TILE
    columns_first = jnp.pad(amplitudes.T, ((0, depth_padded - depth), (0, lanes - occ)))
    edges = np.cumsum([0, *CHUNKS]) * TILE
    chunks = [columns_first[:, edges[h] : edges[h + 1]] for h in range(len(CHUNKS))]

    spread = [spread_line(chunk, chips) for chunk in chunks]
    got, order, half = gather_integrals(values_stored, row_size)

    pos = stored_positions(irrep_virtual, chips, depth, depth_padded)
    stored_rows = values_stored.shape[0]
    natural = add_permuted(pos, [values_stored], [row * stored_rows], None)
    single = [d for d in order if len(got[d]) == 1]
    natural = add_permuted(pos, [got[d][0] for d in single], [(row ^ d) * stored_rows for d in single], natural)
    for d in order:
        if len(got[d]) == 2:
            base = (row ^ d) * stored_rows
            natural = add_permuted(pos, got[d], [base, base + half], natural)

    table = slot_table(chips)
    slots, choices, sources = [[("own", 0)]], [jnp.int32(0)], [chip]
    for t in range(chips - 1):
        candidates = sorted({table[z][t][0] for z in range(chips)})
        slots.append(candidates)
        choices.append(jnp.asarray([candidates.index(table[z][t][0]) for z in range(chips)], jnp.int32)[chip])
        sources.append(jnp.asarray([table[z][t][1] for z in range(chips)], jnp.int32)[chip])

    def info_of(which):
        return jnp.stack([core, *[choices[s] for s in which], *[sources[s] for s in which]]).astype(jnp.int32)

    every = list(range(len(CHUNKS)))
    early, last = list(range(chips - 1)), [chips - 1]
    acc = add_product(
        info_of(early),
        [[[spread[h][c] for h in every] for c in slots[s]] for s in early],
        natural,
        residual_in,
        0,
        False,
    )
    for h in every:
        acc = add_product(
            info_of(last),
            [[[spread[h][c]] for c in slots[s]] for s in last],
            natural,
            acc,
            int(edges[h]) // TILE,
            True,
        )
    return acc


def solution(mesh):
    in_specs = (P("row", "col"), P("row", "col"), P(), P("row", "col"))
    out_specs = P("row", "col")
    body = functools.partial(on_device, mesh.shape["col"] // CORES, mesh.shape["row"])
    return jax.shard_map(body, mesh=mesh, in_specs=in_specs, out_specs=out_specs, check_vma=False)
```

time: 282 us -> 199 us (0.71)
  waiting for transfers between devices: 184 us -> 53.2 us
  Pallas kernels: 0 us -> 76.3 us
  starting transfers between devices: 0.04 us -> 47.8 us
  local copies, waits for them, and re-layouts: 51.8 us -> 14.8 us
  matrix products: 25.7 us -> 0 us
  between operations: 13.4 us -> 0.66 us
    all_gather x2 -> x0, waiting for transfers between devices: 182 us -> none  [the longest x1 102 us: on_device(): gathered = lax.all_gather(amplitudes, 'col', axis=1, tiled=True)]
    pallas_call x0 -> x6, Pallas kernels: none -> 76.3 us  [the longest x3 38.6 us: add_product(): pl.pallas_call(functools.partial(product_kernel, tuple((len(slot) for slo...]
    ppermute x0 -> x30, waiting for transfers between devices: none -> 53.2 us  [the longest x12 50 us: spread_line(): held[way] = lax.ppermute(held[way], 'col', pairs)]
    ppermute x0 -> x30, starting transfers between devices: none -> 47.8 us  [the longest x12 22.7 us: spread_line(): held[way] = lax.ppermute(held[way], 'col', pairs)]
    gather x1 -> x0, local copies, waits for them, and re-layouts: 27.7 us -> none  [on_device(): sorted_columns = jnp.take(gathered, stored, axis=1)]
    dot_general x1 -> x0, matrix products: 25.7 us -> none  [on_device(): jnp.dot(sorted_columns, lax.all_gather(values_stored, 'row', axis=0, tile...]
    unnamed x2 -> x20, local copies, waits for them, and re-layouts: 23.3 us -> 0.89 us
    sort x1 -> x0, other arithmetic: 5.79 us -> none  [stored_order(): return jnp.argsort(sort_key)]
  transfers between devices with their start and end apart: 2 -> 30, of which waited for: 2 -> 6; matrix products, arithmetic and copies ran while one was open for 5% -> 9% of each run, Pallas kernels for 0% -> 35%
where the time goes in v1:
time: 199 us; the launch traced here: 198 us
  Pallas kernels  76.3 us (38%)
  waiting for transfers between devices  53.2 us (27%)
  starting transfers between devices  47.8 us (24%)
  local copies, waits for them, and re-layouts  14.8 us (7%)
  other arithmetic  5.18 us (3%)
    ppermute x12, waiting for transfers between devices, spread_line(): held[way] = lax.ppermute(held[way], 'col', pairs)  50 us
    pallas_call x3, Pallas kernels, add_product(): pl.pallas_call(functools.partial(product_kernel, tuple((len(slot) for slo...  38.6 us
    pallas_call x3, Pallas kernels, add_permuted(): pl.pallas_call(functools.partial(permute_kernel, len(parts), previous is...  37.8 us
    ppermute x12, starting transfers between devices, spread_line(): held[way] = lax.ppermute(held[way], 'col', pairs)  22.7 us
    ppermute x12, starting transfers between devices, spread_line(): got[way, s] = (held[way], lax.ppermute(held[way], 'col', swap))  18.4 us
    ppermute x4, starting transfers between devices, send(): return lax.ppermute(array, 'row', [(i, i ^ bit) for i in range(size)])  6.75 us
  transfers between devices with their start and end apart: 30, of which 6 were waited for; matrix products, arithmetic and copies ran while one was open for 9% of the time, Pallas kernels for 35%

profile of v1, /device:TPU:0, one launch (start us, length us, event | category | flops | bytes accessed | tf_op | source)
XLA Modules:
  0.0 198.0 jit_solution(15600061101270169514)
XLA Ops:
  4.2 6.2 %collective-permute-start.19 = (bf16[352,1024]{1,0:T(8,128)(2,1)S(1)}, bf16[352,1024]{1,0:T(8,128)(2,1)S(1)}, u32[]{:S(2)}, u32[]{:S(2)}) collective-permute-start(bf16[352,1024]{1,0:T(8,128)(2,1)S(1)} %get-tuple-element.5.refs_0_), channel_id=1, source_target_pairs={{0,2},{1,3},{2,4},{3,5},{4,6},{5,7},{8,10},{9,11},{10,12},{11,13},... | collective-permute-start | bytes 2162696 | tf_op jit(solution)/shard_map/ppermute | solution.py:128
  10.4 2.0 %collective-permute-start.10 = (bf16[700,1400]{1,0:T(8,128)(2,1)}, bf16[700,1400]{1,0:T(8,128)(2,1)}, u32[]{:S(2)}, u32[]{:S(2)}) collective-permute-start(bf16[700,1400]{1,0:T(8,128)(2,1)} %refs_0_.1), channel_id=1, source_target_pairs={{0,16},{8,24},{16,0},{24,8},{1,17},{9,25},{17,1},{25,9},{2,18},{10... | collective-permute-start | bytes 5880008 | tf_op jit(solution)/shard_map/ppermute | solution.py:79
  13.9 9.6 %collective-permute-done.14.refs_4_ = bf16[352,1024]{1,0:T(8,128)(2,1)} collective-permute-done((bf16[352,1024]{1,0:T(8,128)(2,1)S(1)}, bf16[352,1024]{1,0:T(8,128)(2,1)}, u32[]{:S(2)}, u32[]{:S(2)}) %collective-permute-start.14) | collective-permute-done | bytes 720928 | tf_op jit(solution)/shard_map/ppermute | solution.py:128
  23.6 4.0 %collective-permute-start.5 = (bf16[352,1024]{1,0:T(8,128)(2,1)S(1)}, bf16[352,1024]{1,0:T(8,128)(2,1)S(1)}, u32[]{:S(2)}, u32[]{:S(2)}) collective-permute-start(bf16[352,1024]{1,0:T(8,128)(2,1)S(1)} %get-tuple-element.6.refs_2_), channel_id=1, source_target_pairs={{0,2},{1,3},{2,4},{3,5},{4,6},{5,7},{8,10},{9,11},{10,12},{11,13},... | collective-permute-start | bytes 2162696 | tf_op jit(solution)/shard_map/ppermute | solution.py:128
  27.6 10.5 %collective-permute-done.refs_6_ = bf16[352,1024]{1,0:T(8,128)(2,1)S(1)} collective-permute-done((bf16[352,1024]{1,0:T(8,128)(2,1)S(1)}, bf16[352,1024]{1,0:T(8,128)(2,1)S(1)}, u32[]{:S(2)}, u32[]{:S(2)}) %collective-permute-start) | collective-permute-done | bytes 720928 | tf_op jit(solution)/shard_map/ppermute | solution.py:128
  39.2 2.0 %collective-permute-done.5.refs_10_.refs_18_ = bf16[352,1024]{1,0:T(8,128)(2,1)S(1)} collective-permute-done((bf16[352,1024]{1,0:T(8,128)(2,1)S(1)}, bf16[352,1024]{1,0:T(8,128)(2,1)S(1)}, u32[]{:S(2)}, u32[]{:S(2)}) %collective-permute-start.5) | collective-permute-done | bytes 720928 | tf_op jit(solution)/shard_map/ppermute | solution.py:128
  45.7 17.3 %collective-permute-done.15.refs_12_.refs_0_ = bf16[352,1024]{1,0:T(8,128)(2,1)} collective-permute-done((bf16[352,1024]{1,0:T(8,128)(2,1)}, bf16[352,1024]{1,0:T(8,128)(2,1)}, u32[]{:S(2)}, u32[]{:S(2)}) %collective-permute-start.15) | collective-permute-done | bytes 720928 | tf_op jit(solution)/shard_map/ppermute | solution.py:128
  62.9 1.9 collective-permute-start.26
  64.9 10.6 %collective-permute-done.1.refs_14_.refs_0_ = bf16[352,1024]{1,0:T(8,128)(2,1)} collective-permute-done((bf16[352,1024]{1,0:T(8,128)(2,1)}, bf16[352,1024]{1,0:T(8,128)(2,1)}, u32[]{:S(2)}, u32[]{:S(2)}) %collective-permute-start.1) | collective-permute-done | bytes 720928 | tf_op jit(solution)/shard_map/ppermute | solution.py:128
  75.4 1.9 collective-permute-start.27
  82.0 3.4 %convert_reduce_fusion = s32[4,704]{1,0:T(4,128)S(1)} fusion(s32[4,704]{1,0:T(4,128)S(1)} %lt.52, s32[2800]{0:T(1024)S(1)} %iota_add_fusion), kind=kLoop, calls=%fused_computation | loop fusion | flops 23651584 | bytes 33728 | tf_op jit(solution)/shard_map/reduce_sum | solution.py:29
  92.1 2.6 %stack.46.info_ref = s32[7]{0:T(128)S(1)} concatenate(s32[1]{0:T(128)} %bitcast, s32[1]{0:T(128)} %constant.63.clone.1, s32[1]{0:T(128)} %dynamic_slice.20, s32[1]{0:T(128)} %dynamic_slice.21, s32[1]{0:T(128)} %bitcast.8, s32[1]{0:T(128)} %dynamic_slice.22, s32[1]{0:T(128)} %dynamic_slice.23), dimensions={0} | concatenate | bytes 56 | tf_op jit(solution)/shard_map/stack | solution.py:268
  97.5 1.7 collective-permute-start.11
  100.9 1.9 collective-permute-start.16
  102.9 2.4 %collective-permute-start.2 = (bf16[352,1024]{1,0:T(8,128)(2,1)}, bf16[352,1024]{1,0:T(8,128)(2,1)S(1)}, u32[]{:S(2)}, u32[]{:S(2)}) collective-permute-start(bf16[352,1024]{1,0:T(8,128)(2,1)} %collective-permute-done.1.refs_14_.refs_0_), channel_id=1, source_target_pairs={{0,1},{1,0},{2,3},{3,2},{8,9},{9,8},{10,11},{11,10},{16,17},{17,16... | collective-permute-start | bytes 2162696 | tf_op jit(solution)/shard_map/ppermute | solution.py:130
  107.4 9.3 %shard_map.100.refs_2_ = bf16[4,704,1400]{2,1,0:T(8,128)(2,1)S(1)} custom-call(s32[1]{0:T(128)} %bitcast.7.base_ref, s32[4,704,1]{2,1,0:T(8,128)S(1)} %broadcast_select_fusion.pos_ref, bf16[700,1400]{1,0:T(8,128)(2,1)} %refs_0_.1), custom_call_target="tpu_custom_call" | custom-call | flops 5519360000 | bytes 15769600 | tf_op jit(solution)/shard_map/pallas_call | solution.py:59
  120.1 3.2 %collective-permute-done.13.refs_1_ = bf16[348,1400]{1,0:T(8,128)(2,1)S(1)} collective-permute-done((bf16[348,1400]{1,0:T(8,128)(2,1)S(1)}, bf16[348,1400]{1,0:T(8,128)(2,1)S(1)}, u32[]{:S(2)}, u32[]{:S(2)}) %collective-permute-start.13) | collective-permute-done | bytes 974432 | tf_op jit(solution)/shard_map/ppermute | solution.py:79
  124.9 17.8 %shard_map.101.refs_2_ = bf16[4,704,1400]{2,1,0:T(8,128)(2,1)S(1)} custom-call(s32[2]{0:T(128)S(1)} %pad_add_fusion.2.base_ref, s32[4,704,1]{2,1,0:T(8,128)S(1)} %broadcast_select_fusion.pos_ref, bf16[700,1400]{1,0:T(8,128)(2,1)} %collective-permute-done.12.refs_0_, ...), custom_call_target="tpu_custom_call", output_to_operand_aliasing={{}: (4, {})} | custom-call | flops 11038720000 | bytes 15769600 | tf_op jit(solution)/shard_map/pallas_call | solution.py:59
  142.7 10.6 %shard_map.102.refs_24_.refs_8_ = bf16[4,704,1400]{2,1,0:T(8,128)(2,1)S(1)} custom-call(s32[2]{0:T(128)S(1)} %pad_add_fusion.1.base_ref, s32[4,704,1]{2,1,0:T(8,128)S(1)} %broadcast_select_fusion.pos_ref, bf16[352,1400]{1,0:T(8,128)(2,1)S(1)} %collective-permute-done.11.refs_0_, ...), custom_call_target="tpu_custom_call", output_to_operand_aliasing={{}: (4, {})} | custom-call | flops 5519360000 | bytes 15769600 | tf_op jit(solution)/shard_map/pallas_call | solution.py:59
  153.4 1.9 collective-permute-start.18
  156.0 2.4 %collective-permute-start.4 = (bf16[352,1024]{1,0:T(8,128)(2,1)S(1)}, bf16[352,1024]{1,0:T(8,128)(2,1)S(1)}, u32[]{:S(2)}, u32[]{:S(2)}) collective-permute-start(bf16[352,1024]{1,0:T(8,128)(2,1)S(1)} %collective-permute-done.3.refs_2_), channel_id=1, source_target_pairs={{0,1},{1,0},{8,9},{9,8},{16,17},{17,16},{24,25},{25,24}} | collective-permute-start | bytes 2162696 | tf_op jit(solution)/shard_map/ppermute | solution.py:130
  159.2 22.5 %shard_map.103.refs_9_ = f32[2000,1400]{1,0:T(8,128)} custom-call(s32[7]{0:T(128)S(1)} %stack.46.info_ref, bf16[352,1024]{1,0:T(8,128)(2,1)S(1)} %get-tuple-element.5.refs_0_, bf16[352,1024]{1,0:T(8,128)(2,1)} %collective-permute-done.24.refs_1_, bf16[352,1024]{1,0:T(8,128)(2,1)S(1)} %get-tuple-element.6.refs_2_, ...), custom_call_target="tpu_custom_call" | custom-call | flops 12111052800 | bytes 37501952 | tf_op jit(solution)/shard_map/pallas_call | solution.py:209
  181.7 8.1 %shard_map.104.refs_9_ = f32[2000,1400]{1,0:T(8,128)} custom-call(s32[3]{0:T(128)S(1)} %pad_add_fusion.info_ref, bf16[352,1024]{1,0:T(8,128)(2,1)} %collective-permute-done.15.refs_12_.refs_0_, bf16[352,1024]{1,0:T(8,128)(2,1)S(1)} %collective-permute-done.16.refs_13_.refs_1_, ...), custom_call_target="tpu_custom_call", output_to_operand_aliasing={{}: (10, {})} | custom-call | flops 2018508800 | bytes 14881792 | tf_op jit(solution)/shard_map/pallas_call | solution.py:209
  189.9 7.9 %shard_map.105 = f32[2000,1400]{1,0:T(8,128)} custom-call(s32[3]{0:T(128)S(1)} %pad_add_fusion.info_ref, bf16[352,1024]{1,0:T(8,128)(2,1)} %collective-permute-done.1.refs_14_.refs_0_, bf16[352,1024]{1,0:T(8,128)(2,1)S(1)} %collective-permute-done.2.refs_15_.refs_1_, ...), custom_call_target="tpu_custom_call", output_to_operand_aliasing={{}: (10, {})} | custom-call | flops 2018508800 | bytes 14881792 | tf_op jit(solution)/shard_map/pallas_call | solution.py:209
  (92 shorter events, 35.4 us)
Async XLA Ops:
  1.6 22.0 %collective-permute-start.14 = (bf16[352,1024]{1,0:T(8,128)(2,1)S(1)}, bf16[352,1024]{1,0:T(8,128)(2,1)}, u32[]{:S(2)}, u32[]{:S(2)}) collective-permute-start(bf16[352,1024]{1,0:T(8,128)(2,1)S(1)} %get-tuple-element.5.refs_0_), channel_id=1, source_target_pairs={{2,0},{3,1},{4,2},{5,3},{6,4},{7,5},{10,8},{11,9},{12,10},{13,11},... | collective-permute-start | bytes 2162696 | tf_op jit(solution)/shard_map/ppermute | solution.py:128
  2.9 35.2 %collective-permute-start = (bf16[352,1024]{1,0:T(8,128)(2,1)S(1)}, bf16[352,1024]{1,0:T(8,128)(2,1)S(1)}, u32[]{:S(2)}, u32[]{:S(2)}) collective-permute-start(bf16[352,1024]{1,0:T(8,128)(2,1)S(1)} %get-tuple-element.6.refs_2_), channel_id=1, source_target_pairs={{2,0},{3,1},{4,2},{5,3},{6,4},{7,5},{10,8},{11,9},{12,10},{13,11},... | collective-permute-start | bytes 2162696 | tf_op jit(solution)/shard_map/ppermute | solution.py:128
  4.2 33.9 %collective-permute-start.19 = (bf16[352,1024]{1,0:T(8,128)(2,1)S(1)}, bf16[352,1024]{1,0:T(8,128)(2,1)S(1)}, u32[]{:S(2)}, u32[]{:S(2)}) collective-permute-start(bf16[352,1024]{1,0:T(8,128)(2,1)S(1)} %get-tuple-element.5.refs_0_), channel_id=1, source_target_pairs={{0,2},{1,3},{2,4},{3,5},{4,6},{5,7},{8,10},{9,11},{10,12},{11,13},... | collective-permute-start | bytes 2162696 | tf_op jit(solution)/shard_map/ppermute | solution.py:128
  10.4 68.5 %collective-permute-start.10 = (bf16[700,1400]{1,0:T(8,128)(2,1)}, bf16[700,1400]{1,0:T(8,128)(2,1)}, u32[]{:S(2)}, u32[]{:S(2)}) collective-permute-start(bf16[700,1400]{1,0:T(8,128)(2,1)} %refs_0_.1), channel_id=1, source_target_pairs={{0,16},{8,24},{16,0},{24,8},{1,17},{9,25},{17,1},{25,9},{2,18},{10... | collective-permute-start | bytes 5880008 | tf_op jit(solution)/shard_map/ppermute | solution.py:79
  12.4 68.0 %collective-permute-start.12 = (bf16[700,1400]{1,0:T(8,128)(2,1)}, bf16[700,1400]{1,0:T(8,128)(2,1)}, u32[]{:S(2)}, u32[]{:S(2)}) collective-permute-start(bf16[700,1400]{1,0:T(8,128)(2,1)} %refs_0_.1), channel_id=1, source_target_pairs={{0,8},{8,0},{16,24},{24,16},{1,9},{9,1},{17,25},{25,17},{2,10},{10... | collective-permute-start | bytes 5880008 | tf_op jit(solution)/shard_map/ppermute | solution.py:79
  41.2 21.7 %collective-permute-start.15 = (bf16[352,1024]{1,0:T(8,128)(2,1)}, bf16[352,1024]{1,0:T(8,128)(2,1)}, u32[]{:S(2)}, u32[]{:S(2)}) collective-permute-start(bf16[352,1024]{1,0:T(8,128)(2,1)} %collective-permute-done.14.refs_4_), channel_id=1, source_target_pairs={{2,0},{3,1},{4,2},{5,3},{10,8},{11,9},{12,10},{13,11},{18,16},{19,... | collective-permute-start | bytes 2162696 | tf_op jit(solution)/shard_map/ppermute | solution.py:128
  42.5 32.9 %collective-permute-start.1 = (bf16[352,1024]{1,0:T(8,128)(2,1)}, bf16[352,1024]{1,0:T(8,128)(2,1)}, u32[]{:S(2)}, u32[]{:S(2)}) collective-permute-start(bf16[352,1024]{1,0:T(8,128)(2,1)} %copy-done), channel_id=1, source_target_pairs={{2,0},{3,1},{4,2},{5,3},{10,8},{11,9},{12,10},{13,11},{18,16},{19,... | collective-permute-start | bytes 2162696 | tf_op jit(solution)/shard_map/ppermute | solution.py:128
  43.8 33.5 %collective-permute-start.20 = (bf16[352,1024]{1,0:T(8,128)(2,1)S(1)}, bf16[352,1024]{1,0:T(8,128)(2,1)}, u32[]{:S(2)}, u32[]{:S(2)}) collective-permute-start(bf16[352,1024]{1,0:T(8,128)(2,1)S(1)} %collective-permute-done.19.refs_8_.refs_16_), channel_id=1, source_target_pairs={{2,4},{3,5},{4,6},{5,7},{10,12},{11,13},{12,14},{13,15},{18,20},{1... | collective-permute-start | bytes 2162696 | tf_op jit(solution)/shard_map/ppermute | solution.py:128
  62.9 36.3 %collective-permute-start.26 = (bf16[352,1024]{1,0:T(8,128)(2,1)}, bf16[352,1024]{1,0:T(8,128)(2,1)}, u32[]{:S(2)}, u32[]{:S(2)}) collective-permute-start(bf16[352,1024]{1,0:T(8,128)(2,1)} %collective-permute-done.14.refs_4_), channel_id=1, source_target_pairs={{0,1},{1,0},{2,3},{3,2},{4,5},{5,4},{8,9},{9,8},{10,11},{11,10},{1... | collective-permute-start | bytes 2162696 | tf_op jit(solution)/shard_map/ppermute | solution.py:130
  75.4 25.5 %collective-permute-start.27 = (bf16[352,1024]{1,0:T(8,128)(2,1)}, bf16[352,1024]{1,0:T(8,128)(2,1)}, u32[]{:S(2)}, u32[]{:S(2)}) collective-permute-start(bf16[352,1024]{1,0:T(8,128)(2,1)} %copy-done), channel_id=1, source_target_pairs={{0,1},{1,0},{2,3},{3,2},{4,5},{5,4},{8,9},{9,8},{10,11},{11,10},{1... | collective-permute-start | bytes 2162696 | tf_op jit(solution)/shard_map/ppermute | solution.py:130
  77.3 25.5 %collective-permute-start.28 = (bf16[352,1024]{1,0:T(8,128)(2,1)S(1)}, bf16[352,1024]{1,0:T(8,128)(2,1)}, u32[]{:S(2)}, u32[]{:S(2)}) collective-permute-start(bf16[352,1024]{1,0:T(8,128)(2,1)S(1)} %collective-permute-done.19.refs_8_.refs_16_), channel_id=1, source_target_pairs={{2,3},{3,2},{4,5},{5,4},{6,7},{7,6},{10,11},{11,10},{12,13},{13,12... | collective-permute-start | bytes 2162696 | tf_op jit(solution)/shard_map/ppermute | solution.py:130
  78.9 18.6 %collective-permute-start.6 = (bf16[352,1024]{1,0:T(8,128)(2,1)S(1)}, bf16[352,1024]{1,0:T(8,128)(2,1)}, u32[]{:S(2)}, u32[]{:S(2)}) collective-permute-start(bf16[352,1024]{1,0:T(8,128)(2,1)S(1)} %collective-permute-done.5.refs_10_.refs_18_), channel_id=1, source_target_pairs={{2,4},{3,5},{4,6},{5,7},{10,12},{11,13},{12,14},{13,15},{18,20},{1... | collective-permute-start | bytes 2162696 | tf_op jit(solution)/shard_map/ppermute | solution.py:128
  80.4 24.9 %collective-permute-start.29 = (bf16[352,1024]{1,0:T(8,128)(2,1)S(1)}, bf16[352,1024]{1,0:T(8,128)(2,1)}, u32[]{:S(2)}, u32[]{:S(2)}) collective-permute-start(bf16[352,1024]{1,0:T(8,128)(2,1)S(1)} %collective-permute-done.5.refs_10_.refs_18_), channel_id=1, source_target_pairs={{2,3},{3,2},{4,5},{5,4},{6,7},{7,6},{10,11},{11,10},{12,13},{13,12... | collective-permute-start | bytes 2162696 | tf_op jit(solution)/shard_map/ppermute | solution.py:130
  97.5 26.5 %collective-permute-start.11 = (bf16[352,1400]{1,0:T(8,128)(2,1)S(1)}, bf16[352,1400]{1,0:T(8,128)(2,1)S(1)}, u32[]{:S(2)}, u32[]{:S(2)}) collective-permute-start(bf16[352,1400]{1,0:T(8,128)(2,1)S(1)} %slice.20), channel_id=1, source_target_pairs={{0,8},{8,0},{16,24},{24,16},{1,9},{9,1},{17,25},{25,17},{2,10},{10... | collective-permute-start | bytes 2956808 | tf_op jit(solution)/shard_map/ppermute | solution.py:79
  99.2 24.1 %collective-permute-start.13 = (bf16[348,1400]{1,0:T(8,128)(2,1)S(1)}, bf16[348,1400]{1,0:T(8,128)(2,1)S(1)}, u32[]{:S(2)}, u32[]{:S(2)}) collective-permute-start(bf16[348,1400]{1,0:T(8,128)(2,1)S(1)} %slice.21), channel_id=1, source_target_pairs={{0,16},{8,24},{16,0},{24,8},{1,17},{9,25},{17,1},{25,9},{2,18},{10... | collective-permute-start | bytes 2923208 | tf_op jit(solution)/shard_map/ppermute | solution.py:79
  116.8 36.6 %collective-permute-start.17 = (bf16[352,1024]{1,0:T(8,128)(2,1)}, bf16[352,1024]{1,0:T(8,128)(2,1)S(1)}, u32[]{:S(2)}, u32[]{:S(2)}) collective-permute-start(bf16[352,1024]{1,0:T(8,128)(2,1)} %collective-permute-done.15.refs_12_.refs_0_), channel_id=1, source_target_pairs={{2,0},{3,1},{10,8},{11,9},{18,16},{19,17},{26,24},{27,25}} | collective-permute-start | bytes 2162696 | tf_op jit(solution)/shard_map/ppermute | solution.py:128
  118.1 37.2 %collective-permute-start.22 = (bf16[352,1024]{1,0:T(8,128)(2,1)}, bf16[352,1024]{1,0:T(8,128)(2,1)S(1)}, u32[]{:S(2)}, u32[]{:S(2)}) collective-permute-start(bf16[352,1024]{1,0:T(8,128)(2,1)} %collective-permute-done.20.refs_20_.refs_4_), channel_id=1, source_target_pairs={{4,6},{5,7},{12,14},{13,15},{20,22},{21,23},{28,30},{29,31}} | collective-permute-start | bytes 2162696 | tf_op jit(solution)/shard_map/ppermute | solution.py:128
  118.8 37.2 %collective-permute-start.3 = (bf16[352,1024]{1,0:T(8,128)(2,1)}, bf16[352,1024]{1,0:T(8,128)(2,1)S(1)}, u32[]{:S(2)}, u32[]{:S(2)}) collective-permute-start(bf16[352,1024]{1,0:T(8,128)(2,1)} %collective-permute-done.1.refs_14_.refs_0_), channel_id=1, source_target_pairs={{2,0},{3,1},{10,8},{11,9},{18,16},{19,17},{26,24},{27,25}} | collective-permute-start | bytes 2162696 | tf_op jit(solution)/shard_map/ppermute | solution.py:128
  123.3 35.9 %collective-permute-start.7 = (bf16[352,1024]{1,0:T(8,128)(2,1)}, bf16[352,1024]{1,0:T(8,128)(2,1)S(1)}, u32[]{:S(2)}, u32[]{:S(2)}) collective-permute-start(bf16[352,1024]{1,0:T(8,128)(2,1)} %collective-permute-done.6.refs_22_.refs_4_), channel_id=1, source_target_pairs={{4,5},{5,4},{6,7},{7,6},{12,13},{13,12},{14,15},{15,14},{20,21},{2... | collective-permute-start | bytes 2162696 | tf_op jit(solution)/shard_map/ppermute | solution.py:130
  124.0 34.4 %collective-permute-start.8 = (bf16[352,1024]{1,0:T(8,128)(2,1)}, bf16[352,1024]{1,0:T(8,128)(2,1)S(1)}, u32[]{:S(2)}, u32[]{:S(2)}) collective-permute-start(bf16[352,1024]{1,0:T(8,128)(2,1)} %collective-permute-done.6.refs_22_.refs_4_), channel_id=1, source_target_pairs={{4,6},{5,7},{12,14},{13,15},{20,22},{21,23},{28,30},{29,31}} | collective-permute-start | bytes 2162696 | tf_op jit(solution)/shard_map/ppermute | solution.py:128
  153.4 28.4 %collective-permute-start.18 = (bf16[352,1024]{1,0:T(8,128)(2,1)S(1)}, bf16[352,1024]{1,0:T(8,128)(2,1)S(1)}, u32[]{:S(2)}, u32[]{:S(2)}) collective-permute-start(bf16[352,1024]{1,0:T(8,128)(2,1)S(1)} %collective-permute-done.17.refs_2_), channel_id=1, source_target_pairs={{0,1},{1,0},{8,9},{9,8},{16,17},{17,16},{24,25},{25,24}} | collective-permute-start | bytes 2162696 | tf_op jit(solution)/shard_map/ppermute | solution.py:130
  155.3 26.4 %collective-permute-start.23 = (bf16[352,1024]{1,0:T(8,128)(2,1)S(1)}, bf16[352,1024]{1,0:T(8,128)(2,1)S(1)}, u32[]{:S(2)}, u32[]{:S(2)}) collective-permute-start(bf16[352,1024]{1,0:T(8,128)(2,1)S(1)} %collective-permute-done.22.refs_6_), channel_id=1, source_target_pairs={{6,7},{7,6},{14,15},{15,14},{22,23},{23,22},{30,31},{31,30}} | collective-permute-start | bytes 2162696 | tf_op jit(solution)/shard_map/ppermute | solution.py:130
  156.0 33.8 %collective-permute-start.4 = (bf16[352,1024]{1,0:T(8,128)(2,1)S(1)}, bf16[352,1024]{1,0:T(8,128)(2,1)S(1)}, u32[]{:S(2)}, u32[]{:S(2)}) collective-permute-start(bf16[352,1024]{1,0:T(8,128)(2,1)S(1)} %collective-permute-done.3.refs_2_), channel_id=1, source_target_pairs={{0,1},{1,0},{8,9},{9,8},{16,17},{17,16},{24,25},{25,24}} | collective-permute-start | bytes 2162696 | tf_op jit(solution)/shard_map/ppermute | solution.py:130
  158.5 31.4 %collective-permute-start.9 = (bf16[352,1024]{1,0:T(8,128)(2,1)S(1)}, bf16[352,1024]{1,0:T(8,128)(2,1)S(1)}, u32[]{:S(2)}, u32[]{:S(2)}) collective-permute-start(bf16[352,1024]{1,0:T(8,128)(2,1)S(1)} %collective-permute-done.8.refs_6_), channel_id=1, source_target_pairs={{6,7},{7,6},{14,15},{15,14},{22,23},{23,22},{30,31},{31,30}} | collective-permute-start | bytes 2162696 | tf_op jit(solution)/shard_map/ppermute | solution.py:130
  (16 other events, 661.5 us)

commit v2 on v1

--- a/solution.py
+++ b/solution.py
@@ -11,7 +11,7 @@
 C_SLAB = 2
 CORES = 2
 TILE = 256
-CHUNKS = (4, 4)
+WHOLE_TILES = 4
 CONTRACT_FIRST = (((0,), (0,)), ((), ()))
 
 
@@ -50,7 +50,7 @@
     in_specs += [
         pl.BlockSpec(part.shape, lambda q, *_: (0, 0), pipeline_mode=pl.Buffered(1)) for part in parts
     ]
-    operands = [jnp.stack(bases).astype(jnp.int32), pos, *parts]
+    operands = [bases, pos, *parts]
     aliases = {}
     if previous is not None:
         in_specs.append(block)
@@ -131,50 +131,43 @@
     return got
 
 
-def product_kernel(slots, chunk_tiles, depth, info_ref, *refs):
+def line_kernel(slots, first_slot, depth, info_ref, *refs):
     count = len(slots)
     offsets = np.cumsum([0, *slots])
-    n_arrays = int(offsets[-1]) * len(chunk_tiles) * CORES
+    n_arrays = int(offsets[-1]) * CORES
     arrays = refs[:n_arrays]
     natural_ref, acc_ref = refs[n_arrays], refs[n_arrays + 1]
     out_ref, buffer, integrals, sems, sem_integrals = refs[n_arrays + 2 :]
     core = info_ref[0]
     tile = acc_ref.shape[0]
     i = pl.program_id(0)
-    steps = sum(chunk_tiles)
-
-    def fetch(step, slot_of_buffer):
-        first = 0
-        for h, tiles in enumerate(chunk_tiles):
-
-            @pl.when(jnp.logical_and(step >= first, step < first + tiles))
-            def _(h=h, first=first):
-                lanes = pl.ds(pl.multiple_of((step - first) * tile, tile), tile)
-                for s in range(count):
-                    for k in range(slots[s]):
-                        at = ((int(offsets[s]) + k) * len(chunk_tiles) + h) * CORES
-
-                        def start(at=at, s=s):
-                            for other in range(CORES):
-                                place = jnp.where(core == other, 0, depth) + 2 * depth * s
-                                pltpu.make_async_copy(
-                                    arrays[at + other].at[:, lanes],
-                                    buffer.at[slot_of_buffer, pl.ds(pl.multiple_of(place, 16), depth), :],
-                                    sems.at[slot_of_buffer],
-                                ).start()
-
-                        if slots[s] == 1:
-                            start()
-                        else:
-                            pl.when(info_ref[1 + s] == k)(start)
-
-            first += tiles
+    steps = arrays[0].shape[1] // tile
+
+    def fetch(step, half):
+        lanes = pl.ds(pl.multiple_of(step * tile, tile), tile)
+        for s in range(count):
+            for k in range(slots[s]):
+                at = (int(offsets[s]) + k) * CORES
+
+                def start(at=at, s=s):
+                    for other in range(CORES):
+                        place = jnp.where(core == other, 0, depth) + 2 * depth * s
+                        pltpu.make_async_copy(
+                            arrays[at + other].at[:, lanes],
+                            buffer.at[half, pl.ds(pl.multiple_of(place, 16), depth), :],
+                            sems.at[half],
+                        ).start()
+
+                if slots[s] == 1:
+                    start()
+                else:
+                    pl.when(info_ref[1 + 2 * (first_slot + s)] == k)(start)
 
     @pl.when(i == 0)
     def _():
         for s in range(count):
             pltpu.make_async_copy(
-                natural_ref.at[info_ref[1 + count + s]],
+                natural_ref.at[info_ref[2 + 2 * (first_slot + s)]],
                 integrals.at[pl.ds(2 * depth * s, 2 * depth), :],
                 sem_integrals,
             ).start()
@@ -195,22 +188,28 @@
     )
 
 
-def add_product(info, slots, natural, acc, first_tile, in_place):
+def product_cost(lanes, rows, columns):
+    return pl.CostEstimate(
+        flops=2 * lanes * rows * columns,
+        bytes_accessed=8 * lanes * columns + 2 * rows * (lanes + columns),
+        transcendentals=0,
+    )
+
+
+def add_line(info, first_slot, slots, natural, acc, first_tile, in_place):
     tile = TILE
-    chunk_tiles = tuple(pair[0].shape[1] // tile for pair in slots[0][0])
-    depth = slots[0][0][0][0].shape[0]
+    depth, lanes = slots[0][0][0].shape
     columns = natural.shape[2]
-    arrays = [a for slot in slots for candidate in slot for pair in candidate for a in pair]
+    arrays = [a for slot in slots for pair in slot for a in pair]
     anywhere = pl.BlockSpec(memory_space=pl.ANY)
     block = pl.BlockSpec((tile, columns), lambda i, *_: (first_tile + i, 0))
     operands = [info, *arrays, natural, acc]
     rows = 2 * depth * len(slots)
-    lanes = sum(chunk_tiles) * tile
     return pl.pallas_call(
-        functools.partial(product_kernel, tuple(len(slot) for slot in slots), chunk_tiles, depth),
+        functools.partial(line_kernel, tuple(len(slot) for slot in slots), first_slot, depth),
         grid_spec=pltpu.PrefetchScalarGridSpec(
             num_scalar_prefetch=1,
-            grid=(sum(chunk_tiles),),
+            grid=(lanes // tile,),
             in_specs=[anywhere] * (len(arrays) + 1) + [block],
             out_specs=block,
             scratch_shapes=[
@@ -223,70 +222,87 @@
         out_shape=jax.ShapeDtypeStruct(acc.shape, acc.dtype),
         input_output_aliases={len(operands) - 1: 0} if in_place else {},
         compiler_params=pltpu.CompilerParams(vmem_limit_bytes=32 << 20),
-        cost_estimate=pl.CostEstimate(
-            flops=2 * lanes * rows * columns,
-            bytes_accessed=8 * lanes * columns + 2 * rows * (lanes + columns),
-            transcendentals=0,
-        ),
+        cost_estimate=product_cost(lanes, rows, columns),
     )(*operands)
+
+
+def whole_kernel(t_ref, v_ref, residual_ref, acc_ref, out_ref):
+    del acc_ref
+    blocks, depth, tile = t_ref.shape
+    out_ref[...] = residual_ref[...] + lax.dot_general(
+        t_ref[...].reshape(blocks * depth, tile),
+        v_ref[...].reshape(blocks * depth, -1),
+        CONTRACT_FIRST,
+        preferred_element_type=jnp.float32,
+    )
+
+
+def add_whole(gathered, natural, residual, acc):
+    tile = TILE
+    blocks, depth, lanes = gathered.shape
+    columns = natural.shape[2]
+    block = pl.BlockSpec((tile, columns), lambda i: (i, 0))
+    return pl.pallas_call(
+        whole_kernel,
+        grid=(lanes // tile,),
+        in_specs=[
+            pl.BlockSpec((blocks, depth, tile), lambda i: (0, 0, i)),
+            pl.BlockSpec(natural.shape, lambda i: (0, 0, 0), pipeline_mode=pl.Buffered(1)),
+            block,
+            pl.BlockSpec(memory_space=pl.ANY),
+        ],
+        out_specs=block,
+        out_shape=jax.ShapeDtypeStruct(acc.shape, acc.dtype),
+        input_output_aliases={3: 0},
+        compiler_params=pltpu.CompilerParams(vmem_limit_bytes=32 << 20),
+        cost_estimate=product_cost(lanes, blocks * depth, columns),
+    )(gathered, natural, residual, acc)
 
 
 def on_device(chips, row_size, amplitudes, values_stored, irrep_virtual, residual_in):
     occ, depth = amplitudes.shape
     depth_padded = round_up(depth, 16)
-    chip = lax.axis_index("col") // CORES
-    core = lax.axis_index("col") % CORES
-    row = lax.axis_index("row")
-
-    lanes = sum(CHUNKS) * TILE
+    stored_rows = values_stored.shape[0]
+    edge = WHOLE_TILES * TILE
+    lanes = round_up(occ, TILE)
+
     columns_first = jnp.pad(amplitudes.T, ((0, depth_padded - depth), (0, lanes - occ)))
-    edges = np.cumsum([0, *CHUNKS]) * TILE
-    chunks = [columns_first[:, edges[h] : edges[h + 1]] for h in range(len(CHUNKS))]
-
-    spread = [spread_line(chunk, chips) for chunk in chunks]
+    whole, chunk = columns_first[:, :edge], columns_first[:, edge:]
+    gathered = lax.all_gather(whole, "col", axis=0)
+    spread = spread_line(chunk, chips)
     got, order, half = gather_integrals(values_stored, row_size)
 
     pos = stored_positions(irrep_virtual, chips, depth, depth_padded)
-    stored_rows = values_stored.shape[0]
-    natural = add_permuted(pos, [values_stored], [row * stored_rows], None)
-    single = [d for d in order if len(got[d]) == 1]
-    natural = add_permuted(pos, [got[d][0] for d in single], [(row ^ d) * stored_rows for d in single], natural)
-    for d in order:
-        if len(got[d]) == 2:
-            base = (row ^ d) * stored_rows
-            natural = add_permuted(pos, got[d], [base, base + half], natural)
+    groups = [[(0, 0)], [(d, 0) for d in order if len(got[d]) == 1]]
+    groups += [[(d, 0), (d, 1)] for d in order if len(got[d]) == 2]
+    natural = None
+    starts = [
+        [[(r ^ d) * stored_rows + which * half for d, which in group] for group in groups]
+        for r in range(row_size)
+    ]
+    width = max(len(group) for group in groups)
+    starts = np.array([[g + [0] * (width - len(g)) for g in of_row] for of_row in starts], np.int32)
+    bases = jnp.asarray(starts)[lax.axis_index("row")]
+    for g, group in enumerate(groups):
+        natural = add_permuted(pos, [got[d][which] for d, which in group], bases[g], natural)
 
     table = slot_table(chips)
-    slots, choices, sources = [[("own", 0)]], [jnp.int32(0)], [chip]
-    for t in range(chips - 1):
-        candidates = sorted({table[z][t][0] for z in range(chips)})
-        slots.append(candidates)
-        choices.append(jnp.asarray([candidates.index(table[z][t][0]) for z in range(chips)], jnp.int32)[chip])
-        sources.append(jnp.asarray([table[z][t][1] for z in range(chips)], jnp.int32)[chip])
-
-    def info_of(which):
-        return jnp.stack([core, *[choices[s] for s in which], *[sources[s] for s in which]]).astype(jnp.int32)
-
-    every = list(range(len(CHUNKS)))
-    early, last = list(range(chips - 1)), [chips - 1]
-    acc = add_product(
-        info_of(early),
-        [[[spread[h][c] for h in every] for c in slots[s]] for s in early],
-        natural,
-        residual_in,
-        0,
-        False,
-    )
-    for h in every:
-        acc = add_product(
-            info_of(last),
-            [[[spread[h][c]] for c in slots[s]] for s in last],
-            natural,
-            acc,
-            int(edges[h]) // TILE,
-            True,
-        )
-    return acc
+    slots = [[("own", 0)]]
+    slots += [sorted({table[z][t][0] for z in range(chips)}) for t in range(chips - 1)]
+    rows_of_info = []
+    for device in range(chips * CORES):
+        z = device // CORES
+        line = [device % CORES, 0, z]
+        for t in range(chips - 1):
+            line += [slots[t + 1].index(table[z][t][0]), table[z][t][1]]
+        rows_of_info.append(line)
+    info = jnp.asarray(np.array(rows_of_info, np.int32))[lax.axis_index("col")]
+
+    arrays = [[spread[c] for c in slot] for slot in slots]
+    last = chips - 1
+    acc = add_line(info, 0, arrays[:last], natural, residual_in, WHOLE_TILES, False)
+    acc = add_whole(gathered, natural, residual_in, acc)
+    return add_line(info, last, arrays[last:], natural, acc, WHOLE_TILES, True)
 
 
 def solution(mesh):

time: 199 us -> 189 us (0.950)
  starting transfers between devices: 47.8 us -> 27.8 us
  between operations: 0.66 us -> 13.7 us
  waiting for transfers between devices: 53.2 us -> 43.9 us
  local copies, waits for them, and re-layouts: 14.8 us -> 22.8 us
  Pallas kernels: 76.3 us -> 72.5 us
    ppermute x12 -> x6, waiting for transfers between devices: 50 us -> 18.4 us  [spread_line(): held[way] = lax.ppermute(held[way], 'col', pairs)]
    ppermute x4, waiting for transfers between devices: 3.22 us -> 25.4 us  [send(): return lax.ppermute(array, 'row', [(i, i ^ bit) for i in range(size)])]
    ppermute x12 -> x6, starting transfers between devices: 22.7 us -> 10.7 us  [spread_line(): held[way] = lax.ppermute(held[way], 'col', pairs)]
    unnamed x20, local copies, waits for them, and re-layouts: 0.89 us -> 11.6 us
    ppermute x12 -> x6, starting transfers between devices: 18.4 us -> 9.2 us  [spread_line(): got[way, s] = (held[way], lax.ppermute(held[way], 'col', swap))]
    dynamic_slice x6 -> x1, local copies, waits for them, and re-layouts: 3.74 us -> 0.68 us  [on_device(): bases = jnp.asarray(starts)[lax.axis_index('row')]]
    pallas_call x3, Pallas kernels: 38.6 us -> 35.8 us  [the longest x2 22.7 us: add_line(): pl.pallas_call(functools.partial(line_kernel, tuple((len(slot) for slot i...]
    another operation x1 -> x0, local copies, waits for them, and re-layouts: 2.62 us -> none  [info_of(): jnp.stack([core, *[choices[s] for s in which], *[sources[s] for s in whic...]
  transfers between devices with their start and end apart: 30 -> 18, of which waited for: 6 -> 2; matrix products, arithmetic and copies ran while one was open for 9% -> 8% of each run, Pallas kernels for 35% -> 34%
where the time goes in v2:
time: 189 us; the launch traced here: 186 us
  Pallas kernels  72.5 us (38%)
  waiting for transfers between devices  43.9 us (23%)
  starting transfers between devices  27.8 us (15%)
  local copies, waits for them, and re-layouts  22.8 us (12%)
  between operations  13.7 us (7%)
  other arithmetic  5.78 us (3%)
    pallas_call x3, Pallas kernels, add_permuted(): pl.pallas_call(functools.partial(permute_kernel, len(parts), previous is...  36.7 us
    ppermute x4, waiting for transfers between devices, send(): return lax.ppermute(array, 'row', [(i, i ^ bit) for i in range(size)])  25.4 us
    pallas_call x2, Pallas kernels, add_line(): pl.pallas_call(functools.partial(line_kernel, tuple((len(slot) for slot i...  22.7 us
    ppermute x6, waiting for transfers between devices, spread_line(): held[way] = lax.ppermute(held[way], 'col', pairs)  18.4 us
    pallas_call x1, Pallas kernels, add_whole(): pl.pallas_call(whole_kernel, grid=(lanes // tile,), in_specs=[pl.BlockSpe...  13.1 us
    unnamed x20, local copies, waits for them, and re-layouts  11.6 us
    ppermute x6, starting transfers between devices, spread_line(): held[way] = lax.ppermute(held[way], 'col', pairs)  10.7 us
    ppermute x6, starting transfers between devices, spread_line(): got[way, s] = (held[way], lax.ppermute(held[way], 'col', swap))  9.2 us
  transfers between devices with their start and end apart: 18, of which 2 were waited for; matrix products, arithmetic and copies ran while one was open for 8% of the time, Pallas kernels for 34%

profile of v2, /device:TPU:0, one launch (start us, length us, event | category | flops | bytes accessed | tf_op | source)
XLA Modules:
  0.0 186.4 jit_solution(1153857848177100610)
XLA Ops:
  6.5 2.4 %pad_slice_fusion = (bf16[352,1024]{1,0:T(8,128)(2,1)}, bf16[352,1024]{1,0:T(8,128)(2,1)S(1)}) fusion(bf16[350,2000]{1,0:T(8,128)(2,1)} %bitcast.12), kind=kLoop, calls=%fused_computation.1 | loop fusion | bytes 2841792 | tf_op jit(solution)/shard_map/slice | solution.py:270
  8.9 3.0 %collective-permute-start.10 = (bf16[700,1400]{1,0:T(8,128)(2,1)}, bf16[700,1400]{1,0:T(8,128)(2,1)}, u32[]{:S(2)}, u32[]{:S(2)}) collective-permute-start(bf16[700,1400]{1,0:T(8,128)(2,1)} %refs_0_.1), channel_id=1, source_target_pairs={{0,16},{8,24},{16,0},{24,8},{1,17},{9,25},{17,1},{25,9},{2,18},{10... | collective-permute-start | bytes 5880008 | tf_op jit(solution)/shard_map/ppermute | solution.py:79
  14.7 4.6 %collective-permute-start.5 = (bf16[352,1024]{1,0:T(8,128)(2,1)S(1)}, bf16[352,1024]{1,0:T(8,128)(2,1)S(1)}, u32[]{:S(2)}, u32[]{:S(2)}) collective-permute-start(bf16[352,1024]{1,0:T(8,128)(2,1)S(1)} %get-tuple-element.6.refs_0_), channel_id=1, source_target_pairs={{0,2},{1,3},{2,4},{3,5},{4,6},{5,7},{8,10},{9,11},{10,12},{11,13},... | collective-permute-start | bytes 2162696 | tf_op jit(solution)/shard_map/ppermute | solution.py:128
  22.1 3.4 %convert_reduce_fusion = s32[4,704]{1,0:T(4,128)S(1)} fusion(s32[4,704]{1,0:T(4,128)S(1)} %lt.44, s32[2800]{0:T(1024)S(1)} %iota_add_fusion), kind=kLoop, calls=%fused_computation | loop fusion | flops 23651584 | bytes 33728 | tf_op jit(solution)/shard_map/reduce_sum | solution.py:29
  25.5 1.6 copy.14
  30.0 25.4 %collective-permute-done.10.refs_1_ = bf16[700,1400]{1,0:T(8,128)(2,1)} collective-permute-done((bf16[700,1400]{1,0:T(8,128)(2,1)}, bf16[700,1400]{1,0:T(8,128)(2,1)}, u32[]{:S(2)}, u32[]{:S(2)}) %collective-permute-start.10) | collective-permute-done | bytes 1960032 | tf_op jit(solution)/shard_map/ppermute | solution.py:79
  56.8 1.7 collective-permute-start.11
  59.8 1.6 collective-permute-start.13
  61.4 1.5 broadcast_select_fusion.pos_ref
  64.2 1.9 %collective-permute-start.15 = (bf16[352,1024]{1,0:T(8,128)(2,1)}, bf16[352,1024]{1,0:T(8,128)(2,1)S(1)}, u32[]{:S(2)}, u32[]{:S(2)}) collective-permute-start(bf16[352,1024]{1,0:T(8,128)(2,1)} %collective-permute-done.refs_2_), channel_id=1, source_target_pairs={{0,1},{1,0},{2,3},{3,2},{4,5},{5,4},{8,9},{9,8},{10,11},{11,10},{1... | collective-permute-start | bytes 2162696 | tf_op jit(solution)/shard_map/ppermute | solution.py:130
  67.8 8.3 %shard_map.64.refs_2_ = bf16[4,704,1400]{2,1,0:T(8,128)(2,1)S(1)} custom-call(s32[2]{0:T(128)S(1)} %get-tuple-element.7.base_ref, s32[4,704,1]{2,1,0:T(8,128)S(1)} %broadcast_select_fusion.pos_ref, bf16[700,1400]{1,0:T(8,128)(2,1)S(1)} %copy-done.9), custom_call_target="tpu_custom_call" | custom-call | flops 5519360000 | bytes 15769600 | tf_op jit(solution)/shard_map/pallas_call | solution.py:59
  76.1 18.4 %collective-permute-done.1.refs_6_.refs_0_ = bf16[352,1024]{1,0:T(8,128)(2,1)S(1)} collective-permute-done((bf16[352,1024]{1,0:T(8,128)(2,1)}, bf16[352,1024]{1,0:T(8,128)(2,1)S(1)}, u32[]{:S(2)}, u32[]{:S(2)}) %collective-permute-start.1) | collective-permute-done | bytes 720928 | tf_op jit(solution)/shard_map/ppermute | solution.py:128
  95.1 1.9 %collective-permute-start.2 = (bf16[352,1024]{1,0:T(8,128)(2,1)S(1)}, bf16[352,1024]{1,0:T(8,128)(2,1)S(1)}, u32[]{:S(2)}, u32[]{:S(2)}) collective-permute-start(bf16[352,1024]{1,0:T(8,128)(2,1)S(1)} %collective-permute-done.1.refs_6_.refs_0_), channel_id=1, source_target_pairs={{0,1},{1,0},{2,3},{3,2},{8,9},{9,8},{10,11},{11,10},{16,17},{17,16... | collective-permute-start | bytes 2162696 | tf_op jit(solution)/shard_map/ppermute | solution.py:130
  99.1 1.5 collective-permute-start.8
  100.7 17.8 %shard_map.65.refs_2_ = bf16[4,704,1400]{2,1,0:T(8,128)(2,1)S(1)} custom-call(s32[2]{0:T(128)S(1)} %get-tuple-element.8.base_ref, s32[4,704,1]{2,1,0:T(8,128)S(1)} %broadcast_select_fusion.pos_ref, bf16[700,1400]{1,0:T(8,128)(2,1)} %collective-permute-done.12.refs_0_, ...), custom_call_target="tpu_custom_call", output_to_operand_aliasing={{}: (4, {})} | custom-call | flops 11038720000 | bytes 15769600 | tf_op jit(solution)/shard_map/pallas_call | solution.py:59
  118.5 10.6 %shard_map.66.refs_12_.v_ref.refs_8_ = bf16[4,704,1400]{2,1,0:T(8,128)(2,1)S(1)} custom-call(s32[2]{0:T(128)S(1)} %get-tuple-element.9.base_ref, s32[4,704,1]{2,1,0:T(8,128)S(1)} %broadcast_select_fusion.pos_ref, bf16[352,1400]{1,0:T(8,128)(2,1)S(1)} %collective-permute-done.11.refs_0_, ...), custom_call_target="tpu_custom_call", output_to_operand_aliasing={{}: (4, {})} | custom-call | flops 5519360000 | bytes 15769600 | tf_op jit(solution)/shard_map/pallas_call | solution.py:59
  129.1 2.4 %collective-permute-start.4 = (bf16[352,1024]{1,0:T(8,128)(2,1)}, bf16[352,1024]{1,0:T(8,128)(2,1)}, u32[]{:S(2)}, u32[]{:S(2)}) collective-permute-start(bf16[352,1024]{1,0:T(8,128)(2,1)} %collective-permute-done.3.refs_2_), channel_id=1, source_target_pairs={{0,1},{1,0},{8,9},{9,8},{16,17},{17,16},{24,25},{25,24}} | collective-permute-start | bytes 2162696 | tf_op jit(solution)/shard_map/ppermute | solution.py:130
  131.5 1.5 collective-permute-start.9
  133.1 13.5 %shard_map.67.acc_ref = f32[2000,1400]{1,0:T(8,128)} custom-call(s32[9]{0:T(128)S(1)} %dynamic-slice_bitcast_fusion.info_ref, bf16[352,1024]{1,0:T(8,128)(2,1)S(1)} %get-tuple-element.6.refs_0_, bf16[352,1024]{1,0:T(8,128)(2,1)S(1)} %copy-done.8, bf16[352,1024]{1,0:T(8,128)(2,1)} %collective-permute-done.refs_2_, ...), custom_call_target="tpu_custom_call" | custom-call | flops 6055526400 | bytes 21707776 | tf_op jit(solution)/shard_map/pallas_call | solution.py:208
  146.6 3.1 %copy-done = bf16[4,704,1400]{2,1,0:T(8,128)(2,1)} copy-done((bf16[4,704,1400]{2,1,0:T(8,128)(2,1)}, bf16[4,704,1400]{2,1,0:T(8,128)(2,1)S(1)}, u32[]{:S(2)}) %copy-start) | copy-done | bytes 7884824
  151.4 3.2 %copy-done.1 = bf16[4,704,1400]{2,1,0:T(8,128)(2,1)S(1)} copy-done((bf16[4,704,1400]{2,1,0:T(8,128)(2,1)S(1)}, bf16[4,704,1400]{2,1,0:T(8,128)(2,1)}, u32[]{:S(2)}) %copy-start.1) | copy-done | bytes 7884824
  154.7 2.6 %copy-done.2 = bf16[2816,1024]{1,0:T(8,128)(2,1)S(1)} copy-done((bf16[2816,1024]{1,0:T(8,128)(2,1)S(1)}, bf16[2816,1024]{1,0:T(8,128)(2,1)}, u32[]{:S(2)}) %copy-start.2) | copy-done | bytes 5767192
  157.3 13.1 %shard_map.68.refs_9_ = f32[2000,1400]{1,0:T(8,128)} custom-call(bf16[8,352,1024]{2,1,0:T(8,128)(2,1)S(1)} %bitcast.11, bf16[4,704,1400]{2,1,0:T(8,128)(2,1)S(1)} %copy-done.1, f32[2000,1400]{1,0:T(8,128)} %residual_ref.1, f32[2000,1400]{1,0:T(8,128)} %shard_map.67.acc_ref), custom_call_target="tpu_custom_call", output_to_operand_aliasing={{}: (3, {})} | custom-call | flops 8074035200 | bytes 25120768 | tf_op jit(solution)/shard_map/pallas_call | solution.py:245
  170.4 9.2 %shard_map.69 = f32[2000,1400]{1,0:T(8,128)} custom-call(s32[9]{0:T(128)S(1)} %dynamic-slice_bitcast_fusion.info_ref, bf16[352,1024]{1,0:T(8,128)(2,1)S(1)} %collective-permute-done.1.refs_6_.refs_0_, bf16[352,1024]{1,0:T(8,128)(2,1)S(1)} %copy-done.4, bf16[352,1024]{1,0:T(8,128)(2,1)} %collective-permute-done.3.refs_2_, ...), custom_call_target="tpu_custom_call", output_to_operand_aliasing={{}: (10, {})} | custom-call | flops 2018508800 | bytes 14881792 | tf_op jit(solution)/shard_map/pallas_call | solution.py:208
  (62 shorter events, 18.4 us)
Async XLA Ops:
  6.5 144.9 %all-gather.3.cloned.1.call-start = ((), (), s32[]{:S(2)}) async-start(), calls=%async_computation | async-start | bytes 6488064 | tf_op jit(solution)/shard_map/all_gather | solution.py:271
  8.9 46.5 %collective-permute-start.10 = (bf16[700,1400]{1,0:T(8,128)(2,1)}, bf16[700,1400]{1,0:T(8,128)(2,1)}, u32[]{:S(2)}, u32[]{:S(2)}) collective-permute-start(bf16[700,1400]{1,0:T(8,128)(2,1)} %refs_0_.1), channel_id=1, source_target_pairs={{0,16},{8,24},{16,0},{24,8},{1,17},{9,25},{17,1},{25,9},{2,18},{10... | collective-permute-start | bytes 5880008 | tf_op jit(solution)/shard_map/ppermute | solution.py:79
  11.9 46.5 %collective-permute-start.12 = (bf16[700,1400]{1,0:T(8,128)(2,1)}, bf16[700,1400]{1,0:T(8,128)(2,1)}, u32[]{:S(2)}, u32[]{:S(2)}) collective-permute-start(bf16[700,1400]{1,0:T(8,128)(2,1)} %refs_0_.1), channel_id=1, source_target_pairs={{0,8},{8,0},{16,24},{24,16},{1,9},{9,1},{17,25},{25,17},{2,10},{10... | collective-permute-start | bytes 5880008 | tf_op jit(solution)/shard_map/ppermute | solution.py:79
  13.4 49.5 %collective-permute-start = (bf16[352,1024]{1,0:T(8,128)(2,1)S(1)}, bf16[352,1024]{1,0:T(8,128)(2,1)}, u32[]{:S(2)}, u32[]{:S(2)}) collective-permute-start(bf16[352,1024]{1,0:T(8,128)(2,1)S(1)} %get-tuple-element.6.refs_0_), channel_id=1, source_target_pairs={{2,0},{3,1},{4,2},{5,3},{6,4},{7,5},{10,8},{11,9},{12,10},{13,11},... | collective-permute-start | bytes 2162696 | tf_op jit(solution)/shard_map/ppermute | solution.py:128
  14.7 49.5 %collective-permute-start.5 = (bf16[352,1024]{1,0:T(8,128)(2,1)S(1)}, bf16[352,1024]{1,0:T(8,128)(2,1)S(1)}, u32[]{:S(2)}, u32[]{:S(2)}) collective-permute-start(bf16[352,1024]{1,0:T(8,128)(2,1)S(1)} %get-tuple-element.6.refs_0_), channel_id=1, source_target_pairs={{0,2},{1,3},{2,4},{3,5},{4,6},{5,7},{8,10},{9,11},{10,12},{11,13},... | collective-permute-start | bytes 2162696 | tf_op jit(solution)/shard_map/ppermute | solution.py:128
  19.3 46.8 %collective-permute-start.14 = (bf16[352,1024]{1,0:T(8,128)(2,1)S(1)}, bf16[352,1024]{1,0:T(8,128)(2,1)S(1)}, u32[]{:S(2)}, u32[]{:S(2)}) collective-permute-start(bf16[352,1024]{1,0:T(8,128)(2,1)S(1)} %get-tuple-element.6.refs_0_), channel_id=1, source_target_pairs={{0,1},{1,0},{2,3},{3,2},{4,5},{5,4},{6,7},{7,6},{8,9},{9,8},{10,11... | collective-permute-start | bytes 2162696 | tf_op jit(solution)/shard_map/ppermute | solution.py:116
  28.5 39.3 %copy-start.9 = (bf16[700,1400]{1,0:T(8,128)(2,1)S(1)}, bf16[700,1400]{1,0:T(8,128)(2,1)}, u32[]{:S(2)}) copy-start(bf16[700,1400]{1,0:T(8,128)(2,1)} %refs_0_.1) | copy-start | bytes 5880004
  56.8 42.4 %collective-permute-start.11 = (bf16[352,1400]{1,0:T(8,128)(2,1)S(1)}, bf16[352,1400]{1,0:T(8,128)(2,1)S(1)}, u32[]{:S(2)}, u32[]{:S(2)}) collective-permute-start(bf16[352,1400]{1,0:T(8,128)(2,1)S(1)} %slice.35), channel_id=1, source_target_pairs={{0,8},{8,0},{16,24},{24,16},{1,9},{9,1},{17,25},{25,17},{2,10},{10... | collective-permute-start | bytes 2956808 | tf_op jit(solution)/shard_map/ppermute | solution.py:79
  59.8 38.6 %collective-permute-start.13 = (bf16[348,1400]{1,0:T(8,128)(2,1)S(1)}, bf16[348,1400]{1,0:T(8,128)(2,1)S(1)}, u32[]{:S(2)}, u32[]{:S(2)}) collective-permute-start(bf16[348,1400]{1,0:T(8,128)(2,1)S(1)} %slice.36), channel_id=1, source_target_pairs={{0,16},{8,24},{16,0},{24,8},{1,17},{9,25},{17,1},{25,9},{2,18},{10... | collective-permute-start | bytes 2923208 | tf_op jit(solution)/shard_map/ppermute | solution.py:79
  62.9 31.5 %collective-permute-start.1 = (bf16[352,1024]{1,0:T(8,128)(2,1)}, bf16[352,1024]{1,0:T(8,128)(2,1)S(1)}, u32[]{:S(2)}, u32[]{:S(2)}) collective-permute-start(bf16[352,1024]{1,0:T(8,128)(2,1)} %collective-permute-done.refs_2_), channel_id=1, source_target_pairs={{2,0},{3,1},{4,2},{5,3},{10,8},{11,9},{12,10},{13,11},{18,16},{19,... | collective-permute-start | bytes 2162696 | tf_op jit(solution)/shard_map/ppermute | solution.py:128
  64.2 32.8 %collective-permute-start.15 = (bf16[352,1024]{1,0:T(8,128)(2,1)}, bf16[352,1024]{1,0:T(8,128)(2,1)S(1)}, u32[]{:S(2)}, u32[]{:S(2)}) collective-permute-start(bf16[352,1024]{1,0:T(8,128)(2,1)} %collective-permute-done.refs_2_), channel_id=1, source_target_pairs={{0,1},{1,0},{2,3},{3,2},{4,5},{5,4},{8,9},{9,8},{10,11},{11,10},{1... | collective-permute-start | bytes 2162696 | tf_op jit(solution)/shard_map/ppermute | solution.py:130
  67.0 28.1 %collective-permute-start.6 = (bf16[352,1024]{1,0:T(8,128)(2,1)S(1)}, bf16[352,1024]{1,0:T(8,128)(2,1)S(1)}, u32[]{:S(2)}, u32[]{:S(2)}) collective-permute-start(bf16[352,1024]{1,0:T(8,128)(2,1)S(1)} %collective-permute-done.5.refs_4_.refs_8_), channel_id=1, source_target_pairs={{2,4},{3,5},{4,6},{5,7},{10,12},{11,13},{12,14},{13,15},{18,20},{1... | collective-permute-start | bytes 2162696 | tf_op jit(solution)/shard_map/ppermute | solution.py:128
  94.4 38.6 %collective-permute-start.16 = (bf16[352,1024]{1,0:T(8,128)(2,1)S(1)}, bf16[352,1024]{1,0:T(8,128)(2,1)S(1)}, u32[]{:S(2)}, u32[]{:S(2)}) collective-permute-start(bf16[352,1024]{1,0:T(8,128)(2,1)S(1)} %collective-permute-done.5.refs_4_.refs_8_), channel_id=1, source_target_pairs={{2,3},{3,2},{4,5},{5,4},{6,7},{7,6},{10,11},{11,10},{12,13},{13,12... | collective-permute-start | bytes 2162696 | tf_op jit(solution)/shard_map/ppermute | solution.py:130
  95.1 37.9 %collective-permute-start.2 = (bf16[352,1024]{1,0:T(8,128)(2,1)S(1)}, bf16[352,1024]{1,0:T(8,128)(2,1)S(1)}, u32[]{:S(2)}, u32[]{:S(2)}) collective-permute-start(bf16[352,1024]{1,0:T(8,128)(2,1)S(1)} %collective-permute-done.1.refs_6_.refs_0_), channel_id=1, source_target_pairs={{0,1},{1,0},{2,3},{3,2},{8,9},{9,8},{10,11},{11,10},{16,17},{17,16... | collective-permute-start | bytes 2162696 | tf_op jit(solution)/shard_map/ppermute | solution.py:130
  97.1 32.0 %collective-permute-start.3 = (bf16[352,1024]{1,0:T(8,128)(2,1)S(1)}, bf16[352,1024]{1,0:T(8,128)(2,1)}, u32[]{:S(2)}, u32[]{:S(2)}) collective-permute-start(bf16[352,1024]{1,0:T(8,128)(2,1)S(1)} %collective-permute-done.1.refs_6_.refs_0_), channel_id=1, source_target_pairs={{2,0},{3,1},{10,8},{11,9},{18,16},{19,17},{26,24},{27,25}} | collective-permute-start | bytes 2162696 | tf_op jit(solution)/shard_map/ppermute | solution.py:128
  98.4 34.7 %collective-permute-start.7 = (bf16[352,1024]{1,0:T(8,128)(2,1)S(1)}, bf16[352,1024]{1,0:T(8,128)(2,1)S(1)}, u32[]{:S(2)}, u32[]{:S(2)}) collective-permute-start(bf16[352,1024]{1,0:T(8,128)(2,1)S(1)} %collective-permute-done.6.refs_10_.refs_4_), channel_id=1, source_target_pairs={{4,5},{5,4},{6,7},{7,6},{12,13},{13,12},{14,15},{15,14},{20,21},{2... | collective-permute-start | bytes 2162696 | tf_op jit(solution)/shard_map/ppermute | solution.py:130
  99.1 32.4 %collective-permute-start.8 = (bf16[352,1024]{1,0:T(8,128)(2,1)S(1)}, bf16[352,1024]{1,0:T(8,128)(2,1)}, u32[]{:S(2)}, u32[]{:S(2)}) collective-permute-start(bf16[352,1024]{1,0:T(8,128)(2,1)S(1)} %collective-permute-done.6.refs_10_.refs_4_), channel_id=1, source_target_pairs={{4,6},{5,7},{12,14},{13,15},{20,22},{21,23},{28,30},{29,31}} | collective-permute-start | bytes 2162696 | tf_op jit(solution)/shard_map/ppermute | solution.py:128
  118.5 14.6 %copy-start.8 = (bf16[352,1024]{1,0:T(8,128)(2,1)S(1)}, bf16[352,1024]{1,0:T(8,128)(2,1)}, u32[]{:S(2)}) copy-start(bf16[352,1024]{1,0:T(8,128)(2,1)} %copy-done.7) | copy-start | bytes 2162692
  129.1 41.3 %collective-permute-start.4 = (bf16[352,1024]{1,0:T(8,128)(2,1)}, bf16[352,1024]{1,0:T(8,128)(2,1)}, u32[]{:S(2)}, u32[]{:S(2)}) collective-permute-start(bf16[352,1024]{1,0:T(8,128)(2,1)} %collective-permute-done.3.refs_2_), channel_id=1, source_target_pairs={{0,1},{1,0},{8,9},{9,8},{16,17},{17,16},{24,25},{25,24}} | collective-permute-start | bytes 2162696 | tf_op jit(solution)/shard_map/ppermute | solution.py:130
  131.5 38.9 %collective-permute-start.9 = (bf16[352,1024]{1,0:T(8,128)(2,1)}, bf16[352,1024]{1,0:T(8,128)(2,1)}, u32[]{:S(2)}, u32[]{:S(2)}) collective-permute-start(bf16[352,1024]{1,0:T(8,128)(2,1)} %collective-permute-done.8.refs_6_), channel_id=1, source_target_pairs={{6,7},{7,6},{14,15},{15,14},{22,23},{23,22},{30,31},{31,30}} | collective-permute-start | bytes 2162696 | tf_op jit(solution)/shard_map/ppermute | solution.py:130
  146.6 3.1 %copy-start = (bf16[4,704,1400]{2,1,0:T(8,128)(2,1)}, bf16[4,704,1400]{2,1,0:T(8,128)(2,1)S(1)}, u32[]{:S(2)}) copy-start(bf16[4,704,1400]{2,1,0:T(8,128)(2,1)S(1)} %shard_map.66.refs_12_.v_ref.refs_8_) | copy-start | bytes 23654404
  151.4 3.3 %copy-start.1 = (bf16[4,704,1400]{2,1,0:T(8,128)(2,1)S(1)}, bf16[4,704,1400]{2,1,0:T(8,128)(2,1)}, u32[]{:S(2)}) copy-start(bf16[4,704,1400]{2,1,0:T(8,128)(2,1)} %copy-done) | copy-start | bytes 23654404
  157.3 13.1 %copy-start.4 = (bf16[352,1024]{1,0:T(8,128)(2,1)S(1)}, bf16[352,1024]{1,0:T(8,128)(2,1)}, u32[]{:S(2)}) copy-start(bf16[352,1024]{1,0:T(8,128)(2,1)} %copy-done.3) | copy-start | bytes 2162692
  157.3 13.1 %copy-start.6 = (bf16[352,1024]{1,0:T(8,128)(2,1)S(1)}, bf16[352,1024]{1,0:T(8,128)(2,1)}, u32[]{:S(2)}) copy-start(bf16[352,1024]{1,0:T(8,128)(2,1)} %copy-done.5) | copy-start | bytes 2162692
  (4 other events, 5.2 us)
Sparse Core Ops, SparseCore 0:
  9.0 78.5 all-gather.2

commit v3 on v2

--- a/solution.py
+++ b/solution.py
@@ -11,6 +11,7 @@
 C_SLAB = 2
 CORES = 2
 TILE = 256
+VMEM_BYTES = 58 << 20
 WHOLE_TILES = 4
 CONTRACT_FIRST = (((0,), (0,)), ((), ()))
 
@@ -63,7 +64,7 @@
         ),
         out_shape=jax.ShapeDtypeStruct((chips, rows, columns), parts[0].dtype),
         input_output_aliases=aliases,
-        compiler_params=pltpu.CompilerParams(vmem_limit_bytes=32 << 20),
+        compiler_params=pltpu.CompilerParams(vmem_limit_bytes=VMEM_BYTES),
         cost_estimate=pl.CostEstimate(
             flops=2 * chips * rows * columns * sum(part.shape[0] for part in parts),
             bytes_accessed=4 * chips * rows * columns,
@@ -110,25 +111,24 @@
     return table
 
 
-def spread_line(chunk, chips):
-    got = {}
-    swap_all = [(i, i ^ 1) for i in range(chips * CORES)]
-    got["own", 0] = (chunk, lax.ppermute(chunk, "col", swap_all))
-    held = {"L": chunk, "R": chunk}
-    for s in range(1, chips):
-        for way, step in (("L", -1), ("R", 1)):
-            pairs = []
-            ends = []
-            for z in range(chips):
-                source = z + s if step < 0 else z - s
-                if 0 <= source < chips:
-                    ends.append(z)
-                    for core in range(CORES):
-                        pairs.append(((z - step) * CORES + core, z * CORES + core))
-            held[way] = lax.ppermute(held[way], "col", pairs)
-            swap = [(z * CORES + core, z * CORES + 1 - core) for z in ends for core in range(CORES)]
-            got[way, s] = (held[way], lax.ppermute(held[way], "col", swap))
-    return got
+def line_step(held, s, chips):
+    arrived = {}
+    for way, step in (("L", -1), ("R", 1)):
+        pairs = []
+        for z in range(chips):
+            if 0 <= z - step * s < chips:
+                pairs += [((z - step) * CORES + core, z * CORES + core) for core in range(CORES)]
+        arrived[way] = lax.ppermute(held[way], "col", pairs)
+    return arrived
+
+
+def swap_cores(block, way, s, chips):
+    step = {"L": -1, "R": 1}[way]
+    pairs = []
+    for z in range(chips):
+        if 0 <= z - step * s < chips:
+            pairs += [(z * CORES + core, z * CORES + 1 - core) for core in range(CORES)]
+    return lax.ppermute(block, "col", pairs)
 
 
 def line_kernel(slots, first_slot, depth, info_ref, *refs):
@@ -221,7 +221,7 @@
         ),
         out_shape=jax.ShapeDtypeStruct(acc.shape, acc.dtype),
         input_output_aliases={len(operands) - 1: 0} if in_place else {},
-        compiler_params=pltpu.CompilerParams(vmem_limit_bytes=32 << 20),
+        compiler_params=pltpu.CompilerParams(vmem_limit_bytes=VMEM_BYTES),
         cost_estimate=product_cost(lanes, rows, columns),
     )(*operands)
 
@@ -254,7 +254,7 @@
         out_specs=block,
         out_shape=jax.ShapeDtypeStruct(acc.shape, acc.dtype),
         input_output_aliases={3: 0},
-        compiler_params=pltpu.CompilerParams(vmem_limit_bytes=32 << 20),
+        compiler_params=pltpu.CompilerParams(vmem_limit_bytes=VMEM_BYTES),
         cost_estimate=product_cost(lanes, blocks * depth, columns),
     )(gathered, natural, residual, acc)
 
@@ -269,13 +269,13 @@
     columns_first = jnp.pad(amplitudes.T, ((0, depth_padded - depth), (0, lanes - occ)))
     whole, chunk = columns_first[:, :edge], columns_first[:, edge:]
     gathered = lax.all_gather(whole, "col", axis=0)
-    spread = spread_line(chunk, chips)
+    held = line_step({"L": chunk, "R": chunk}, 1, chips)
     got, order, half = gather_integrals(values_stored, row_size)
+    spread = {("own", 0): (chunk, swap_cores(chunk, "L", 0, chips))}
 
     pos = stored_positions(irrep_virtual, chips, depth, depth_padded)
     groups = [[(0, 0)], [(d, 0) for d in order if len(got[d]) == 1]]
     groups += [[(d, 0), (d, 1)] for d in order if len(got[d]) == 2]
-    natural = None
     starts = [
         [[(r ^ d) * stored_rows + which * half for d, which in group] for group in groups]
         for r in range(row_size)
@@ -283,8 +283,22 @@
     width = max(len(group) for group in groups)
     starts = np.array([[g + [0] * (width - len(g)) for g in of_row] for of_row in starts], np.int32)
     bases = jnp.asarray(starts)[lax.axis_index("row")]
+    naturals = [None]
     for g, group in enumerate(groups):
-        natural = add_permuted(pos, [got[d][which] for d, which in group], bases[g], natural)
+        naturals.append(add_permuted(pos, [got[d][which] for d, which in group], bases[g], naturals[-1]))
+        s = g + 1
+        if s < chips - 1:
+            held["L"], held["R"], naturals[-1] = lax.optimization_barrier((held["L"], held["R"], naturals[-1]))
+            following = line_step(held, s + 1, chips)
+            for way in ("L", "R"):
+                spread[way, s] = (held[way], swap_cores(held[way], way, s, chips))
+            held = following
+    for s in range(len(groups) + 1, chips - 1):
+        following = line_step(held, s + 1, chips)
+        for way in ("L", "R"):
+            spread[way, s] = (held[way], swap_cores(held[way], way, s, chips))
+        held = following
+    natural = naturals[-1]
 
     table = slot_table(chips)
     slots = [[("own", 0)]]
@@ -298,11 +312,14 @@
         rows_of_info.append(line)
     info = jnp.asarray(np.array(rows_of_info, np.int32))[lax.axis_index("col")]
 
-    arrays = [[spread[c] for c in slot] for slot in slots]
     last = chips - 1
-    acc = add_line(info, 0, arrays[:last], natural, residual_in, WHOLE_TILES, False)
+    early = [[spread[c] for c in slot] for slot in slots[:last]]
+    acc = add_line(info, 0, early, natural, residual_in, WHOLE_TILES, False)
+    held["L"], held["R"], acc = lax.optimization_barrier((held["L"], held["R"], acc))
+    for way in ("L", "R"):
+        spread[way, last] = (held[way], swap_cores(held[way], way, last, chips))
     acc = add_whole(gathered, natural, residual_in, acc)
-    return add_line(info, last, arrays[last:], natural, acc, WHOLE_TILES, True)
+    return add_line(info, last, [[spread[c] for c in slots[last]]], natural, acc, WHOLE_TILES, True)
 
 
 def solution(mesh):

time: 189 us -> 192 us (1.016); the launches traced: 186 us -> 192 us
  Pallas kernels: 72.5 us -> 84.2 us
  local copies, waits for them, and re-layouts: 22.8 us -> 16.7 us
    ppermute x4, waiting for transfers between devices: 25.4 us -> 0.01 us  [send(): return lax.ppermute(array, 'row', [(i, i ^ bit) for i in range(size)])]
    ppermute x13, waiting for transfers between devices: 18.4 us -> 43.8 us  [the longest x6 43.8 us: line_step(): arrived[way] = lax.ppermute(held[way], 'col', pairs)]
    pallas_call x3, Pallas kernels: 36.7 us -> 44.6 us  [add_permuted(): pl.pallas_call(functools.partial(permute_kernel, len(parts), previous is...]
    unnamed x20 -> x16, local copies, waits for them, and re-layouts: 11.6 us -> 3.67 us
    pallas_call x1, Pallas kernels: 13.1 us -> 15.1 us  [add_whole(): pl.pallas_call(whole_kernel, grid=(lanes // tile,), in_specs=[pl.BlockSpe...]
  transfers between devices with their start and end apart: 18 -> 18, of which waited for: 2 -> 2; matrix products, arithmetic and copies ran while one was open for 8% -> 8% of each run, Pallas kernels for 34% -> 39%
where the time goes in v3:
time: 192 us
  Pallas kernels  84.2 us (44%)
  waiting for transfers between devices  43.8 us (23%)
  starting transfers between devices  27.6 us (14%)
  local copies, waits for them, and re-layouts  16.7 us (9%)
  between operations  13.7 us (7%)
  other arithmetic  5.51 us (3%)
    pallas_call x3, Pallas kernels, add_permuted(): pl.pallas_call(functools.partial(permute_kernel, len(parts), previous is...  44.6 us
    ppermute x6, waiting for transfers between devices, line_step(): arrived[way] = lax.ppermute(held[way], 'col', pairs)  43.8 us
    pallas_call x2, Pallas kernels, add_line(): pl.pallas_call(functools.partial(line_kernel, tuple((len(slot) for slot i...  24.5 us
    pallas_call x1, Pallas kernels, add_whole(): pl.pallas_call(whole_kernel, grid=(lanes // tile,), in_specs=[pl.BlockSpe...  15.1 us
    ppermute x6, starting transfers between devices, line_step(): arrived[way] = lax.ppermute(held[way], 'col', pairs)  11.9 us
    ppermute x7, starting transfers between devices, swap_cores(): return lax.ppermute(block, 'col', pairs)  9.72 us
    ppermute x4, starting transfers between devices, send(): return lax.ppermute(array, 'row', [(i, i ^ bit) for i in range(size)])  5.99 us
    slice x2, local copies, waits for them, and re-layouts, gather_integrals(): piece = source[0][:half] if which == 0 else source[0][half:]  4.49 us
  transfers between devices with their start and end apart: 18, of which 2 were waited for; matrix products, arithmetic and copies ran while one was open for 8% of the time, Pallas kernels for 39%

profile of v3, /device:TPU:0, one launch (start us, length us, event | category | flops | bytes accessed | tf_op | source)
XLA Modules:
  0.0 191.6 jit_solution(15400886539500973557)
XLA Ops:
  6.5 2.4 %pad_slice_fusion = (bf16[352,1024]{1,0:T(8,128)(2,1)}, bf16[352,1024]{1,0:T(8,128)(2,1)S(1)}) fusion(bf16[350,2000]{1,0:T(8,128)(2,1)} %bitcast.12), kind=kLoop, calls=%fused_computation.1 | loop fusion | bytes 2841792 | tf_op jit(solution)/shard_map/slice | solution.py:270
  9.0 5.0 %collective-permute-start.1 = (bf16[352,1024]{1,0:T(8,128)(2,1)S(1)}, bf16[352,1024]{1,0:T(8,128)(2,1)S(1)}, u32[]{:S(2)}, u32[]{:S(2)}) collective-permute-start(bf16[352,1024]{1,0:T(8,128)(2,1)S(1)} %get-tuple-element.24.refs_0_), channel_id=1, source_target_pairs={{0,2},{1,3},{2,4},{3,5},{4,6},{5,7},{8,10},{9,11},{10,12},{11,13},... | collective-permute-start | bytes 2162696 | tf_op jit(solution)/shard_map/ppermute | solution.py:121
  15.3 1.6 collective-permute-start.5
  16.8 1.5 collective-permute-start.4
  21.0 3.4 %convert_reduce_fusion = s32[4,704]{1,0:T(4,128)S(1)} fusion(s32[4,704]{1,0:T(4,128)S(1)} %lt.44, s32[2800]{0:T(1024)S(1)} %iota_add_fusion), kind=kLoop, calls=%fused_computation | loop fusion | flops 23651584 | bytes 33728 | tf_op jit(solution)/shard_map/reduce_sum | solution.py:30
  24.4 1.4 lt.47
  28.8 11.5 %shard_map.64.refs_2_ = bf16[4,704,1400]{2,1,0:T(8,128)(2,1)} custom-call(s32[2]{0:T(128)} %get-tuple-element.27.base_ref, s32[4,704,1]{2,1,0:T(8,128)} %broadcast_select_fusion.pos_ref, bf16[700,1400]{1,0:T(8,128)(2,1)} %refs_0_.1), custom_call_target="tpu_custom_call" | custom-call | flops 5519360000 | bytes 15769600 | tf_op jit(solution)/shard_map/pallas_call | solution.py:60
  40.2 17.6 %collective-permute-done.refs_2_ = bf16[352,1024]{1,0:T(8,128)(2,1)} collective-permute-done((bf16[352,1024]{1,0:T(8,128)(2,1)S(1)}, bf16[352,1024]{1,0:T(8,128)(2,1)}, u32[]{:S(2)}, u32[]{:S(2)}) %collective-permute-start) | collective-permute-done | bytes 720928 | tf_op jit(solution)/shard_map/ppermute | solution.py:121
  59.2 2.4 %collective-permute-start.10 = (bf16[352,1024]{1,0:T(8,128)(2,1)}, bf16[352,1024]{1,0:T(8,128)(2,1)}, u32[]{:S(2)}, u32[]{:S(2)}) collective-permute-start(bf16[352,1024]{1,0:T(8,128)(2,1)} %collective-permute-done.refs_2_), channel_id=1, source_target_pairs={{0,1},{1,0},{2,3},{3,2},{4,5},{5,4},{8,9},{9,8},{10,11},{11,10},{1... | collective-permute-start | bytes 2162696 | tf_op jit(solution)/shard_map/ppermute | solution.py:131
  61.6 1.5 collective-permute-start.3
  63.1 2.2 %slice.35 = bf16[352,1400]{1,0:T(8,128)(2,1)} slice(bf16[700,1400]{1,0:T(8,128)(2,1)} %collective-permute-done.5.refs_1_), slice={[0:352], [0:1400]} | slice | bytes 1971200 | tf_op jit(solution)/shard_map/slice | solution.py:95
  65.4 1.4 collective-permute-start.13
  66.8 2.2 %slice.36 = bf16[348,1400]{1,0:T(8,128)(2,1)} slice(bf16[700,1400]{1,0:T(8,128)(2,1)} %collective-permute-done.4.refs_0_), slice={[352:700], [0:1400]} | slice | bytes 1948800 | tf_op jit(solution)/shard_map/slice | solution.py:95
  69.0 26.2 %collective-permute-done.2.refs_6_.refs_0_ = bf16[352,1024]{1,0:T(8,128)(2,1)S(1)} collective-permute-done((bf16[352,1024]{1,0:T(8,128)(2,1)}, bf16[352,1024]{1,0:T(8,128)(2,1)S(1)}, u32[]{:S(2)}, u32[]{:S(2)}) %collective-permute-start.2) | collective-permute-done | bytes 720928 | tf_op jit(solution)/shard_map/ppermute | solution.py:121
  95.2 1.5 collective-permute-start.14
  96.7 19.3 %shard_map.65.refs_2_ = bf16[4,704,1400]{2,1,0:T(8,128)(2,1)} custom-call(s32[2]{0:T(128)} %get-tuple-element.26.base_ref, s32[4,704,1]{2,1,0:T(8,128)} %broadcast_select_fusion.pos_ref, bf16[700,1400]{1,0:T(8,128)(2,1)} %collective-permute-done.4.refs_0_, bf16[700,1400]{1,0:T(8,128)(2,1)} %collective-permute-done.5.refs_1_, ...), custom_call_target="tpu_custom_call", output_to_operand_aliasing={{}: (4, {})} | custom-call | flops 11038720000 | bytes 15769600 | tf_op jit(solution)/shard_map/pallas_call | solution.py:60
  117.7 1.9 collective-permute-start.6
  119.6 1.5 collective-permute-start.12
  123.6 1.5 collective-permute-start.8
  125.2 13.9 %shard_map.66.refs_12_.v_ref.refs_8_ = bf16[4,704,1400]{2,1,0:T(8,128)(2,1)} custom-call(s32[2]{0:T(128)} %get-tuple-element.25.base_ref, s32[4,704,1]{2,1,0:T(8,128)} %broadcast_select_fusion.pos_ref, bf16[352,1400]{1,0:T(8,128)(2,1)} %collective-permute-done.13.refs_0_, ...), custom_call_target="tpu_custom_call", output_to_operand_aliasing={{}: (4, {})} | custom-call | flops 5519360000 | bytes 15769600 | tf_op jit(solution)/shard_map/pallas_call | solution.py:60
  140.2 14.6 %shard_map.67.acc_ref = f32[2000,1400]{1,0:T(8,128)} custom-call(s32[9]{0:T(128)} %dynamic-slice_bitcast_fusion.info_ref, bf16[352,1024]{1,0:T(8,128)(2,1)} %copy-done, bf16[352,1024]{1,0:T(8,128)(2,1)} %copy-done.5, bf16[352,1024]{1,0:T(8,128)(2,1)} %collective-permute-done.refs_2_, bf16[352,1024]{1,0:T(8,128)(2,1)} %collective-permute-done.10.refs_3_, ...), custom_call_target="tpu_custom_call" | custom-call | flops 6055526400 | bytes 21707776 | tf_op jit(solution)/shard_map/pallas_call | solution.py:208
  154.8 2.4 %collective-permute-start.15 = (bf16[352,1024]{1,0:T(8,128)(2,1)}, bf16[352,1024]{1,0:T(8,128)(2,1)S(1)}, u32[]{:S(2)}, u32[]{:S(2)}) collective-permute-start(bf16[352,1024]{1,0:T(8,128)(2,1)} %collective-permute-done.7.refs_2_), channel_id=1, source_target_pairs={{0,1},{1,0},{8,9},{9,8},{16,17},{17,16},{24,25},{25,24}} | collective-permute-start | bytes 2162696 | tf_op jit(solution)/shard_map/ppermute | solution.py:131
  158.0 15.1 %shard_map.68.refs_9_ = f32[2000,1400]{1,0:T(8,128)} custom-call(bf16[8,352,1024]{2,1,0:T(8,128)(2,1)} %bitcast.11, bf16[4,704,1400]{2,1,0:T(8,128)(2,1)} %shard_map.66.refs_12_.v_ref.refs_8_, f32[2000,1400]{1,0:T(8,128)} %residual_ref.1, f32[2000,1400]{1,0:T(8,128)} %shard_map.67.acc_ref), custom_call_target="tpu_custom_call", output_to_operand_aliasing={{}: (3, {})} | custom-call | flops 8074035200 | bytes 25120768 | tf_op jit(solution)/shard_map/pallas_call | solution.py:245
  174.8 9.9 %shard_map.69 = f32[2000,1400]{1,0:T(8,128)} custom-call(s32[9]{0:T(128)} %dynamic-slice_bitcast_fusion.info_ref, bf16[352,1024]{1,0:T(8,128)(2,1)} %copy-done.3, bf16[352,1024]{1,0:T(8,128)(2,1)} %copy-done.4, bf16[352,1024]{1,0:T(8,128)(2,1)} %collective-permute-done.7.refs_2_, bf16[352,1024]{1,0:T(8,128)(2,1)} %copy-done.6, ...), custom_call_target="tpu_custom_call", output_to_operand_aliasing={{}: (10, {})} | custom-call | flops 2018508800 | bytes 14881792 | tf_op jit(solution)/shard_map/pallas_call | solution.py:208
  (58 shorter events, 16.0 us)
Async XLA Ops:
  6.5 151.4 %all-gather.3.cloned.1.call-start = ((), (), s32[]{:S(2)}) async-start(), calls=%async_computation | async-start | bytes 6488064 | tf_op jit(solution)/shard_map/all_gather | solution.py:271
  8.9 50.1 %copy-start = (bf16[352,1024]{1,0:T(8,128)(2,1)}, bf16[352,1024]{1,0:T(8,128)(2,1)S(1)}, u32[]{:S(2)}) copy-start(bf16[352,1024]{1,0:T(8,128)(2,1)S(1)} %get-tuple-element.24.refs_0_) | copy-start | bytes 2162692
  9.0 31.3 %collective-permute-start.1 = (bf16[352,1024]{1,0:T(8,128)(2,1)S(1)}, bf16[352,1024]{1,0:T(8,128)(2,1)S(1)}, u32[]{:S(2)}, u32[]{:S(2)}) collective-permute-start(bf16[352,1024]{1,0:T(8,128)(2,1)S(1)} %get-tuple-element.24.refs_0_), channel_id=1, source_target_pairs={{0,2},{1,3},{2,4},{3,5},{4,6},{5,7},{8,10},{9,11},{10,12},{11,13},... | collective-permute-start | bytes 2162696 | tf_op jit(solution)/shard_map/ppermute | solution.py:121
  14.0 43.8 %collective-permute-start = (bf16[352,1024]{1,0:T(8,128)(2,1)S(1)}, bf16[352,1024]{1,0:T(8,128)(2,1)}, u32[]{:S(2)}, u32[]{:S(2)}) collective-permute-start(bf16[352,1024]{1,0:T(8,128)(2,1)S(1)} %get-tuple-element.24.refs_0_), channel_id=1, source_target_pairs={{2,0},{3,1},{4,2},{5,3},{6,4},{7,5},{10,8},{11,9},{12,10},{13,11},... | collective-permute-start | bytes 2162696 | tf_op jit(solution)/shard_map/ppermute | solution.py:121
  15.3 46.3 %collective-permute-start.5 = (bf16[700,1400]{1,0:T(8,128)(2,1)}, bf16[700,1400]{1,0:T(8,128)(2,1)}, u32[]{:S(2)}, u32[]{:S(2)}) collective-permute-start(bf16[700,1400]{1,0:T(8,128)(2,1)} %refs_0_.1), channel_id=1, source_target_pairs={{0,16},{8,24},{16,0},{24,8},{1,17},{9,25},{17,1},{25,9},{2,18},{10... | collective-permute-start | bytes 5880008 | tf_op jit(solution)/shard_map/ppermute | solution.py:80
  16.8 48.5 %collective-permute-start.4 = (bf16[700,1400]{1,0:T(8,128)(2,1)}, bf16[700,1400]{1,0:T(8,128)(2,1)}, u32[]{:S(2)}, u32[]{:S(2)}) collective-permute-start(bf16[700,1400]{1,0:T(8,128)(2,1)} %refs_0_.1), channel_id=1, source_target_pairs={{0,8},{8,0},{16,24},{24,16},{1,9},{9,1},{17,25},{25,17},{2,10},{10... | collective-permute-start | bytes 5880008 | tf_op jit(solution)/shard_map/ppermute | solution.py:80
  40.2 75.9 %copy-start.1 = (bf16[352,1024]{1,0:T(8,128)(2,1)}, bf16[352,1024]{1,0:T(8,128)(2,1)S(1)}, u32[]{:S(2)}) copy-start(bf16[352,1024]{1,0:T(8,128)(2,1)S(1)} %collective-permute-done.1.refs_4_.refs_8_) | copy-start | bytes 2162692
  57.8 37.4 %collective-permute-start.2 = (bf16[352,1024]{1,0:T(8,128)(2,1)}, bf16[352,1024]{1,0:T(8,128)(2,1)S(1)}, u32[]{:S(2)}, u32[]{:S(2)}) collective-permute-start(bf16[352,1024]{1,0:T(8,128)(2,1)} %collective-permute-done.refs_2_), channel_id=1, source_target_pairs={{2,0},{3,1},{4,2},{5,3},{10,8},{11,9},{12,10},{13,11},{18,16},{19,... | collective-permute-start | bytes 2162696 | tf_op jit(solution)/shard_map/ppermute | solution.py:121
  59.1 57.7 %collective-permute-start.9 = (bf16[352,1024]{1,0:T(8,128)(2,1)S(1)}, bf16[352,1024]{1,0:T(8,128)(2,1)S(1)}, u32[]{:S(2)}, u32[]{:S(2)}) collective-permute-start(bf16[352,1024]{1,0:T(8,128)(2,1)S(1)} %get-tuple-element.24.refs_0_), channel_id=1, source_target_pairs={{0,1},{1,0},{2,3},{3,2},{4,5},{5,4},{6,7},{7,6},{8,9},{9,8},{10,11... | collective-permute-start | bytes 2162696 | tf_op jit(solution)/shard_map/ppermute | solution.py:131
  59.2 60.4 %collective-permute-start.10 = (bf16[352,1024]{1,0:T(8,128)(2,1)}, bf16[352,1024]{1,0:T(8,128)(2,1)}, u32[]{:S(2)}, u32[]{:S(2)}) collective-permute-start(bf16[352,1024]{1,0:T(8,128)(2,1)} %collective-permute-done.refs_2_), channel_id=1, source_target_pairs={{0,1},{1,0},{2,3},{3,2},{4,5},{5,4},{8,9},{9,8},{10,11},{11,10},{1... | collective-permute-start | bytes 2162696 | tf_op jit(solution)/shard_map/ppermute | solution.py:131
  61.6 54.5 %collective-permute-start.3 = (bf16[352,1024]{1,0:T(8,128)(2,1)S(1)}, bf16[352,1024]{1,0:T(8,128)(2,1)}, u32[]{:S(2)}, u32[]{:S(2)}) collective-permute-start(bf16[352,1024]{1,0:T(8,128)(2,1)S(1)} %collective-permute-done.1.refs_4_.refs_8_), channel_id=1, source_target_pairs={{2,4},{3,5},{4,6},{5,7},{10,12},{11,13},{12,14},{13,15},{18,20},{1... | collective-permute-start | bytes 2162696 | tf_op jit(solution)/shard_map/ppermute | solution.py:121
  65.4 58.3 %collective-permute-start.13 = (bf16[352,1400]{1,0:T(8,128)(2,1)}, bf16[352,1400]{1,0:T(8,128)(2,1)}, u32[]{:S(2)}, u32[]{:S(2)}) collective-permute-start(bf16[352,1400]{1,0:T(8,128)(2,1)} %slice.35), channel_id=1, source_target_pairs={{0,8},{8,0},{16,24},{24,16},{1,9},{9,1},{17,25},{25,17},{2,10},{10... | collective-permute-start | bytes 2956808 | tf_op jit(solution)/shard_map/ppermute | solution.py:80
  95.2 27.1 %copy-start.3 = (bf16[352,1024]{1,0:T(8,128)(2,1)}, bf16[352,1024]{1,0:T(8,128)(2,1)S(1)}, u32[]{:S(2)}) copy-start(bf16[352,1024]{1,0:T(8,128)(2,1)S(1)} %collective-permute-done.2.refs_6_.refs_0_) | copy-start | bytes 2162692
  95.2 27.1 %collective-permute-start.14 = (bf16[348,1400]{1,0:T(8,128)(2,1)}, bf16[348,1400]{1,0:T(8,128)(2,1)}, u32[]{:S(2)}, u32[]{:S(2)}) collective-permute-start(bf16[348,1400]{1,0:T(8,128)(2,1)} %slice.36), channel_id=1, source_target_pairs={{0,16},{8,24},{16,0},{24,8},{1,17},{9,25},{17,1},{25,9},{2,18},{10... | collective-permute-start | bytes 2923208 | tf_op jit(solution)/shard_map/ppermute | solution.py:80
  116.1 23.0 %collective-permute-start.11 = (bf16[352,1024]{1,0:T(8,128)(2,1)S(1)}, bf16[352,1024]{1,0:T(8,128)(2,1)S(1)}, u32[]{:S(2)}, u32[]{:S(2)}) collective-permute-start(bf16[352,1024]{1,0:T(8,128)(2,1)S(1)} %collective-permute-done.1.refs_4_.refs_8_), channel_id=1, source_target_pairs={{2,3},{3,2},{4,5},{5,4},{6,7},{7,6},{10,11},{11,10},{12,13},{13,12... | collective-permute-start | bytes 2162696 | tf_op jit(solution)/shard_map/ppermute | solution.py:131
  116.8 0.9 copy-start.5
  117.7 21.4 %collective-permute-start.6 = (bf16[352,1024]{1,0:T(8,128)(2,1)S(1)}, bf16[352,1024]{1,0:T(8,128)(2,1)S(1)}, u32[]{:S(2)}, u32[]{:S(2)}) collective-permute-start(bf16[352,1024]{1,0:T(8,128)(2,1)S(1)} %collective-permute-done.2.refs_6_.refs_0_), channel_id=1, source_target_pairs={{0,1},{1,0},{2,3},{3,2},{8,9},{9,8},{10,11},{11,10},{16,17},{17,16... | collective-permute-start | bytes 2162696 | tf_op jit(solution)/shard_map/ppermute | solution.py:131
  119.6 19.5 %collective-permute-start.12 = (bf16[352,1024]{1,0:T(8,128)(2,1)}, bf16[352,1024]{1,0:T(8,128)(2,1)}, u32[]{:S(2)}, u32[]{:S(2)}) collective-permute-start(bf16[352,1024]{1,0:T(8,128)(2,1)} %collective-permute-done.3.refs_10_.refs_4_), channel_id=1, source_target_pairs={{4,5},{5,4},{6,7},{7,6},{12,13},{13,12},{14,15},{15,14},{20,21},{2... | collective-permute-start | bytes 2162696 | tf_op jit(solution)/shard_map/ppermute | solution.py:131
  122.3 32.4 %collective-permute-start.7 = (bf16[352,1024]{1,0:T(8,128)(2,1)S(1)}, bf16[352,1024]{1,0:T(8,128)(2,1)}, u32[]{:S(2)}, u32[]{:S(2)}) collective-permute-start(bf16[352,1024]{1,0:T(8,128)(2,1)S(1)} %collective-permute-done.2.refs_6_.refs_0_), channel_id=1, source_target_pairs={{2,0},{3,1},{10,8},{11,9},{18,16},{19,17},{26,24},{27,25}} | collective-permute-start | bytes 2162696 | tf_op jit(solution)/shard_map/ppermute | solution.py:121
  123.6 31.2 %collective-permute-start.8 = (bf16[352,1024]{1,0:T(8,128)(2,1)}, bf16[352,1024]{1,0:T(8,128)(2,1)}, u32[]{:S(2)}, u32[]{:S(2)}) collective-permute-start(bf16[352,1024]{1,0:T(8,128)(2,1)} %collective-permute-done.3.refs_10_.refs_4_), channel_id=1, source_target_pairs={{4,6},{5,7},{12,14},{13,15},{20,22},{21,23},{28,30},{29,31}} | collective-permute-start | bytes 2162696 | tf_op jit(solution)/shard_map/ppermute | solution.py:121
  139.1 0.9 copy-start.2
  139.1 1.1 copy-start.4
  154.8 18.3 %collective-permute-start.15 = (bf16[352,1024]{1,0:T(8,128)(2,1)}, bf16[352,1024]{1,0:T(8,128)(2,1)S(1)}, u32[]{:S(2)}, u32[]{:S(2)}) collective-permute-start(bf16[352,1024]{1,0:T(8,128)(2,1)} %collective-permute-done.7.refs_2_), channel_id=1, source_target_pairs={{0,1},{1,0},{8,9},{9,8},{16,17},{17,16},{24,25},{25,24}} | collective-permute-start | bytes 2162696 | tf_op jit(solution)/shard_map/ppermute | solution.py:131
  157.2 15.9 %collective-permute-start.16 = (bf16[352,1024]{1,0:T(8,128)(2,1)}, bf16[352,1024]{1,0:T(8,128)(2,1)S(1)}, u32[]{:S(2)}, u32[]{:S(2)}) collective-permute-start(bf16[352,1024]{1,0:T(8,128)(2,1)} %collective-permute-done.8.refs_6_), channel_id=1, source_target_pairs={{6,7},{7,6},{14,15},{15,14},{22,23},{23,22},{30,31},{31,30}} | collective-permute-start | bytes 2162696 | tf_op jit(solution)/shard_map/ppermute | solution.py:131
  (2 other events, 1.7 us)
Sparse Core Ops, SparseCore 0:
  9.1 84.1 all-gather.2

commit v4 on v3

--- a/solution.py
+++ b/solution.py
@@ -10,6 +10,8 @@
 
 C_SLAB = 2
 CORES = 2
+LANES = 128
+SUBLANES = 8
 TILE = 256
 VMEM_BYTES = 58 << 20
 WHOLE_TILES = 4
@@ -24,53 +26,93 @@
     pair_irrep = jnp.bitwise_xor(irrep_virtual[:C_SLAB][:, None], irrep_virtual[None, :]).reshape(-1)
     count = pair_irrep.shape[0]
     key = pair_irrep * count + jnp.arange(count, dtype=jnp.int32)
-    blocks = jnp.pad(
-        key.reshape(chips * CORES, depth), ((0, 0), (0, depth_padded - depth)), constant_values=-1
-    ).reshape(chips, CORES * depth_padded, 1)
-    rank = jnp.sum((key[None, None, :] < blocks).astype(jnp.int32), axis=2, keepdims=True)
-    return jnp.where(blocks < 0, -1, rank)
-
-
-def permute_kernel(count, has_previous, base_ref, pos_ref, *refs):
-    out_ref = refs[-1]
-    total = refs[count][0].astype(jnp.float32) if has_previous else None
-    pos = pos_ref[0]
-    for s in range(count):
-        rows = refs[s].shape[0]
-        picks = pos - base_ref[s] == lax.broadcasted_iota(jnp.int32, (pos.shape[0], rows), 1)
-        term = jnp.dot(picks.astype(jnp.bfloat16), refs[s][...], preferred_element_type=jnp.float32)
-        total = term if total is None else total + term
-    out_ref[0] = total.astype(out_ref.dtype)
-
-
-def add_permuted(pos, parts, bases, previous):
-    chips, rows, _ = pos.shape
-    columns = parts[0].shape[1]
-    block = pl.BlockSpec((1, rows, columns), lambda q, *_: (q, 0, 0))
-    in_specs = [pl.BlockSpec((1, rows, 1), lambda q, *_: (q, 0, 0))]
-    in_specs += [
-        pl.BlockSpec(part.shape, lambda q, *_: (0, 0), pipeline_mode=pl.Buffered(1)) for part in parts
-    ]
-    operands = [bases, pos, *parts]
-    aliases = {}
-    if previous is not None:
-        in_specs.append(block)
-        aliases = {len(operands): 0}
-        operands.append(previous)
-    return pl.pallas_call(
-        functools.partial(permute_kernel, len(parts), previous is not None),
+    rank = jnp.sum((key[:, None] < key[None, :]).astype(jnp.int32), axis=0)
+    return jnp.pad(rank.reshape(chips * CORES, depth), ((0, 0), (0, depth_padded - depth))).reshape(-1)
+
+
+def gather_kernel(firsts, depth_of, place_ref, *refs):
+    parts, (out_ref, rows_ref, taken_ref) = refs[: len(firsts)], refs[len(firsts) :]
+    total, columns = out_ref.shape
+    tiles = -(-columns // LANES)
+    per_eight = depth_of * SUBLANES
+    widths = [min(LANES, columns - t * LANES) for t in range(tiles)]
+    i = pl.program_id(0)
+
+    @pl.when(i == 0)
+    def _():
+        for part, first in zip(parts, firsts):
+            height = part.shape[0]
+
+            def spread_rows(values, at):
+                for top in range(0, values.shape[0], SUBLANES):
+                    eight = values[top : top + SUBLANES].astype(jnp.float32)
+                    for t, width in enumerate(widths):
+                        base = at + top // SUBLANES * per_eight + t * SUBLANES
+                        rows_ref[pl.ds(base, eight.shape[0]), 0:width] = eight[:, t * LANES : t * LANES + width]
+
+            def body(g, carry, part=part, first=first, spread_rows=spread_rows):
+                at = pl.multiple_of((first // SUBLANES + 2 * g) * per_eight, per_eight)
+                spread_rows(part[pl.ds(pl.multiple_of(g * 16, 16), 16), :], at)
+                return carry
+
+            whole = height // 16
+            lax.fori_loop(0, whole, body, 0)
+            if height > whole * 16:
+                spread_rows(part[whole * 16 : height, :], (first // SUBLANES + 2 * whole) * per_eight)
+
+    def take(g, carry):
+        for u in range(16):
+            place = place_ref[i * total + g * 16 + u]
+            target = g * 2 * per_eight + u // SUBLANES * per_eight + u % SUBLANES
+            taken_ref[pl.ds(target, depth_of, stride=SUBLANES), :] = rows_ref[
+                pl.ds(place, depth_of, stride=SUBLANES), :
+            ]
+        return carry
+
+    lax.fori_loop(0, total // 16, take, 0)
+
+    def put(g, carry):
+        for t, width in enumerate(widths):
+            pieces = [
+                taken_ref[pl.ds(pl.multiple_of((2 * g + e) * per_eight + t * SUBLANES, SUBLANES), SUBLANES), 0:width]
+                for e in range(2)
+            ]
+            out_ref[pl.ds(pl.multiple_of(g * 16, 16), 16), t * LANES : t * LANES + width] = jnp.concatenate(
+                pieces, axis=0
+            ).astype(out_ref.dtype)
+        return carry
+
+    lax.fori_loop(0, total // 16, put, 0)
+
+
+def natural_rows(rank, parts, row, stored_rows, chips):
+    columns = parts[0][0].shape[1]
+    block_rows = round_up(stored_rows, 16)
+    blocks = 1 + max(distance for _, distance, _ in parts)
+    depth_of = round_up(-(-columns // LANES), SUBLANES)
+    at = ((rank // stored_rows) ^ row) * block_rows + rank % stored_rows
+    place = at // SUBLANES * (depth_of * SUBLANES) + at % SUBLANES
+    step_rows = rank.shape[0] // chips
+    firsts = tuple(distance * block_rows + first for _, distance, first in parts)
+    natural = pl.pallas_call(
+        functools.partial(gather_kernel, firsts, depth_of),
         grid_spec=pltpu.PrefetchScalarGridSpec(
-            num_scalar_prefetch=1, grid=(chips,), in_specs=in_specs, out_specs=block
+            num_scalar_prefetch=1,
+            grid=(chips,),
+            in_specs=[
+                pl.BlockSpec(part.shape, lambda q, *_: (0, 0), pipeline_mode=pl.Buffered(1)) for part, _, _ in parts
+            ],
+            out_specs=pl.BlockSpec((step_rows, columns), lambda q, *_: (q, 0)),
+            scratch_shapes=[
+                pltpu.VMEM((blocks * block_rows * depth_of, LANES), jnp.float32),
+                pltpu.VMEM((step_rows * depth_of, LANES), jnp.float32),
+            ],
         ),
-        out_shape=jax.ShapeDtypeStruct((chips, rows, columns), parts[0].dtype),
-        input_output_aliases=aliases,
+        out_shape=jax.ShapeDtypeStruct((rank.shape[0], columns), parts[0][0].dtype),
         compiler_params=pltpu.CompilerParams(vmem_limit_bytes=VMEM_BYTES),
-        cost_estimate=pl.CostEstimate(
-            flops=2 * chips * rows * columns * sum(part.shape[0] for part in parts),
-            bytes_accessed=4 * chips * rows * columns,
-            transcendentals=0,
-        ),
-    )(*operands)
+        cost_estimate=pl.CostEstimate(flops=15 * 10**9, bytes_accessed=4 * rank.shape[0] * columns, transcendentals=0),
+    )(place, *[part for part, _, _ in parts])
+    return natural.reshape(chips, step_rows, columns)
 
 
 def gather_integrals(values, size):
@@ -136,10 +178,10 @@
     offsets = np.cumsum([0, *slots])
     n_arrays = int(offsets[-1]) * CORES
     arrays = refs[:n_arrays]
-    natural_ref, acc_ref = refs[n_arrays], refs[n_arrays + 1]
-    out_ref, buffer, integrals, sems, sem_integrals = refs[n_arrays + 2 :]
+    natural_ref, residual_ref, _ = refs[n_arrays : n_arrays + 3]
+    out_ref, buffer, integrals, sems, sem_integrals = refs[n_arrays + 3 :]
     core = info_ref[0]
-    tile = acc_ref.shape[0]
+    tile = residual_ref.shape[0]
     i = pl.program_id(0)
     steps = arrays[0].shape[1] // tile
 
@@ -183,7 +225,7 @@
 
     now = lax.rem(i, 2)
     pltpu.make_async_copy(buffer.at[now], buffer.at[now], sems.at[now]).wait()
-    out_ref[...] = acc_ref[...] + lax.dot_general(
+    out_ref[...] = residual_ref[...] + lax.dot_general(
         buffer[now], integrals[...], CONTRACT_FIRST, preferred_element_type=jnp.float32
     )
 
@@ -196,21 +238,21 @@
     )
 
 
-def add_line(info, first_slot, slots, natural, acc, first_tile, in_place):
+def add_line(info, first_slot, slots, natural, residual, acc, first_tile):
     tile = TILE
     depth, lanes = slots[0][0][0].shape
     columns = natural.shape[2]
     arrays = [a for slot in slots for pair in slot for a in pair]
     anywhere = pl.BlockSpec(memory_space=pl.ANY)
     block = pl.BlockSpec((tile, columns), lambda i, *_: (first_tile + i, 0))
-    operands = [info, *arrays, natural, acc]
+    operands = [info, *arrays, natural, residual, acc]
     rows = 2 * depth * len(slots)
     return pl.pallas_call(
         functools.partial(line_kernel, tuple(len(slot) for slot in slots), first_slot, depth),
         grid_spec=pltpu.PrefetchScalarGridSpec(
             num_scalar_prefetch=1,
             grid=(lanes // tile,),
-            in_specs=[anywhere] * (len(arrays) + 1) + [block],
+            in_specs=[anywhere] * (len(arrays) + 1) + [block, anywhere],
             out_specs=block,
             scratch_shapes=[
                 pltpu.VMEM((2, rows, tile), natural.dtype),
@@ -220,14 +262,13 @@
             ],
         ),
         out_shape=jax.ShapeDtypeStruct(acc.shape, acc.dtype),
-        input_output_aliases={len(operands) - 1: 0} if in_place else {},
+        input_output_aliases={len(operands) - 1: 0},
         compiler_params=pltpu.CompilerParams(vmem_limit_bytes=VMEM_BYTES),
         cost_estimate=product_cost(lanes, rows, columns),
     )(*operands)
 
 
-def whole_kernel(t_ref, v_ref, residual_ref, acc_ref, out_ref):
-    del acc_ref
+def whole_kernel(t_ref, v_ref, residual_ref, out_ref):
     blocks, depth, tile = t_ref.shape
     out_ref[...] = residual_ref[...] + lax.dot_general(
         t_ref[...].reshape(blocks * depth, tile),
@@ -237,7 +278,7 @@
     )
 
 
-def add_whole(gathered, natural, residual, acc):
+def add_whole(gathered, natural, residual):
     tile = TILE
     blocks, depth, lanes = gathered.shape
     columns = natural.shape[2]
@@ -249,14 +290,12 @@
             pl.BlockSpec((blocks, depth, tile), lambda i: (0, 0, i)),
             pl.BlockSpec(natural.shape, lambda i: (0, 0, 0), pipeline_mode=pl.Buffered(1)),
             block,
-            pl.BlockSpec(memory_space=pl.ANY),
         ],
         out_specs=block,
-        out_shape=jax.ShapeDtypeStruct(acc.shape, acc.dtype),
-        input_output_aliases={3: 0},
+        out_shape=jax.ShapeDtypeStruct(residual.shape, residual.dtype),
         compiler_params=pltpu.CompilerParams(vmem_limit_bytes=VMEM_BYTES),
         cost_estimate=product_cost(lanes, blocks * depth, columns),
-    )(gathered, natural, residual, acc)
+    )(gathered, natural, residual)
 
 
 def on_device(chips, row_size, amplitudes, values_stored, irrep_virtual, residual_in):
@@ -271,34 +310,18 @@
     gathered = lax.all_gather(whole, "col", axis=0)
     held = line_step({"L": chunk, "R": chunk}, 1, chips)
     got, order, half = gather_integrals(values_stored, row_size)
-    spread = {("own", 0): (chunk, swap_cores(chunk, "L", 0, chips))}
-
-    pos = stored_positions(irrep_virtual, chips, depth, depth_padded)
-    groups = [[(0, 0)], [(d, 0) for d in order if len(got[d]) == 1]]
-    groups += [[(d, 0), (d, 1)] for d in order if len(got[d]) == 2]
-    starts = [
-        [[(r ^ d) * stored_rows + which * half for d, which in group] for group in groups]
-        for r in range(row_size)
-    ]
-    width = max(len(group) for group in groups)
-    starts = np.array([[g + [0] * (width - len(g)) for g in of_row] for of_row in starts], np.int32)
-    bases = jnp.asarray(starts)[lax.axis_index("row")]
-    naturals = [None]
-    for g, group in enumerate(groups):
-        naturals.append(add_permuted(pos, [got[d][which] for d, which in group], bases[g], naturals[-1]))
-        s = g + 1
-        if s < chips - 1:
-            held["L"], held["R"], naturals[-1] = lax.optimization_barrier((held["L"], held["R"], naturals[-1]))
-            following = line_step(held, s + 1, chips)
-            for way in ("L", "R"):
-                spread[way, s] = (held[way], swap_cores(held[way], way, s, chips))
-            held = following
-    for s in range(len(groups) + 1, chips - 1):
-        following = line_step(held, s + 1, chips)
-        for way in ("L", "R"):
-            spread[way, s] = (held[way], swap_cores(held[way], way, s, chips))
-        held = following
-    natural = naturals[-1]
+    parts = [(piece, d, half * which) for d in got for which, piece in enumerate(got[d])]
+    rank = stored_positions(irrep_virtual, chips, depth, depth_padded)
+
+    travelled = [("own", 0, chunk)]
+    for s in range(1, chips - 1):
+        travelled += [(way, s, held[way]) for way in ("L", "R")]
+        held = line_step(held, s + 1, chips)
+    blocks = lax.optimization_barrier(tuple(block for _, _, block in travelled))
+    spread = {}
+    for (way, s, _), block in zip(travelled, blocks):
+        spread[way, s] = (block, swap_cores(block, "L" if way == "own" else way, s, chips))
+    natural = natural_rows(rank, parts, lax.axis_index("row"), stored_rows, chips)
 
     table = slot_table(chips)
     slots = [[("own", 0)]]
@@ -313,13 +336,11 @@
     info = jnp.asarray(np.array(rows_of_info, np.int32))[lax.axis_index("col")]
 
     last = chips - 1
-    early = [[spread[c] for c in slot] for slot in slots[:last]]
-    acc = add_line(info, 0, early, natural, residual_in, WHOLE_TILES, False)
-    held["L"], held["R"], acc = lax.optimization_barrier((held["L"], held["R"], acc))
+    held["L"], held["R"], natural = lax.optimization_barrier((held["L"], held["R"], natural))
     for way in ("L", "R"):
         spread[way, last] = (held[way], swap_cores(held[way], way, last, chips))
-    acc = add_whole(gathered, natural, residual_in, acc)
-    return add_line(info, last, [[spread[c] for c in slots[last]]], natural, acc, WHOLE_TILES, True)
+    acc = add_whole(gathered, natural, residual_in)
+    return add_line(info, 0, [[spread[c] for c in slot] for slot in slots], natural, residual_in, acc, WHOLE_TILES)
 
 
 def solution(mesh):

time: 192 us -> 171 us (0.89)
  Pallas kernels: 84.2 us -> 49.5 us
  waiting for transfers between devices: 43.8 us -> 65.7 us
  local copies, waits for them, and re-layouts: 16.7 us -> 10.9 us
  starting transfers between devices: 27.6 us -> 25.4 us
    pallas_call x3 -> x1, Pallas kernels: 44.6 us -> 17.5 us  [natural_rows(): pl.pallas_call(functools.partial(gather_kernel, firsts, depth_of), grid_s...]
    ppermute x6, waiting for transfers between devices: 43.8 us -> 65.6 us  [line_step(): arrived[way] = lax.ppermute(held[way], 'col', pairs)]
    pallas_call x2 -> x1, Pallas kernels: 24.5 us -> 16.9 us  [add_line(): pl.pallas_call(functools.partial(line_kernel, tuple((len(slot) for slot i...]
    ppermute x6, starting transfers between devices: 11.9 us -> 9.58 us  [line_step(): arrived[way] = lax.ppermute(held[way], 'col', pairs)]
    unnamed x16 -> x12, local copies, waits for them, and re-layouts: 3.67 us -> 1.7 us
  transfers between devices with their start and end apart: 18 -> 18, of which waited for: 2 -> 3; matrix products, arithmetic and copies ran while one was open for 8% -> 7% of each run, Pallas kernels for 39% -> 19%
where the time goes in v4:
time: 171 us; the launch traced here: 170 us
  waiting for transfers between devices  65.7 us (38%)
  Pallas kernels  49.5 us (29%)
  starting transfers between devices  25.4 us (15%)
  between operations  13.6 us (8%)
  local copies, waits for them, and re-layouts  10.9 us (6%)
  other arithmetic  4.94 us (3%)
    ppermute x6, waiting for transfers between devices, line_step(): arrived[way] = lax.ppermute(held[way], 'col', pairs)  65.6 us
    pallas_call x1, Pallas kernels, natural_rows(): pl.pallas_call(functools.partial(gather_kernel, firsts, depth_of), grid_s...  17.5 us
    pallas_call x1, Pallas kernels, add_line(): pl.pallas_call(functools.partial(line_kernel, tuple((len(slot) for slot i...  16.9 us
    pallas_call x1, Pallas kernels, add_whole(): pl.pallas_call(whole_kernel, grid=(lanes // tile,), in_specs=[pl.BlockSpe...  15.1 us
    ppermute x7, starting transfers between devices, swap_cores(): return lax.ppermute(block, 'col', pairs)  11.3 us
    ppermute x6, starting transfers between devices, line_step(): arrived[way] = lax.ppermute(held[way], 'col', pairs)  9.58 us
    ppermute x4, starting transfers between devices, send(): return lax.ppermute(array, 'row', [(i, i ^ bit) for i in range(size)])  4.53 us
    slice x2, local copies, waits for them, and re-layouts, gather_integrals(): piece = source[0][:half] if which == 0 else source[0][half:]  4.48 us
  transfers between devices with their start and end apart: 18, of which 3 were waited for; matrix products, arithmetic and copies ran while one was open for 7% of the time, Pallas kernels for 19%

profile of v4, /device:TPU:0, one launch (start us, length us, event | category | flops | bytes accessed | tf_op | source)
XLA Modules:
  0.0 170.0 jit_solution(648123211909564951)
XLA Ops:
  6.5 2.3 %pad_slice_fusion = (bf16[352,1024]{1,0:T(8,128)(2,1)}, bf16[352,1024]{1,0:T(8,128)(2,1)S(1)}) fusion(bf16[350,2000]{1,0:T(8,128)(2,1)} %bitcast.8), kind=kLoop, calls=%fused_computation.1 | loop fusion | bytes 2841792 | tf_op jit(solution)/shard_map/slice | solution.py:309
  8.9 3.0 %collective-permute-start.11 = (bf16[700,1400]{1,0:T(8,128)(2,1)}, bf16[700,1400]{1,0:T(8,128)(2,1)}, u32[]{:S(2)}, u32[]{:S(2)}) collective-permute-start(bf16[700,1400]{1,0:T(8,128)(2,1)} %refs_0_.1), channel_id=1, source_target_pairs={{0,8},{8,0},{16,24},{24,16},{1,9},{9,1},{17,25},{25,17},{2,10},{10... | collective-permute-start | bytes 5880008 | tf_op jit(solution)/shard_map/ppermute | solution.py:122
  11.9 1.5 collective-permute-start.12
  13.4 3.5 %collective-permute-start.1 = (bf16[352,1024]{1,0:T(8,128)(2,1)S(1)}, bf16[352,1024]{1,0:T(8,128)(2,1)S(1)}, u32[]{:S(2)}, u32[]{:S(2)}) collective-permute-start(bf16[352,1024]{1,0:T(8,128)(2,1)S(1)} %get-tuple-element.13.refs_0_), channel_id=1, source_target_pairs={{0,2},{1,3},{2,4},{3,5},{4,6},{5,7},{8,10},{9,11},{10,12},{11,13},... | collective-permute-start | bytes 2162696 | tf_op jit(solution)/shard_map/ppermute | solution.py:163
  16.9 1.3 collective-permute-start
  19.8 25.1 %collective-permute-done.1.refs_4_.refs_8_ = bf16[352,1024]{1,0:T(8,128)(2,1)S(1)} collective-permute-done((bf16[352,1024]{1,0:T(8,128)(2,1)S(1)}, bf16[352,1024]{1,0:T(8,128)(2,1)S(1)}, u32[]{:S(2)}, u32[]{:S(2)}) %collective-permute-start.1) | collective-permute-done | bytes 720928 | tf_op jit(solution)/shard_map/ppermute | solution.py:163
  45.6 21.1 %collective-permute-done.refs_2_ = bf16[352,1024]{1,0:T(8,128)(2,1)} collective-permute-done((bf16[352,1024]{1,0:T(8,128)(2,1)S(1)}, bf16[352,1024]{1,0:T(8,128)(2,1)}, u32[]{:S(2)}, u32[]{:S(2)}) %collective-permute-start) | collective-permute-done | bytes 720928 | tf_op jit(solution)/shard_map/ppermute | solution.py:163
  66.6 1.3 collective-permute-start.2
  67.9 2.2 %slice.21 = bf16[348,1400]{1,0:T(8,128)(2,1)} slice(bf16[700,1400]{1,0:T(8,128)(2,1)} %collective-permute-done.11.refs_1_), slice={[352:700], [0:1400]} | slice | bytes 1948800 | tf_op jit(solution)/shard_map/slice | solution.py:137
  70.2 2.2 %slice.20 = bf16[352,1400]{1,0:T(8,128)(2,1)} slice(bf16[700,1400]{1,0:T(8,128)(2,1)} %collective-permute-done.12.refs_2_), slice={[0:352], [0:1400]} | slice | bytes 1971200 | tf_op jit(solution)/shard_map/slice | solution.py:137
  72.4 3.5 %convert_reduce_fusion = s32[2800]{0:T(1024)S(1)} fusion(s32[2800]{0:T(1024)S(1)} %iota_add_fusion), kind=kLoop, calls=%fused_computation | loop fusion | flops 23517200 | bytes 22400 | tf_op jit(solution)/shard_map/reduce_sum | solution.py:29
  76.3 1.3 dynamic-slice_bitcast_fusion.info_ref
  78.2 19.5 %collective-permute-done.2.refs_6_.refs_12_ = bf16[352,1024]{1,0:T(8,128)(2,1)S(1)} collective-permute-done((bf16[352,1024]{1,0:T(8,128)(2,1)}, bf16[352,1024]{1,0:T(8,128)(2,1)S(1)}, u32[]{:S(2)}, u32[]{:S(2)}) %collective-permute-start.2) | collective-permute-done | bytes 720928 | tf_op jit(solution)/shard_map/ppermute | solution.py:163
  97.7 2.4 %collective-permute-start.5 = (bf16[352,1024]{1,0:T(8,128)(2,1)}, bf16[352,1024]{1,0:T(8,128)(2,1)}, u32[]{:S(2)}, u32[]{:S(2)}) collective-permute-start(bf16[352,1024]{1,0:T(8,128)(2,1)} %collective-permute-done.refs_2_), channel_id=1, source_target_pairs={{0,1},{1,0},{2,3},{3,2},{4,5},{5,4},{8,9},{9,8},{10,11},{11,10},{1... | collective-permute-start | bytes 2162696 | tf_op jit(solution)/shard_map/ppermute | solution.py:173
  100.1 1.5 collective-permute-start.6
  101.6 1.5 collective-permute-start.10
  103.1 1.3 collective-permute-start.9
  104.4 17.5 %shard_map.55 = bf16[2816,1400]{1,0:T(8,128)(2,1)} custom-call(s32[2816]{0:T(1024)} %fusion.4.place_ref, bf16[700,1400]{1,0:T(8,128)(2,1)} %refs_0_.1, bf16[700,1400]{1,0:T(8,128)(2,1)} %collective-permute-done.11.refs_1_, bf16[700,1400]{1,0:T(8,128)(2,1)} %collective-permute-done.12.refs_2_, bf16[352,1400]{1,0:T(8,128)(2,1)} %collective-permute-done.13.refs_3_, ...), custom_call_target="tpu_custom_call" | custom-call | flops 15000000512 | bytes 15769600 | tf_op jit(solution)/shard_map/pallas_call | solution.py:97
  122.0 1.9 %collective-permute-start.7 = (bf16[352,1024]{1,0:T(8,128)(2,1)S(1)}, bf16[352,1024]{1,0:T(8,128)(2,1)}, u32[]{:S(2)}, u32[]{:S(2)}) collective-permute-start(bf16[352,1024]{1,0:T(8,128)(2,1)S(1)} %collective-permute-done.2.refs_6_.refs_12_), channel_id=1, source_target_pairs={{0,1},{1,0},{2,3},{3,2},{8,9},{9,8},{10,11},{11,10},{16,17},{17,16... | collective-permute-start | bytes 2162696 | tf_op jit(solution)/shard_map/ppermute | solution.py:173
  123.9 1.5 collective-permute-start.8
  126.3 2.4 %collective-permute-start.15 = (bf16[352,1024]{1,0:T(8,128)(2,1)}, bf16[352,1024]{1,0:T(8,128)(2,1)S(1)}, u32[]{:S(2)}, u32[]{:S(2)}) collective-permute-start(bf16[352,1024]{1,0:T(8,128)(2,1)} %collective-permute-done.9.refs_14_), channel_id=1, source_target_pairs={{0,1},{1,0},{8,9},{9,8},{16,17},{17,16},{24,25},{25,24}} | collective-permute-start | bytes 2162696 | tf_op jit(solution)/shard_map/ppermute | solution.py:173
  128.7 1.5 collective-permute-start.16
  130.3 15.1 %shard_map.56.refs_22_ = f32[2000,1400]{1,0:T(8,128)} custom-call(bf16[8,352,1024]{2,1,0:T(8,128)(2,1)} %bitcast.7, bf16[4,704,1400]{2,1,0:T(8,128)(2,1)} %bitcast.5, f32[2000,1400]{1,0:T(8,128)} %refs_21_.1), custom_call_target="tpu_custom_call" | custom-call | flops 8074035200 | bytes 25120768 | tf_op jit(solution)/shard_map/pallas_call | solution.py:286
  146.2 16.9 %shard_map.57 = f32[2000,1400]{1,0:T(8,128)} custom-call(s32[9]{0:T(128)} %dynamic-slice_bitcast_fusion.info_ref, bf16[352,1024]{1,0:T(8,128)(2,1)} %copy-done, bf16[352,1024]{1,0:T(8,128)(2,1)} %copy-done.4, bf16[352,1024]{1,0:T(8,128)(2,1)} %collective-permute-done.refs_2_, ...), custom_call_target="tpu_custom_call", output_to_operand_aliasing={{}: (23, {})} | custom-call | flops 8074035200 | bytes 25120768 | tf_op jit(solution)/shard_map/pallas_call | solution.py:250
  (44 shorter events, 5.0 us)
Async XLA Ops:
  6.5 123.7 %all-gather.3.cloned.1.call-start = ((), (), s32[]{:S(2)}) async-start(), calls=%async_computation | async-start | bytes 6488064 | tf_op jit(solution)/shard_map/all_gather | solution.py:310
  8.9 113.1 %copy-start = (bf16[352,1024]{1,0:T(8,128)(2,1)}, bf16[352,1024]{1,0:T(8,128)(2,1)S(1)}, u32[]{:S(2)}) copy-start(bf16[352,1024]{1,0:T(8,128)(2,1)S(1)} %get-tuple-element.13.refs_0_) | copy-start | bytes 2162692
  8.9 59.0 %collective-permute-start.11 = (bf16[700,1400]{1,0:T(8,128)(2,1)}, bf16[700,1400]{1,0:T(8,128)(2,1)}, u32[]{:S(2)}, u32[]{:S(2)}) collective-permute-start(bf16[700,1400]{1,0:T(8,128)(2,1)} %refs_0_.1), channel_id=1, source_target_pairs={{0,8},{8,0},{16,24},{24,16},{1,9},{9,1},{17,25},{25,17},{2,10},{10... | collective-permute-start | bytes 5880008 | tf_op jit(solution)/shard_map/ppermute | solution.py:122
  11.9 58.3 %collective-permute-start.12 = (bf16[700,1400]{1,0:T(8,128)(2,1)}, bf16[700,1400]{1,0:T(8,128)(2,1)}, u32[]{:S(2)}, u32[]{:S(2)}) collective-permute-start(bf16[700,1400]{1,0:T(8,128)(2,1)} %refs_0_.1), channel_id=1, source_target_pairs={{0,16},{8,24},{16,0},{24,8},{1,17},{9,25},{17,1},{25,9},{2,18},{10... | collective-permute-start | bytes 5880008 | tf_op jit(solution)/shard_map/ppermute | solution.py:122
  13.4 31.4 %collective-permute-start.1 = (bf16[352,1024]{1,0:T(8,128)(2,1)S(1)}, bf16[352,1024]{1,0:T(8,128)(2,1)S(1)}, u32[]{:S(2)}, u32[]{:S(2)}) collective-permute-start(bf16[352,1024]{1,0:T(8,128)(2,1)S(1)} %get-tuple-element.13.refs_0_), channel_id=1, source_target_pairs={{0,2},{1,3},{2,4},{3,5},{4,6},{5,7},{8,10},{9,11},{10,12},{11,13},... | collective-permute-start | bytes 2162696 | tf_op jit(solution)/shard_map/ppermute | solution.py:163
  16.9 49.7 %collective-permute-start = (bf16[352,1024]{1,0:T(8,128)(2,1)S(1)}, bf16[352,1024]{1,0:T(8,128)(2,1)}, u32[]{:S(2)}, u32[]{:S(2)}) collective-permute-start(bf16[352,1024]{1,0:T(8,128)(2,1)S(1)} %get-tuple-element.13.refs_0_), channel_id=1, source_target_pairs={{2,0},{3,1},{4,2},{5,3},{6,4},{7,5},{10,8},{11,9},{12,10},{13,11},... | collective-permute-start | bytes 2162696 | tf_op jit(solution)/shard_map/ppermute | solution.py:163
  44.9 77.1 %copy-start.1 = (bf16[352,1024]{1,0:T(8,128)(2,1)}, bf16[352,1024]{1,0:T(8,128)(2,1)S(1)}, u32[]{:S(2)}) copy-start(bf16[352,1024]{1,0:T(8,128)(2,1)S(1)} %collective-permute-done.1.refs_4_.refs_8_) | copy-start | bytes 2162692
  44.9 33.3 %collective-permute-start.3 = (bf16[352,1024]{1,0:T(8,128)(2,1)S(1)}, bf16[352,1024]{1,0:T(8,128)(2,1)S(1)}, u32[]{:S(2)}, u32[]{:S(2)}) collective-permute-start(bf16[352,1024]{1,0:T(8,128)(2,1)S(1)} %collective-permute-done.1.refs_4_.refs_8_), channel_id=1, source_target_pairs={{2,4},{3,5},{4,6},{5,7},{10,12},{11,13},{12,14},{13,15},{18,20},{1... | collective-permute-start | bytes 2162696 | tf_op jit(solution)/shard_map/ppermute | solution.py:163
  66.6 31.0 %collective-permute-start.2 = (bf16[352,1024]{1,0:T(8,128)(2,1)}, bf16[352,1024]{1,0:T(8,128)(2,1)S(1)}, u32[]{:S(2)}, u32[]{:S(2)}) collective-permute-start(bf16[352,1024]{1,0:T(8,128)(2,1)} %collective-permute-done.refs_2_), channel_id=1, source_target_pairs={{2,0},{3,1},{4,2},{5,3},{10,8},{11,9},{12,10},{13,11},{18,16},{19,... | collective-permute-start | bytes 2162696 | tf_op jit(solution)/shard_map/ppermute | solution.py:163
  70.2 31.4 %collective-permute-start.14 = (bf16[348,1400]{1,0:T(8,128)(2,1)}, bf16[348,1400]{1,0:T(8,128)(2,1)}, u32[]{:S(2)}, u32[]{:S(2)}) collective-permute-start(bf16[348,1400]{1,0:T(8,128)(2,1)} %slice.21), channel_id=1, source_target_pairs={{0,16},{8,24},{16,0},{24,8},{1,17},{9,25},{17,1},{25,9},{2,18},{10... | collective-permute-start | bytes 2923208 | tf_op jit(solution)/shard_map/ppermute | solution.py:122
  72.4 30.7 %collective-permute-start.13 = (bf16[352,1400]{1,0:T(8,128)(2,1)}, bf16[352,1400]{1,0:T(8,128)(2,1)}, u32[]{:S(2)}, u32[]{:S(2)}) collective-permute-start(bf16[352,1400]{1,0:T(8,128)(2,1)} %slice.20), channel_id=1, source_target_pairs={{0,8},{8,0},{16,24},{24,16},{1,9},{9,1},{17,25},{25,17},{2,10},{10... | collective-permute-start | bytes 2956808 | tf_op jit(solution)/shard_map/ppermute | solution.py:122
  78.2 45.7 %copy-start.2 = (bf16[352,1024]{1,0:T(8,128)(2,1)}, bf16[352,1024]{1,0:T(8,128)(2,1)S(1)}, u32[]{:S(2)}) copy-start(bf16[352,1024]{1,0:T(8,128)(2,1)S(1)} %collective-permute-done.3.refs_10_.refs_16_) | copy-start | bytes 2162692
  97.7 24.3 %copy-start.3 = (bf16[352,1024]{1,0:T(8,128)(2,1)}, bf16[352,1024]{1,0:T(8,128)(2,1)S(1)}, u32[]{:S(2)}) copy-start(bf16[352,1024]{1,0:T(8,128)(2,1)S(1)} %collective-permute-done.2.refs_6_.refs_12_) | copy-start | bytes 2162692
  97.7 27.8 %collective-permute-start.4 = (bf16[352,1024]{1,0:T(8,128)(2,1)S(1)}, bf16[352,1024]{1,0:T(8,128)(2,1)S(1)}, u32[]{:S(2)}, u32[]{:S(2)}) collective-permute-start(bf16[352,1024]{1,0:T(8,128)(2,1)S(1)} %get-tuple-element.13.refs_0_), channel_id=1, source_target_pairs={{0,1},{1,0},{2,3},{3,2},{4,5},{5,4},{6,7},{7,6},{8,9},{9,8},{10,11... | collective-permute-start | bytes 2162696 | tf_op jit(solution)/shard_map/ppermute | solution.py:173
  97.7 31.0 %collective-permute-start.5 = (bf16[352,1024]{1,0:T(8,128)(2,1)}, bf16[352,1024]{1,0:T(8,128)(2,1)}, u32[]{:S(2)}, u32[]{:S(2)}) collective-permute-start(bf16[352,1024]{1,0:T(8,128)(2,1)} %collective-permute-done.refs_2_), channel_id=1, source_target_pairs={{0,1},{1,0},{2,3},{3,2},{4,5},{5,4},{8,9},{9,8},{10,11},{11,10},{1... | collective-permute-start | bytes 2162696 | tf_op jit(solution)/shard_map/ppermute | solution.py:173
  100.1 45.2 %collective-permute-start.6 = (bf16[352,1024]{1,0:T(8,128)(2,1)S(1)}, bf16[352,1024]{1,0:T(8,128)(2,1)}, u32[]{:S(2)}, u32[]{:S(2)}) collective-permute-start(bf16[352,1024]{1,0:T(8,128)(2,1)S(1)} %collective-permute-done.1.refs_4_.refs_8_), channel_id=1, source_target_pairs={{2,3},{3,2},{4,5},{5,4},{6,7},{7,6},{10,11},{11,10},{12,13},{13,12... | collective-permute-start | bytes 2162696 | tf_op jit(solution)/shard_map/ppermute | solution.py:173
  101.6 20.3 %collective-permute-start.10 = (bf16[352,1024]{1,0:T(8,128)(2,1)S(1)}, bf16[352,1024]{1,0:T(8,128)(2,1)}, u32[]{:S(2)}, u32[]{:S(2)}) collective-permute-start(bf16[352,1024]{1,0:T(8,128)(2,1)S(1)} %collective-permute-done.3.refs_10_.refs_16_), channel_id=1, source_target_pairs={{4,6},{5,7},{12,14},{13,15},{20,22},{21,23},{28,30},{29,31}} | collective-permute-start | bytes 2162696 | tf_op jit(solution)/shard_map/ppermute | solution.py:163
  103.1 20.8 %collective-permute-start.9 = (bf16[352,1024]{1,0:T(8,128)(2,1)S(1)}, bf16[352,1024]{1,0:T(8,128)(2,1)}, u32[]{:S(2)}, u32[]{:S(2)}) collective-permute-start(bf16[352,1024]{1,0:T(8,128)(2,1)S(1)} %collective-permute-done.2.refs_6_.refs_12_), channel_id=1, source_target_pairs={{2,0},{3,1},{10,8},{11,9},{18,16},{19,17},{26,24},{27,25}} | collective-permute-start | bytes 2162696 | tf_op jit(solution)/shard_map/ppermute | solution.py:163
  122.0 23.4 %collective-permute-start.7 = (bf16[352,1024]{1,0:T(8,128)(2,1)S(1)}, bf16[352,1024]{1,0:T(8,128)(2,1)}, u32[]{:S(2)}, u32[]{:S(2)}) collective-permute-start(bf16[352,1024]{1,0:T(8,128)(2,1)S(1)} %collective-permute-done.2.refs_6_.refs_12_), channel_id=1, source_target_pairs={{0,1},{1,0},{2,3},{3,2},{8,9},{9,8},{10,11},{11,10},{16,17},{17,16... | collective-permute-start | bytes 2162696 | tf_op jit(solution)/shard_map/ppermute | solution.py:173
  123.9 21.4 %collective-permute-start.8 = (bf16[352,1024]{1,0:T(8,128)(2,1)S(1)}, bf16[352,1024]{1,0:T(8,128)(2,1)}, u32[]{:S(2)}, u32[]{:S(2)}) collective-permute-start(bf16[352,1024]{1,0:T(8,128)(2,1)S(1)} %collective-permute-done.3.refs_10_.refs_16_), channel_id=1, source_target_pairs={{4,5},{5,4},{6,7},{7,6},{12,13},{13,12},{14,15},{15,14},{20,21},{2... | collective-permute-start | bytes 2162696 | tf_op jit(solution)/shard_map/ppermute | solution.py:173
  125.5 0.9 copy-start.4
  126.3 19.0 %collective-permute-start.15 = (bf16[352,1024]{1,0:T(8,128)(2,1)}, bf16[352,1024]{1,0:T(8,128)(2,1)S(1)}, u32[]{:S(2)}, u32[]{:S(2)}) collective-permute-start(bf16[352,1024]{1,0:T(8,128)(2,1)} %collective-permute-done.9.refs_14_), channel_id=1, source_target_pairs={{0,1},{1,0},{8,9},{9,8},{16,17},{17,16},{24,25},{25,24}} | collective-permute-start | bytes 2162696 | tf_op jit(solution)/shard_map/ppermute | solution.py:173
  128.7 16.7 %collective-permute-start.16 = (bf16[352,1024]{1,0:T(8,128)(2,1)}, bf16[352,1024]{1,0:T(8,128)(2,1)}, u32[]{:S(2)}, u32[]{:S(2)}) collective-permute-start(bf16[352,1024]{1,0:T(8,128)(2,1)} %collective-permute-done.10.refs_18_), channel_id=1, source_target_pairs={{6,7},{7,6},{14,15},{15,14},{22,23},{23,22},{30,31},{31,30}} | collective-permute-start | bytes 2162696 | tf_op jit(solution)/shard_map/ppermute | solution.py:173
  145.4 0.9 copy-start.5
Sparse Core Ops, SparseCore 0:
  9.0 83.9 all-gather.2

commit v5 on v2

v5 whole, which is shorter than its diff:
```python
import functools

import jax
import jax.numpy as jnp
import numpy as np
from jax import lax
from jax.experimental import pallas as pl
from jax.experimental.pallas import tpu as pltpu
from jax.sharding import PartitionSpec as P

C_SLAB = 2
CORES = 2
TILE = 256
VMEM_BYTES = 58 << 20
WHOLE_TILES = (4, 2)
CONTRACT_FIRST = (((0,), (0,)), ((), ()))


def round_up(value, step):
    return -(-value // step) * step


def stored_positions(irrep_virtual, chips, depth, depth_padded):
    pair_irrep = jnp.bitwise_xor(irrep_virtual[:C_SLAB][:, None], irrep_virtual[None, :]).reshape(-1)
    count = pair_irrep.shape[0]
    key = pair_irrep * count + jnp.arange(count, dtype=jnp.int32)
    blocks = jnp.pad(
        key.reshape(chips * CORES, depth), ((0, 0), (0, depth_padded - depth)), constant_values=-1
    ).reshape(chips, CORES * depth_padded, 1)
    rank = jnp.sum((key[None, None, :] < blocks).astype(jnp.int32), axis=2, keepdims=True)
    return jnp.where(blocks < 0, -1, rank)


def permute_kernel(groups, has_previous, base_ref, pos_ref, *refs):
    count = sum(len(group) for group in groups)
    out_ref = refs[count + has_previous]
    joined = list(refs[count + has_previous + 1 :])
    total = refs[count][0].astype(jnp.float32) if has_previous else None
    pos = pos_ref[0]
    for group in groups:
        if len(group) == 1:
            rows_ref = refs[group[0]]
        else:
            rows_ref = joined.pop(0)

            @pl.when(pl.program_id(0) == 0)
            def _(group=group, rows_ref=rows_ref):
                at = 0
                for p in group:
                    rows_ref[at : at + refs[p].shape[0], :] = refs[p][...]
                    at += refs[p].shape[0]

        rows = rows_ref.shape[0]
        picks = pos - base_ref[group[0]] == lax.broadcasted_iota(jnp.int32, (pos.shape[0], rows), 1)
        term = jnp.dot(picks.astype(jnp.bfloat16), rows_ref[...], preferred_element_type=jnp.float32)
        total = term if total is None else total + term
    out_ref[0] = total.astype(out_ref.dtype)


def add_permuted(pos, blocks, bases, previous):
    chips, rows, _ = pos.shape
    parts = [part for block in blocks for part in block]
    columns = parts[0].shape[1]
    numbers = iter(range(len(parts)))
    groups = tuple(tuple(next(numbers) for _ in block) for block in blocks)
    joined = [
        pltpu.VMEM((sum(part.shape[0] for part in block), columns), parts[0].dtype) for block in blocks if len(block) > 1
    ]
    block_spec = pl.BlockSpec((1, rows, columns), lambda q, *_: (q, 0, 0))
    in_specs = [pl.BlockSpec((1, rows, 1), lambda q, *_: (q, 0, 0))]
    in_specs += [pl.BlockSpec(part.shape, lambda q, *_: (0, 0), pipeline_mode=pl.Buffered(1)) for part in parts]
    operands = [bases, pos, *parts]
    aliases = {}
    if previous is not None:
        in_specs.append(block_spec)
        aliases = {len(operands): 0}
        operands.append(previous)
    return pl.pallas_call(
        functools.partial(permute_kernel, groups, previous is not None),
        grid_spec=pltpu.PrefetchScalarGridSpec(
            num_scalar_prefetch=1, grid=(chips,), in_specs=in_specs, out_specs=block_spec, scratch_shapes=joined
        ),
        out_shape=jax.ShapeDtypeStruct((chips, rows, columns), parts[0].dtype),
        input_output_aliases=aliases,
        compiler_params=pltpu.CompilerParams(vmem_limit_bytes=VMEM_BYTES),
        cost_estimate=pl.CostEstimate(
            flops=2 * chips * rows * columns * sum(part.shape[0] for part in parts),
            bytes_accessed=4 * chips * rows * columns,
            transcendentals=0,
        ),
    )(*operands)


def gather_integrals(values, size):
    half = round_up(values.shape[0] // 2, 16)

    def send(array, bit):
        return lax.ppermute(array, "row", [(i, i ^ bit) for i in range(size)])

    got = {0: [values]}
    order = sorted(range(1, size), key=lambda d: (bin(d).count("1"), d))
    for d in order:
        low, high = d & -d, 1 << (d.bit_length() - 1)
        if low == high:
            got[d] = [send(values, d)]
            continue
        parts = []
        for which, bit in ((0, low), (1, high)):
            source = got[d ^ bit]
            if len(source) == 2:
                piece = source[which]
            else:
                piece = source[0][:half] if which == 0 else source[0][half:]
            parts.append(send(piece, bit))
        got[d] = parts
    return got, order, half


def send_chips(block, distance, chips):
    pairs = [(z * CORES + core, (z ^ distance) * CORES + core) for z in range(chips) for core in range(CORES)]
    return lax.ppermute(block, "col", pairs)


def swap_cores(block, chips):
    return lax.ppermute(block, "col", [(i, i ^ 1) for i in range(chips * CORES)])


def direct_kernel(depth, info_ref, *refs):
    natural_ref, residual_ref, out_ref, buffer, integrals, sems, sem_integrals = refs[-7:]
    arrays = refs[:-7]
    count = len(arrays) // CORES
    core = info_ref[0]
    tile = residual_ref.shape[0]
    i = pl.program_id(0)
    steps = arrays[0].shape[1] // tile

    def fetch(step, half):
        lanes = pl.ds(pl.multiple_of(step * tile, tile), tile)
        for s in range(count):
            for other in range(CORES):
                place = jnp.where(core == other, 0, depth) + CORES * depth * s
                pltpu.make_async_copy(
                    arrays[CORES * s + other].at[:, lanes],
                    buffer.at[half, pl.ds(pl.multiple_of(place, 16), depth), :],
                    sems.at[half],
                ).start()

    @pl.when(i == 0)
    def _():
        for s in range(count):
            pltpu.make_async_copy(
                natural_ref.at[info_ref[1 + s]],
                integrals.at[pl.ds(CORES * depth * s, CORES * depth), :],
                sem_integrals,
            ).start()
        fetch(0, 0)

    @pl.when(i + 1 < steps)
    def _():
        fetch(i + 1, lax.rem(i + 1, 2))

    @pl.when(i == 0)
    def _():
        pltpu.make_async_copy(integrals, integrals, sem_integrals).wait()

    now = lax.rem(i, 2)
    pltpu.make_async_copy(buffer.at[now], buffer.at[now], sems.at[now]).wait()
    out_ref[...] = residual_ref[...] + lax.dot_general(
        buffer[now], integrals[...], CONTRACT_FIRST, preferred_element_type=jnp.float32
    )


def product_cost(lanes, rows, columns):
    return pl.CostEstimate(
        flops=2 * lanes * rows * columns,
        bytes_accessed=8 * lanes * columns + 2 * rows * (lanes + columns),
        transcendentals=0,
    )


def add_direct(info, slots, natural, residual, first_tile):
    tile = TILE
    depth, lanes = slots[0][0].shape
    columns = natural.shape[2]
    arrays = [a for pair in slots for a in pair]
    anywhere = pl.BlockSpec(memory_space=pl.ANY)
    block = pl.BlockSpec((tile, columns), lambda i, *_: (first_tile + i, 0))
    operands = [info, *arrays, natural, residual]
    rows = CORES * depth * len(slots)
    return pl.pallas_call(
        functools.partial(direct_kernel, depth),
        grid_spec=pltpu.PrefetchScalarGridSpec(
            num_scalar_prefetch=1,
            grid=(lanes // tile,),
            in_specs=[anywhere] * (len(arrays) + 1) + [block],
            out_specs=block,
            scratch_shapes=[
                pltpu.VMEM((2, rows, tile), natural.dtype),
                pltpu.VMEM((rows, columns), natural.dtype),
                pltpu.SemaphoreType.DMA((2,)),
                pltpu.SemaphoreType.DMA,
            ],
        ),
        out_shape=jax.ShapeDtypeStruct(residual.shape, residual.dtype),
        compiler_params=pltpu.CompilerParams(vmem_limit_bytes=VMEM_BYTES),
        cost_estimate=product_cost(lanes, rows, columns),
    )(*operands)


def whole_kernel(t_ref, v_ref, residual_ref, _, out_ref):
    blocks, depth, tile = t_ref.shape
    out_ref[...] = residual_ref[...] + lax.dot_general(
        t_ref[...].reshape(blocks * depth, tile),
        v_ref[...].reshape(blocks * depth, -1),
        CONTRACT_FIRST,
        preferred_element_type=jnp.float32,
    )


def add_whole(gathered, natural, residual, acc, first_tile):
    tile = TILE
    blocks, depth, lanes = gathered.shape
    columns = natural.shape[2]
    block = pl.BlockSpec((tile, columns), lambda i: (first_tile + i, 0))
    return pl.pallas_call(
        whole_kernel,
        grid=(lanes // tile,),
        in_specs=[
            pl.BlockSpec((blocks, depth, tile), lambda i: (0, 0, i)),
            pl.BlockSpec(natural.shape, lambda i: (0, 0, 0), pipeline_mode=pl.Buffered(1)),
            block,
            pl.BlockSpec(memory_space=pl.ANY),
        ],
        out_specs=block,
        out_shape=jax.ShapeDtypeStruct(residual.shape, residual.dtype),
        input_output_aliases={3: 0},
        compiler_params=pltpu.CompilerParams(vmem_limit_bytes=VMEM_BYTES),
        cost_estimate=product_cost(lanes, blocks * depth, columns),
    )(gathered, natural, residual, acc)


def on_device(chips, row_size, amplitudes, values_stored, irrep_virtual, residual_in):
    occ, depth = amplitudes.shape
    depth_padded = round_up(depth, 16)
    stored_rows = values_stored.shape[0]
    lanes = round_up(occ, TILE)
    edges = [int(edge) for edge in np.cumsum([0, *WHOLE_TILES]) * TILE]

    columns_first = jnp.pad(amplitudes.T, ((0, depth_padded - depth), (0, lanes - occ)))
    chunk = columns_first[:, edges[-1] :]
    got, order, half = gather_integrals(values_stored, row_size)
    blocks = [chunk] + [send_chips(chunk, d, chips) for d in range(1, chips)]
    gathered = [
        lax.all_gather(columns_first[:, left:right], "col", axis=0) for left, right in zip(edges[:-1], edges[1:])
    ]

    pos = stored_positions(irrep_virtual, chips, depth, depth_padded)
    natural = None
    for hops in range(row_size.bit_length()):
        distances = [d for d in got if bin(d).count("1") == hops]
        if not distances:
            continue
        bases = jnp.stack(
            [(lax.axis_index("row") ^ d) * stored_rows for d in distances for _ in got[d]]
        ).astype(jnp.int32)
        natural = add_permuted(pos, [got[d] for d in distances], bases, natural)
        if hops == 1:
            *blocks, natural = lax.optimization_barrier((*blocks, natural))
    slots = [(block, swap_cores(block, chips)) for block in blocks]

    core, chip = lax.axis_index("col") % CORES, lax.axis_index("col") // CORES
    info = jnp.stack([core] + [chip ^ d for d in range(chips)]).astype(jnp.int32)
    acc = add_direct(info, slots, natural, residual_in, edges[-1] // TILE)
    for part, left in zip(gathered, edges):
        acc = add_whole(part, natural, residual_in, acc, left // TILE)
    return acc


def solution(mesh):
    in_specs = (P("row", "col"), P("row", "col"), P(), P("row", "col"))
    out_specs = P("row", "col")
    body = functools.partial(on_device, mesh.shape["col"] // CORES, mesh.shape["row"])
    return jax.shard_map(body, mesh=mesh, in_specs=in_specs, out_specs=out_specs, check_vma=False)
```

time: 189 us -> 151 us (0.80)
  waiting for transfers between devices: 43.9 us -> 25.5 us
  starting transfers between devices: 27.8 us -> 13 us
  local copies, waits for them, and re-layouts: 22.8 us -> 11.1 us
  Pallas kernels: 72.5 us -> 81 us
    ppermute x13 -> x7, waiting for transfers between devices: 18.4 us -> 0.02 us  [the longest x4 0.01 us: swap_cores(): lax.ppermute(block, 'col', [(i, i ^ 1) for i in range(chips * CORES)])]
    ppermute x13 -> x7, starting transfers between devices: 20 us -> 5.04 us  [the longest x3 4.39 us: send_chips(): return lax.ppermute(block, 'col', pairs)]
    pallas_call x1 -> x2, Pallas kernels: 13.1 us -> 25.4 us  [add_whole(): pl.pallas_call(whole_kernel, grid=(lanes // tile,), in_specs=[pl.BlockSpe...]
    unnamed x20 -> x22, local copies, waits for them, and re-layouts: 11.6 us -> 2.64 us
    all_gather x1 -> x2, waiting for transfers between devices: 0.01 us -> 7.38 us  [on_device(): lax.all_gather(columns_first[:, left:right], 'col', axis=0)]
    ppermute x4, waiting for transfers between devices: 25.4 us -> 18.1 us  [send(): return lax.ppermute(array, 'row', [(i, i ^ bit) for i in range(size)])]
    pallas_call x5 -> x4, Pallas kernels: 59.4 us -> 55.6 us  [the longest x3 43.2 us: add_permuted(): pl.pallas_call(functools.partial(permute_kernel, groups, previous is not...]
  transfers between devices with their start and end apart: 18 -> 13, of which waited for: 2 -> 3; matrix products, arithmetic and copies ran while one was open for 8% -> 8% of each run, Pallas kernels for 34% -> 47%
where the time goes in v5:
time: 151 us; the launch traced here: 150 us
  Pallas kernels  81 us (54%)
  waiting for transfers between devices  25.5 us (17%)
  between operations  13.6 us (9%)
  starting transfers between devices  13 us (9%)
  local copies, waits for them, and re-layouts  11.1 us (7%)
  other arithmetic  5.95 us (4%)
    pallas_call x3, Pallas kernels, add_permuted(): pl.pallas_call(functools.partial(permute_kernel, groups, previous is not...  43.2 us
    pallas_call x2, Pallas kernels, add_whole(): pl.pallas_call(whole_kernel, grid=(lanes // tile,), in_specs=[pl.BlockSpe...  25.4 us
    ppermute x4, waiting for transfers between devices, send(): return lax.ppermute(array, 'row', [(i, i ^ bit) for i in range(size)])  18.1 us
    pallas_call x1, Pallas kernels, add_direct(): pl.pallas_call(functools.partial(direct_kernel, depth), grid_spec=pltpu.P...  12.4 us
    ppermute x4, starting transfers between devices, send(): return lax.ppermute(array, 'row', [(i, i ^ bit) for i in range(size)])  7.88 us
    all_gather x2, waiting for transfers between devices, on_device(): lax.all_gather(columns_first[:, left:right], 'col', axis=0)  7.38 us
    ppermute x3, starting transfers between devices, send_chips(): return lax.ppermute(block, 'col', pairs)  4.39 us
    reduce_sum x1, other arithmetic, stored_positions(): jnp.sum((key[None, None, :] < blocks).astype(jnp.int32), axis=2, keepdims...  3.39 us
  transfers between devices with their start and end apart: 13, of which 3 were waited for; matrix products, arithmetic and copies ran while one was open for 8% of the time, Pallas kernels for 47%

profile of v5, /device:TPU:0, one launch (start us, length us, event | category | flops | bytes accessed | tf_op | source)
XLA Modules:
  0.0 150.1 jit_solution(4317819455260828510)
XLA Ops:
  6.5 2.2 %pad_slice_fusion = bf16[352,1024]{1,0:T(8,128)(2,1)} fusion(bf16[350,2000]{1,0:T(8,128)(2,1)} %bitcast.13), kind=kLoop, calls=%fused_computation.1 | loop fusion | bytes 2120896 | tf_op jit(solution)/shard_map/slice | solution.py:254
  8.8 3.0 %collective-permute-start = (bf16[700,1400]{1,0:T(8,128)(2,1)}, bf16[700,1400]{1,0:T(8,128)(2,1)}, u32[]{:S(2)}, u32[]{:S(2)}) collective-permute-start(bf16[700,1400]{1,0:T(8,128)(2,1)} %refs_0_.1), channel_id=1, source_target_pairs={{0,16},{8,24},{16,0},{24,8},{1,17},{9,25},{17,1},{25,9},{2,18},{10... | collective-permute-start | bytes 5880008 | tf_op jit(solution)/shard_map/ppermute | solution.py:98
  11.8 1.5 collective-permute-start.2
  13.3 0.8 pad_slice_fusion.1
  14.1 1.6 %collective-permute-start.4 = (bf16[352,512]{1,0:T(8,128)(2,1)S(1)}, bf16[352,512]{1,0:T(8,128)(2,1)S(1)}, u32[]{:S(2)}, u32[]{:S(2)}) collective-permute-start(bf16[352,512]{1,0:T(8,128)(2,1)S(1)} %get-tuple-element.11.refs_0_), channel_id=1, source_target_pairs={{0,2},{1,3},{2,0},{3,1},{4,6},{5,7},{6,4},{7,5},{8,10},{9,11},{10,... | collective-permute-start | bytes 1081352 | tf_op jit(solution)/shard_map/ppermute | solution.py:121
  15.7 2.6 %collective-permute-start.5 = (bf16[352,512]{1,0:T(8,128)(2,1)S(1)}, bf16[352,512]{1,0:T(8,128)(2,1)S(1)}, u32[]{:S(2)}, u32[]{:S(2)}) collective-permute-start(bf16[352,512]{1,0:T(8,128)(2,1)S(1)} %get-tuple-element.11.refs_0_), channel_id=1, source_target_pairs={{0,4},{1,5},{2,6},{3,7},{4,0},{5,1},{6,2},{7,3},{8,12},{9,13},{10,... | collective-permute-start | bytes 1081352 | tf_op jit(solution)/shard_map/ppermute | solution.py:121
  19.1 3.4 %convert_reduce_fusion = s32[4,704]{1,0:T(4,128)S(1)} fusion(s32[4,704]{1,0:T(4,128)S(1)} %lt.42, s32[2800]{0:T(1024)S(1)} %iota_add_fusion), kind=kLoop, calls=%fused_computation | loop fusion | flops 23651584 | bytes 33728 | tf_op jit(solution)/shard_map/reduce_sum | solution.py:30
  23.0 1.4 lt.46
  26.3 1.2 broadcast_select_fusion.pos_ref
  27.5 10.8 %shard_map.46.refs_2_ = bf16[4,704,1400]{2,1,0:T(8,128)(2,1)} custom-call(s32[1]{0:T(128)} %bitcast.6.base_ref, s32[4,704,1]{2,1,0:T(8,128)} %broadcast_select_fusion.pos_ref, bf16[700,1400]{1,0:T(8,128)(2,1)} %refs_0_.1), custom_call_target="tpu_custom_call" | custom-call | flops 5519360000 | bytes 15769600 | tf_op jit(solution)/shard_map/pallas_call | solution.py:78
  38.3 17.0 %collective-permute-done.refs_1_ = bf16[700,1400]{1,0:T(8,128)(2,1)} collective-permute-done((bf16[700,1400]{1,0:T(8,128)(2,1)}, bf16[700,1400]{1,0:T(8,128)(2,1)}, u32[]{:S(2)}, u32[]{:S(2)}) %collective-permute-start) | collective-permute-done | bytes 1960032 | tf_op jit(solution)/shard_map/ppermute | solution.py:98
  55.3 1.3 slice.24
  56.6 1.8 %collective-permute-start.1 = (bf16[352,1400]{1,0:T(8,128)(2,1)S(1)}, bf16[352,1400]{1,0:T(8,128)(2,1)S(1)}, u32[]{:S(2)}, u32[]{:S(2)}) collective-permute-start(bf16[352,1400]{1,0:T(8,128)(2,1)S(1)} %slice.24), channel_id=1, source_target_pairs={{0,8},{8,0},{16,24},{24,16},{1,9},{9,1},{17,25},{25,17},{2,10},{10... | collective-permute-start | bytes 2956808 | tf_op jit(solution)/shard_map/ppermute | solution.py:98
  58.4 1.3 slice.25
  59.6 1.6 %collective-permute-start.3 = (bf16[348,1400]{1,0:T(8,128)(2,1)S(1)}, bf16[348,1400]{1,0:T(8,128)(2,1)}, u32[]{:S(2)}, u32[]{:S(2)}) collective-permute-start(bf16[348,1400]{1,0:T(8,128)(2,1)S(1)} %slice.25), channel_id=1, source_target_pairs={{0,16},{8,24},{16,0},{24,8},{1,17},{9,25},{17,1},{25,9},{2,18},{10... | collective-permute-start | bytes 2923208 | tf_op jit(solution)/shard_map/ppermute | solution.py:98
  61.2 19.3 %shard_map.47.refs_2_ = bf16[4,704,1400]{2,1,0:T(8,128)(2,1)} custom-call(s32[2]{0:T(128)} %pad_add_fusion.1.base_ref, s32[4,704,1]{2,1,0:T(8,128)} %broadcast_select_fusion.pos_ref, bf16[700,1400]{1,0:T(8,128)(2,1)} %collective-permute-done.2.refs_0_, bf16[700,1400]{1,0:T(8,128)(2,1)} %collective-permute-done.refs_1_, ...), custom_call_target="tpu_custom_call", output_to_operand_aliasing={{}: (4, {})} | custom-call | flops 11038720000 | bytes 15769600 | tf_op jit(solution)/shard_map/pallas_call | solution.py:78
  81.3 1.1 collective-permute-done.3.refs_1_
  82.3 1.0 copy-done.10
  83.3 13.1 %shard_map.48.refs_8_.v_ref = bf16[4,704,1400]{2,1,0:T(8,128)(2,1)} custom-call(s32[2]{0:T(128)} %pad_add_fusion.base_ref, s32[4,704,1]{2,1,0:T(8,128)} %broadcast_select_fusion.pos_ref, bf16[352,1400]{1,0:T(8,128)(2,1)} %copy-done.10, bf16[348,1400]{1,0:T(8,128)(2,1)} %collective-permute-done.3.refs_1_, ...), custom_call_target="tpu_custom_call", output_to_operand_aliasing={{}: (4, {})} | custom-call | flops 5519360000 | bytes 15769600 | tf_op jit(solution)/shard_map/pallas_call | solution.py:78
  97.4 0.7 copy-done.8
  98.1 12.4 %shard_map.49._ = f32[2000,1400]{1,0:T(8,128)} custom-call(s32[5]{0:T(128)} %stack.48.info_ref, bf16[352,512]{1,0:T(8,128)(2,1)} %copy-done.1, bf16[352,512]{1,0:T(8,128)(2,1)} %copy-done.6, bf16[352,512]{1,0:T(8,128)(2,1)} %copy-done.2, bf16[352,512]{1,0:T(8,128)(2,1)} %copy-done.7, bf16[352,512]{1,0:T(8,128)(2,1)} %copy-done.3, ...), custom_call_target="tpu_custom_call" | custom-call | flops 4037017600 | bytes 16502784 | tf_op jit(solution)/shard_map/pallas_call | solution.py:190
  110.6 15.2 %shard_map.50._ = f32[2000,1400]{1,0:T(8,128)} custom-call(bf16[8,352,1024]{2,1,0:T(8,128)(2,1)} %bitcast.15, bf16[4,704,1400]{2,1,0:T(8,128)(2,1)} %shard_map.48.refs_8_.v_ref, f32[2000,1400]{1,0:T(8,128)} %residual_ref.3, f32[2000,1400]{1,0:T(8,128)} %shard_map.49._), custom_call_target="tpu_custom_call", output_to_operand_aliasing={{}: (3, {})} | custom-call | flops 8074035200 | bytes 25120768 | tf_op jit(solution)/shard_map/pallas_call | solution.py:225
  125.8 7.4 %all-gather.5.cloned.1.call-done = bf16[2816,512]{1,0:T(8,128)(2,1)} async-done(((bf16[352,512]{1,0:T(8,128)(2,1)}), bf16[2816,512]{1,0:T(8,128)(2,1)}) %all-gather.5.cloned.1.call-update) | async-done | bytes 2883600 | tf_op jit(solution)/shard_map/all_gather | solution.py:254
  133.1 10.1 %shard_map.51 = f32[2000,1400]{1,0:T(8,128)} custom-call(bf16[8,352,512]{2,1,0:T(8,128)(2,1)} %bitcast.16, bf16[4,704,1400]{2,1,0:T(8,128)(2,1)} %shard_map.48.refs_8_.v_ref, f32[2000,1400]{1,0:T(8,128)} %residual_ref.3, f32[2000,1400]{1,0:T(8,128)} %shard_map.50._), custom_call_target="tpu_custom_call", output_to_operand_aliasing={{}: (3, {})} | custom-call | flops 4037017600 | bytes 16502784 | tf_op jit(solution)/shard_map/pallas_call | solution.py:225
  (56 shorter events, 4.8 us)
Async XLA Ops:
  6.5 6.8 %copy-start = (bf16[2000,350]{0,1:T(8,128)(2,1)S(1)}, bf16[2000,350]{0,1:T(8,128)(2,1)}, u32[]{:S(2)}) copy-start(bf16[2000,350]{0,1:T(8,128)(2,1)} %param.4) | copy-start | bytes 4200004
  6.5 104.0 %all-gather.7.cloned.1.call-start = ((), (), s32[]{:S(2)}) async-start(), calls=%async_computation.1 | async-start | bytes 6488064 | tf_op jit(solution)/shard_map/all_gather | solution.py:254
  8.7 9.8 %copy-start.9 = (s32[1400]{0:T(1024)S(1)}, s32[1400]{0:T(1024)}, u32[]{:S(2)}) copy-start(s32[1400]{0:T(1024)} %param.6) | copy-start | bytes 16804
  8.7 124.4 %all-gather.5.cloned.1.call-start = ((), (), s32[]{:S(2)}) async-start(), calls=%async_computation | async-start | bytes 3244032 | tf_op jit(solution)/shard_map/all_gather | solution.py:254
  8.8 46.5 %collective-permute-start = (bf16[700,1400]{1,0:T(8,128)(2,1)}, bf16[700,1400]{1,0:T(8,128)(2,1)}, u32[]{:S(2)}, u32[]{:S(2)}) collective-permute-start(bf16[700,1400]{1,0:T(8,128)(2,1)} %refs_0_.1), channel_id=1, source_target_pairs={{0,16},{8,24},{16,0},{24,8},{1,17},{9,25},{17,1},{25,9},{2,18},{10... | collective-permute-start | bytes 5880008 | tf_op jit(solution)/shard_map/ppermute | solution.py:98
  11.8 46.5 %collective-permute-start.2 = (bf16[700,1400]{1,0:T(8,128)(2,1)}, bf16[700,1400]{1,0:T(8,128)(2,1)}, u32[]{:S(2)}, u32[]{:S(2)}) collective-permute-start(bf16[700,1400]{1,0:T(8,128)(2,1)} %refs_0_.1), channel_id=1, source_target_pairs={{0,8},{8,0},{16,24},{24,16},{1,9},{9,1},{17,25},{25,17},{2,10},{10... | collective-permute-start | bytes 5880008 | tf_op jit(solution)/shard_map/ppermute | solution.py:98
  14.1 66.6 %copy-start.1 = (bf16[352,512]{1,0:T(8,128)(2,1)}, bf16[352,512]{1,0:T(8,128)(2,1)S(1)}, u32[]{:S(2)}) copy-start(bf16[352,512]{1,0:T(8,128)(2,1)S(1)} %get-tuple-element.11.refs_0_) | copy-start | bytes 1081348
  14.1 66.4 %collective-permute-start.4 = (bf16[352,512]{1,0:T(8,128)(2,1)S(1)}, bf16[352,512]{1,0:T(8,128)(2,1)S(1)}, u32[]{:S(2)}, u32[]{:S(2)}) collective-permute-start(bf16[352,512]{1,0:T(8,128)(2,1)S(1)} %get-tuple-element.11.refs_0_), channel_id=1, source_target_pairs={{0,2},{1,3},{2,0},{3,1},{4,6},{5,7},{6,4},{7,5},{8,10},{9,11},{10,... | collective-permute-start | bytes 1081352 | tf_op jit(solution)/shard_map/ppermute | solution.py:121
  15.7 64.9 %collective-permute-start.5 = (bf16[352,512]{1,0:T(8,128)(2,1)S(1)}, bf16[352,512]{1,0:T(8,128)(2,1)S(1)}, u32[]{:S(2)}, u32[]{:S(2)}) collective-permute-start(bf16[352,512]{1,0:T(8,128)(2,1)S(1)} %get-tuple-element.11.refs_0_), channel_id=1, source_target_pairs={{0,4},{1,5},{2,6},{3,7},{4,0},{5,1},{6,2},{7,3},{8,12},{9,13},{10,... | collective-permute-start | bytes 1081352 | tf_op jit(solution)/shard_map/ppermute | solution.py:121
  18.3 62.3 %collective-permute-start.6 = (bf16[352,512]{1,0:T(8,128)(2,1)S(1)}, bf16[352,512]{1,0:T(8,128)(2,1)S(1)}, u32[]{:S(2)}, u32[]{:S(2)}) collective-permute-start(bf16[352,512]{1,0:T(8,128)(2,1)S(1)} %get-tuple-element.11.refs_0_), channel_id=1, source_target_pairs={{0,6},{1,7},{2,4},{3,5},{4,2},{5,3},{6,0},{7,1},{8,14},{9,15},{10,... | collective-permute-start | bytes 1081352 | tf_op jit(solution)/shard_map/ppermute | solution.py:121
  56.6 25.8 %collective-permute-start.1 = (bf16[352,1400]{1,0:T(8,128)(2,1)S(1)}, bf16[352,1400]{1,0:T(8,128)(2,1)S(1)}, u32[]{:S(2)}, u32[]{:S(2)}) collective-permute-start(bf16[352,1400]{1,0:T(8,128)(2,1)S(1)} %slice.24), channel_id=1, source_target_pairs={{0,8},{8,0},{16,24},{24,16},{1,9},{9,1},{17,25},{25,17},{2,10},{10... | collective-permute-start | bytes 2956808 | tf_op jit(solution)/shard_map/ppermute | solution.py:98
  59.6 22.7 %collective-permute-start.3 = (bf16[348,1400]{1,0:T(8,128)(2,1)S(1)}, bf16[348,1400]{1,0:T(8,128)(2,1)}, u32[]{:S(2)}, u32[]{:S(2)}) collective-permute-start(bf16[348,1400]{1,0:T(8,128)(2,1)S(1)} %slice.25), channel_id=1, source_target_pairs={{0,16},{8,24},{16,0},{24,8},{1,17},{9,25},{17,1},{25,9},{2,18},{10... | collective-permute-start | bytes 2923208 | tf_op jit(solution)/shard_map/ppermute | solution.py:98
  80.6 15.8 %copy-start.2 = (bf16[352,512]{1,0:T(8,128)(2,1)}, bf16[352,512]{1,0:T(8,128)(2,1)S(1)}, u32[]{:S(2)}) copy-start(bf16[352,512]{1,0:T(8,128)(2,1)S(1)} %collective-permute-done.4.refs_2_) | copy-start | bytes 1081348
  80.6 15.8 %copy-start.3 = (bf16[352,512]{1,0:T(8,128)(2,1)}, bf16[352,512]{1,0:T(8,128)(2,1)S(1)}, u32[]{:S(2)}) copy-start(bf16[352,512]{1,0:T(8,128)(2,1)S(1)} %collective-permute-done.5.refs_4_) | copy-start | bytes 1081348
  80.6 15.8 %copy-start.4 = (bf16[352,512]{1,0:T(8,128)(2,1)}, bf16[352,512]{1,0:T(8,128)(2,1)S(1)}, u32[]{:S(2)}) copy-start(bf16[352,512]{1,0:T(8,128)(2,1)S(1)} %collective-permute-done.6.refs_6_) | copy-start | bytes 1081348
  80.6 15.8 %collective-permute-start.10 = (bf16[352,512]{1,0:T(8,128)(2,1)S(1)}, bf16[352,512]{1,0:T(8,128)(2,1)S(1)}, u32[]{:S(2)}, u32[]{:S(2)}) collective-permute-start(bf16[352,512]{1,0:T(8,128)(2,1)S(1)} %collective-permute-done.6.refs_6_), channel_id=1, source_target_pairs={{0,1},{1,0},{2,3},{3,2},{4,5},{5,4},{6,7},{7,6},{8,9},{9,8},{10,11... | collective-permute-start | bytes 1081352 | tf_op jit(solution)/shard_map/ppermute | solution.py:125
  80.7 15.7 %collective-permute-start.7 = (bf16[352,512]{1,0:T(8,128)(2,1)S(1)}, bf16[352,512]{1,0:T(8,128)(2,1)S(1)}, u32[]{:S(2)}, u32[]{:S(2)}) collective-permute-start(bf16[352,512]{1,0:T(8,128)(2,1)S(1)} %get-tuple-element.11.refs_0_), channel_id=1, source_target_pairs={{0,1},{1,0},{2,3},{3,2},{4,5},{5,4},{6,7},{7,6},{8,9},{9,8},{10,11... | collective-permute-start | bytes 1081352 | tf_op jit(solution)/shard_map/ppermute | solution.py:125
  81.2 15.3 %collective-permute-start.8 = (bf16[352,512]{1,0:T(8,128)(2,1)S(1)}, bf16[352,512]{1,0:T(8,128)(2,1)S(1)}, u32[]{:S(2)}, u32[]{:S(2)}) collective-permute-start(bf16[352,512]{1,0:T(8,128)(2,1)S(1)} %collective-permute-done.4.refs_2_), channel_id=1, source_target_pairs={{0,1},{1,0},{2,3},{3,2},{4,5},{5,4},{6,7},{7,6},{8,9},{9,8},{10,11... | collective-permute-start | bytes 1081352 | tf_op jit(solution)/shard_map/ppermute | solution.py:125
  82.3 14.2 %collective-permute-start.9 = (bf16[352,512]{1,0:T(8,128)(2,1)S(1)}, bf16[352,512]{1,0:T(8,128)(2,1)S(1)}, u32[]{:S(2)}, u32[]{:S(2)}) collective-permute-start(bf16[352,512]{1,0:T(8,128)(2,1)S(1)} %collective-permute-done.5.refs_4_), channel_id=1, source_target_pairs={{0,1},{1,0},{2,3},{3,2},{4,5},{5,4},{6,7},{7,6},{8,9},{9,8},{10,11... | collective-permute-start | bytes 1081352 | tf_op jit(solution)/shard_map/ppermute | solution.py:125
  82.3 1.0 copy-start.10
  96.4 0.7 copy-start.5
  96.4 0.9 copy-start.6
  96.5 0.9 copy-start.7
  97.4 0.7 copy-start.8
Sparse Core Ops, SparseCore 0:
  9.0 88.0 all-gather.6
  98.7 34.3 all-gather.4

commit v6 on v5

v6 whole, which is shorter than its diff:
```python
import functools

import jax
import jax.numpy as jnp
import numpy as np
from jax import lax
from jax.experimental import pallas as pl
from jax.experimental.pallas import tpu as pltpu
from jax.sharding import PartitionSpec as P

C_SLAB = 2
CORES = 2
TILE = 512
VMEM_BYTES = 58 << 20
CONTRACT_FIRST = (((0,), (0,)), ((), ()))


def round_up(value, step):
    return -(-value // step) * step


def stored_positions(irrep_virtual, chips, depth, depth_padded):
    pair_irrep = jnp.bitwise_xor(irrep_virtual[:C_SLAB][:, None], irrep_virtual[None, :]).reshape(-1)
    count = pair_irrep.shape[0]
    key = pair_irrep * count + jnp.arange(count, dtype=jnp.int32)
    blocks = jnp.pad(
        key.reshape(chips * CORES, depth), ((0, 0), (0, depth_padded - depth)), constant_values=-1
    ).reshape(chips, CORES * depth_padded, 1)
    rank = jnp.sum((key[None, None, :] < blocks).astype(jnp.int32), axis=2, keepdims=True)
    return jnp.where(blocks < 0, -1, rank)


def permute_kernel(groups, has_previous, base_ref, pos_ref, *refs):
    count = sum(len(group) for group in groups)
    joins = sum(len(group) > 1 for group in groups)
    out_ref, token_ref = refs[-2 - joins :][:2]
    joined = list(refs[len(refs) - joins :])
    token_ref[...] = jnp.zeros_like(token_ref)
    total = None
    pos = pos_ref[0]
    for group in groups:
        if len(group) == 1:
            rows_ref = refs[group[0]]
        else:
            rows_ref = joined.pop(0)

            @pl.when(pl.program_id(0) == 0)
            def _(group=group, rows_ref=rows_ref):
                at = 0
                for p in group:
                    rows_ref[at : at + refs[p].shape[0], :] = refs[p][...]
                    at += refs[p].shape[0]

        rows = rows_ref.shape[0]
        picks = pos - base_ref[group[0]] == lax.broadcasted_iota(jnp.int32, (pos.shape[0], rows), 1)
        term = jnp.dot(picks.astype(jnp.bfloat16), rows_ref[...], preferred_element_type=jnp.float32)
        total = term if total is None else total + term
    total = total.astype(out_ref.dtype)
    out_ref[0] = total + refs[count][0] if has_previous else total


def add_permuted(pos, blocks, bases, previous, before):
    chips, rows, _ = pos.shape
    parts = [part for block in blocks for part in block]
    columns = parts[0].shape[1]
    numbers = iter(range(len(parts)))
    groups = tuple(tuple(next(numbers) for _ in block) for block in blocks)
    joined = [
        pltpu.VMEM((sum(part.shape[0] for part in block), columns), parts[0].dtype) for block in blocks if len(block) > 1
    ]
    block_spec = pl.BlockSpec((1, rows, columns), lambda q, *_: (q, 0, 0))
    in_specs = [pl.BlockSpec((1, rows, 1), lambda q, *_: (q, 0, 0))]
    in_specs += [pl.BlockSpec(part.shape, lambda q, *_: (0, 0), pipeline_mode=pl.Buffered(1)) for part in parts]
    operands = [bases, pos, *parts]
    aliases = {}
    if previous is not None:
        in_specs.append(block_spec)
        aliases = {len(operands): 0}
        operands.append(previous)
    in_specs += [pl.BlockSpec(memory_space=pl.ANY)] * len(before)
    operands += before
    return pl.pallas_call(
        functools.partial(permute_kernel, groups, previous is not None),
        grid_spec=pltpu.PrefetchScalarGridSpec(
            num_scalar_prefetch=1, grid=(chips,), in_specs=in_specs,
            out_specs=[block_spec, pl.BlockSpec((8, 128), lambda q, *_: (0, 0))],
            scratch_shapes=joined,
        ),
        out_shape=[
            jax.ShapeDtypeStruct((chips, rows, columns), parts[0].dtype),
            jax.ShapeDtypeStruct((8, 128), jnp.float32),
        ],
        input_output_aliases=aliases,
        compiler_params=pltpu.CompilerParams(vmem_limit_bytes=VMEM_BYTES),
        cost_estimate=pl.CostEstimate(
            flops=2 * chips * rows * columns * sum(part.shape[0] for part in parts),
            bytes_accessed=4 * chips * rows * columns,
            transcendentals=0,
        ),
    )(*operands)


def gather_integrals(values, size):
    half = round_up(values.shape[0] // 2, 16)

    def send(array, bit):
        return lax.ppermute(array, "row", [(i, i ^ bit) for i in range(size)])

    got = {0: [values]}
    order = sorted(range(1, size), key=lambda d: (bin(d).count("1"), d))
    for d in order:
        low, high = d & -d, 1 << (d.bit_length() - 1)
        if low == high:
            got[d] = [send(values, d)]
            continue
        parts = []
        for which, bit in ((0, low), (1, high)):
            source = got[d ^ bit]
            if len(source) == 2:
                piece = source[which]
            else:
                piece = source[0][:half] if which == 0 else source[0][half:]
            parts.append(send(piece, bit))
        got[d] = parts
    return got, order, half


def send_chips(block, moves):
    return lax.ppermute(block, "col", [(z * CORES + core, to * CORES + core) for z, to in moves for core in range(CORES)])


def swap_cores(block, chips):
    return lax.ppermute(block, "col", [(z * CORES + core, z * CORES + 1 - core) for z in chips for core in range(CORES)])


def product_kernel(slots, depth, info_ref, *refs):
    out_ref, buffer, integrals, sems, sem_integrals = refs[-5:]
    n_arrays = CORES * sum(slots)
    arrays, natural_ref, residual_ref = refs[:n_arrays], refs[n_arrays], refs[n_arrays + 1]
    core = info_ref[0]
    tile = residual_ref.shape[0]
    i = pl.program_id(0)

    def fetch(step, half):
        lanes = pl.ds(pl.multiple_of(step * tile, tile), tile)
        at = 0
        for s, slot in enumerate(slots):
            for k in range(slot):

                def start(at=at, s=s):
                    for other in range(CORES):
                        place = (CORES * s + jnp.where(core == other, 0, 1)) * depth
                        pltpu.make_async_copy(
                            arrays[at + other].at[:, lanes],
                            buffer.at[half, pl.ds(pl.multiple_of(place, 16), depth), :],
                            sems.at[half],
                        ).start()

                if slot == 1:
                    start()
                else:
                    pl.when(info_ref[1 + 2 * s] == k)(start)
                at += CORES

    @pl.when(i == 0)
    def _():
        for s in range(len(slots)):
            pltpu.make_async_copy(
                natural_ref.at[info_ref[2 + 2 * s]],
                integrals.at[pl.ds(CORES * depth * s, CORES * depth), :],
                sem_integrals,
            ).start()
        fetch(0, 0)

    @pl.when(i + 1 < pl.num_programs(0))
    def _():
        fetch(i + 1, lax.rem(i + 1, 2))

    @pl.when(i == 0)
    def _():
        pltpu.make_async_copy(integrals, integrals, sem_integrals).wait()

    now = lax.rem(i, 2)
    pltpu.make_async_copy(buffer.at[now], buffer.at[now], sems.at[now]).wait()
    out_ref[...] = residual_ref[...] + lax.dot_general(
        buffer[now], integrals[...], CONTRACT_FIRST, preferred_element_type=jnp.float32
    )


def product_cost(lanes, rows, columns):
    return pl.CostEstimate(
        flops=2 * lanes * columns,
        bytes_accessed=8 * columns,
        transcendentals=0,
    )


def add_product(info, slots, natural, acc, in_place, token):
    tile = TILE
    depth, lanes = slots[0][0][0].shape
    tiles = lanes // tile
    columns = natural.shape[2]
    arrays = [a for slot in slots for pair in slot for a in pair]
    anywhere = pl.BlockSpec(memory_space=pl.ANY)
    block = pl.BlockSpec((tile, columns), lambda i, *_: (i, 0))
    operands = [info, *arrays, natural, acc, token]
    aliases = {len(operands) - 2: 0} if in_place else {}
    rows = CORES * depth * len(slots)
    return pl.pallas_call(
        functools.partial(product_kernel, tuple(len(slot) for slot in slots), depth),
        grid_spec=pltpu.PrefetchScalarGridSpec(
            num_scalar_prefetch=1,
            grid=(tiles,),
            in_specs=[anywhere] * (len(arrays) + 1) + [block, anywhere],
            out_specs=block,
            scratch_shapes=[
                pltpu.VMEM((2, rows, tile), natural.dtype),
                pltpu.VMEM((rows, columns), natural.dtype),
                pltpu.SemaphoreType.DMA((2,)),
                pltpu.SemaphoreType.DMA,
            ],
        ),
        out_shape=jax.ShapeDtypeStruct(acc.shape, acc.dtype),
        input_output_aliases=aliases,
        compiler_params=pltpu.CompilerParams(vmem_limit_bytes=VMEM_BYTES),
        cost_estimate=product_cost(tiles * tile, rows, columns),
    )(*operands)


def on_device(chips, row_size, amplitudes, values_stored, irrep_virtual, residual_in):
    occ, depth = amplitudes.shape
    depth_padded = round_up(depth, 16)
    stored_rows = values_stored.shape[0]
    line = chips == 4
    middle, outward, ends, inner = [(1, 2), (2, 1)], [(1, 0), (2, 3)], [0, 3], [1, 2]

    whole = jnp.pad(amplitudes.T, ((0, depth_padded - depth), (0, round_up(occ, TILE) - occ)))
    a = send_chips(whole, [(z, z ^ 1) for z in range(chips)])
    if line:
        b = send_chips(whole, middle)
    swapped = swap_cores(whole, range(chips))
    got, order, half = gather_integrals(values_stored, row_size)

    pos = stored_positions(irrep_virtual, chips, depth, depth_padded)

    def permuted(distances, previous, before):
        bases = jnp.stack([(lax.axis_index("row") ^ d) * stored_rows for d in distances for _ in got[d]])
        return add_permuted(pos, [got[d] for d in distances], bases.astype(jnp.int32), previous, before)

    near = [d for d in order if bin(d).count("1") == 1]
    far = [d for d in order if bin(d).count("1") > 1]
    natural, token = permuted([0], None, [])
    if line:
        a, b, token = lax.optimization_barrier((a, b, token))
        d = send_chips(a, middle)
        c = send_chips(b, outward)
    if near:
        natural, token = permuted(near, natural, [token] + ([swapped] if line else []))
    if line:
        a, b, d, token = lax.optimization_barrier((a, b, d, token))
        a, b = (a, swap_cores(a, range(chips))), (b, swap_cores(b, inner))
        e = send_chips(d, outward)
        d, c = (d, swap_cores(d, inner)), (c, swap_cores(c, ends))
    for distance in far:
        natural, token = permuted([distance], natural, [token] + ([a[1], b[1], d[1]] if line else []))

    core, chip = lax.axis_index("col") % CORES, lax.axis_index("col") // CORES
    if line:
        at_end = ((chip == 0) | (chip == 3)).astype(jnp.int32)
        left = chip < 2
        info = [core, 0, chip, 0, chip ^ 1, at_end, jnp.where(left, 2, 1), at_end, jnp.where(left, 3, 0)]
        slots = [
            [(whole, swapped)],
            [a],
            [b, c],
        ]
    else:
        blocks = [a] + [send_chips(whole, [(z, z ^ n) for z in range(chips)]) for n in range(2, chips)]
        slots = [[(whole, swapped)]] + [[(block, swap_cores(block, range(chips)))] for block in blocks]
        info = [core] + [number for distance in range(chips) for number in (0, chip ^ distance)]
    info = [jnp.asarray(number, jnp.int32) for number in info]
    early = 1 + 2 * len(slots)
    acc = add_product(jnp.stack(info[:early]), slots, natural, residual_in, False, token)
    if line:
        e, acc = lax.optimization_barrier((e, acc))
        last = [[d, (e, swap_cores(e, ends))]]
        acc = add_product(jnp.stack([core, *info[early:]]), last, natural, acc, True, token)
    return acc


def solution(mesh):
    in_specs = (P("row", "col"), P("row", "col"), P(), P("row", "col"))
    out_specs = P("row", "col")
    body = functools.partial(on_device, mesh.shape["col"] // CORES, mesh.shape["row"])
    return jax.shard_map(body, mesh=mesh, in_specs=in_specs, out_specs=out_specs, check_vma=False)
```

time: 151 us -> 146 us (0.967)
  between operations: 13.6 us -> 0.39 us
  starting transfers between devices: 13 us -> 23.3 us
  local copies, waits for them, and re-layouts: 11.1 us -> 9.26 us
    ppermute x7 -> x11, waiting for transfers between devices: 0.02 us -> 14 us  [the longest x5 11.2 us: send_chips(): lax.ppermute(block, 'col', [(z * CORES + core, to * CORES + core) for z,...]
    ppermute x7 -> x11, starting transfers between devices: 5.04 us -> 17.1 us  [the longest x5 9.65 us: send_chips(): lax.ppermute(block, 'col', [(z * CORES + core, to * CORES + core) for z,...]
    ppermute x4, waiting for transfers between devices: 18.1 us -> 10.5 us  [send(): return lax.ppermute(array, 'row', [(i, i ^ bit) for i in range(size)])]
    all_gather x2 -> x0, waiting for transfers between devices: 7.38 us -> none  [on_device(): lax.all_gather(columns_first[:, left:right], 'col', axis=0)]
    slice x2 -> x0, local copies, waits for them, and re-layouts: 2.97 us -> none  [the longest x1 2.15 us: on_device(): columns_first[:, left:right]]
    ppermute x4, starting transfers between devices: 7.88 us -> 6.15 us  [send(): return lax.ppermute(array, 'row', [(i, i ^ bit) for i in range(size)])]
    pallas_call x3 -> x2, Pallas kernels: 37.7 us -> 38.4 us  [add_product(): pl.pallas_call(functools.partial(product_kernel, tuple((len(slot) for slo...]
  transfers between devices with their start and end apart: 13 -> 15, of which waited for: 3 -> 3; matrix products, arithmetic and copies ran while one was open for 8% -> 8% of each run, Pallas kernels for 47% -> 46%
where the time goes in v6:
time: 146 us; the launch traced here: 145 us
  Pallas kernels  81.2 us (56%)
  waiting for transfers between devices  24.6 us (17%)
  starting transfers between devices  23.3 us (16%)
  local copies, waits for them, and re-layouts  9.26 us (6%)
  other arithmetic  6.73 us (5%)
    pallas_call x3, Pallas kernels, add_permuted(): pl.pallas_call(functools.partial(permute_kernel, groups, previous is not...  42.8 us
    pallas_call x2, Pallas kernels, add_product(): pl.pallas_call(functools.partial(product_kernel, tuple((len(slot) for slo...  38.4 us
    ppermute x5, waiting for transfers between devices, send_chips(): lax.ppermute(block, 'col', [(z * CORES + core, to * CORES + core) for z,...  11.2 us
    ppermute x4, waiting for transfers between devices, send(): return lax.ppermute(array, 'row', [(i, i ^ bit) for i in range(size)])  10.5 us
    ppermute x5, starting transfers between devices, send_chips(): lax.ppermute(block, 'col', [(z * CORES + core, to * CORES + core) for z,...  9.65 us
    ppermute x6, starting transfers between devices, swap_cores(): lax.ppermute(block, 'col', [(z * CORES + core, z * CORES + 1 - core) for...  7.46 us
    ppermute x4, starting transfers between devices, send(): return lax.ppermute(array, 'row', [(i, i ^ bit) for i in range(size)])  6.15 us
    reduce_sum x1, other arithmetic, stored_positions(): jnp.sum((key[None, None, :] < blocks).astype(jnp.int32), axis=2, keepdims...  3.38 us
  transfers between devices with their start and end apart: 15, of which 3 were waited for; matrix products, arithmetic and copies ran while one was open for 8% of the time, Pallas kernels for 46%

profile of v6, /device:TPU:0, one launch (start us, length us, event | category | flops | bytes accessed | tf_op | source)
XLA Modules:
  0.0 145.4 jit_solution(7241953081491884415)
XLA Ops:
  0.0 1.5 %pad.8.refs_0_ = bf16[352,2048]{1,0:T(8,128)(2,1)S(1)} pad(bf16[350,2000]{1,0:T(8,128)(2,1)} %bitcast.12, bf16[]{:T(256)} %constant.42.clone.1), padding=0_2x0_48 | pad | bytes 2841794 | tf_op jit(solution)/shard_map/jit(_pad)/pad | solution.py:237
  2.0 1.8 %collective-permute-start.1 = (bf16[352,2048]{1,0:T(8,128)(2,1)S(1)}, bf16[352,2048]{1,0:T(8,128)(2,1)}, u32[]{:S(2)}, u32[]{:S(2)}) collective-permute-start(bf16[352,2048]{1,0:T(8,128)(2,1)S(1)} %pad.8.refs_0_), channel_id=1, source_target_pairs={{2,4},{3,5},{4,2},{5,3},{10,12},{11,13},{12,10},{13,11},{18,20},{1... | collective-permute-start | bytes 4325384 | tf_op jit(solution)/shard_map/ppermute | solution.py:129
  3.8 4.4 %collective-permute-start = (bf16[352,2048]{1,0:T(8,128)(2,1)S(1)}, bf16[352,2048]{1,0:T(8,128)(2,1)}, u32[]{:S(2)}, u32[]{:S(2)}) collective-permute-start(bf16[352,2048]{1,0:T(8,128)(2,1)S(1)} %pad.8.refs_0_), channel_id=1, source_target_pairs={{0,2},{1,3},{2,0},{3,1},{4,6},{5,7},{6,4},{7,5},{8,10},{9,11},{10,... | collective-permute-start | bytes 4325384 | tf_op jit(solution)/shard_map/ppermute | solution.py:129
  8.2 1.5 %collective-permute-start.4 = (bf16[700,1400]{1,0:T(8,128)(2,1)}, bf16[700,1400]{1,0:T(8,128)(2,1)}, u32[]{:S(2)}, u32[]{:S(2)}) collective-permute-start(bf16[700,1400]{1,0:T(8,128)(2,1)} %refs_0_.1), channel_id=1, source_target_pairs={{0,16},{8,24},{16,0},{24,8},{1,17},{9,25},{17,1},{25,9},{2,18},{10... | collective-permute-start | bytes 5880008 | tf_op jit(solution)/shard_map/ppermute | solution.py:107
  9.7 1.5 %collective-permute-start.3 = (bf16[700,1400]{1,0:T(8,128)(2,1)}, bf16[700,1400]{1,0:T(8,128)(2,1)}, u32[]{:S(2)}, u32[]{:S(2)}) collective-permute-start(bf16[700,1400]{1,0:T(8,128)(2,1)} %refs_0_.1), channel_id=1, source_target_pairs={{0,8},{8,0},{16,24},{24,16},{1,9},{9,1},{17,25},{25,17},{2,10},{10... | collective-permute-start | bytes 5880008 | tf_op jit(solution)/shard_map/ppermute | solution.py:107
  11.8 3.4 %convert_reduce_fusion = s32[4,704]{1,0:T(4,128)S(1)} fusion(s32[4,704]{1,0:T(4,128)S(1)} %lt.47, s32[2800]{0:T(1024)S(1)} %iota_add_fusion), kind=kLoop, calls=%fused_computation | loop fusion | flops 23651584 | bytes 33728 | tf_op jit(solution)/shard_map/reduce_sum | solution.py:29
  15.2 1.4 lt.50
  18.3 10.7 %shard_map.46 = (bf16[4,704,1400]{2,1,0:T(8,128)(2,1)}, f32[8,128]{1,0:T(8,128)}) custom-call(s32[1]{0:T(128)} %bitcast.4.base_ref, s32[4,704,1]{2,1,0:T(8,128)} %broadcast_select_fusion.pos_ref, bf16[700,1400]{1,0:T(8,128)(2,1)} %refs_0_.1), custom_call_target="tpu_custom_call" | custom-call | flops 5519360000 | bytes 15769600 | tf_op jit(solution)/shard_map/pallas_call | solution.py:82
  29.0 11.2 %collective-permute-done.refs_2_ = bf16[352,2048]{1,0:T(8,128)(2,1)} collective-permute-done((bf16[352,2048]{1,0:T(8,128)(2,1)S(1)}, bf16[352,2048]{1,0:T(8,128)(2,1)}, u32[]{:S(2)}, u32[]{:S(2)}) %collective-permute-start) | collective-permute-done | bytes 1441824 | tf_op jit(solution)/shard_map/ppermute | solution.py:129
  41.0 1.3 collective-permute-start.10
  43.0 10.5 %collective-permute-done.4.refs_1_ = bf16[700,1400]{1,0:T(8,128)(2,1)} collective-permute-done((bf16[700,1400]{1,0:T(8,128)(2,1)}, bf16[700,1400]{1,0:T(8,128)(2,1)}, u32[]{:S(2)}, u32[]{:S(2)}) %collective-permute-start.4) | collective-permute-done | bytes 1960032 | tf_op jit(solution)/shard_map/ppermute | solution.py:107
  53.5 1.3 slice.12
  54.8 1.6 %collective-permute-start.12 = (bf16[352,1400]{1,0:T(8,128)(2,1)S(1)}, bf16[352,1400]{1,0:T(8,128)(2,1)}, u32[]{:S(2)}, u32[]{:S(2)}) collective-permute-start(bf16[352,1400]{1,0:T(8,128)(2,1)S(1)} %slice.12), channel_id=1, source_target_pairs={{0,8},{8,0},{16,24},{24,16},{1,9},{9,1},{17,25},{25,17},{2,10},{10... | collective-permute-start | bytes 2956808 | tf_op jit(solution)/shard_map/ppermute | solution.py:107
  56.3 1.3 slice.13
  57.6 1.6 %collective-permute-start.13 = (bf16[348,1400]{1,0:T(8,128)(2,1)S(1)}, bf16[348,1400]{1,0:T(8,128)(2,1)}, u32[]{:S(2)}, u32[]{:S(2)}) collective-permute-start(bf16[348,1400]{1,0:T(8,128)(2,1)S(1)} %slice.13), channel_id=1, source_target_pairs={{0,16},{8,24},{16,0},{24,8},{1,17},{9,25},{17,1},{25,9},{2,18},{10... | collective-permute-start | bytes 2923208 | tf_op jit(solution)/shard_map/ppermute | solution.py:107
  59.2 19.4 %shard_map.47 = (bf16[4,704,1400]{2,1,0:T(8,128)(2,1)}, f32[8,128]{1,0:T(8,128)}) custom-call(s32[2]{0:T(128)} %pad_add_fusion.1.base_ref, s32[4,704,1]{2,1,0:T(8,128)} %broadcast_select_fusion.pos_ref, bf16[700,1400]{1,0:T(8,128)(2,1)} %collective-permute-done.3.refs_0_, ...), custom_call_target="tpu_custom_call", output_to_operand_aliasing={{0}: (4, {})} | custom-call | flops 11038720000 | bytes 15769600 | tf_op jit(solution)/shard_map/pallas_call | solution.py:82
  78.6 1.8 %collective-permute-start.9 = (bf16[352,2048]{1,0:T(8,128)(2,1)}, bf16[352,2048]{1,0:T(8,128)(2,1)}, u32[]{:S(2)}, u32[]{:S(2)}) collective-permute-start(bf16[352,2048]{1,0:T(8,128)(2,1)} %collective-permute-done.1.refs_4_), channel_id=1, source_target_pairs={{2,3},{3,2},{4,5},{5,4},{10,11},{11,10},{12,13},{13,12},{18,19},{1... | collective-permute-start | bytes 4325384 | tf_op jit(solution)/shard_map/ppermute | solution.py:133
  81.2 2.4 %collective-permute-start.11 = (bf16[352,2048]{1,0:T(8,128)(2,1)}, bf16[352,2048]{1,0:T(8,128)(2,1)}, u32[]{:S(2)}, u32[]{:S(2)}) collective-permute-start(bf16[352,2048]{1,0:T(8,128)(2,1)} %collective-permute-done.10.refs_6_), channel_id=1, source_target_pairs={{0,1},{1,0},{6,7},{7,6},{8,9},{9,8},{14,15},{15,14},{16,17},{17,16... | collective-permute-start | bytes 4325384 | tf_op jit(solution)/shard_map/ppermute | solution.py:133
  83.6 1.5 %collective-permute-start.7 = (bf16[352,2048]{1,0:T(8,128)(2,1)S(1)}, bf16[352,2048]{1,0:T(8,128)(2,1)}, u32[]{:S(2)}, u32[]{:S(2)}) collective-permute-start(bf16[352,2048]{1,0:T(8,128)(2,1)S(1)} %collective-permute-done.2.refs_0_), channel_id=1, source_target_pairs={{2,0},{3,1},{4,6},{5,7},{10,8},{11,9},{12,14},{13,15},{18,16},{19,... | collective-permute-start | bytes 4325384 | tf_op jit(solution)/shard_map/ppermute | solution.py:129
  87.7 12.7 %shard_map.48 = (bf16[4,704,1400]{2,1,0:T(8,128)(2,1)}, f32[8,128]{1,0:T(8,128)}) custom-call(s32[2]{0:T(128)} %pad_add_fusion.2.base_ref, s32[4,704,1]{2,1,0:T(8,128)} %broadcast_select_fusion.pos_ref, bf16[352,1400]{1,0:T(8,128)(2,1)} %collective-permute-done.12.refs_0_, ...), custom_call_target="tpu_custom_call", output_to_operand_aliasing={{0}: (4, {})} | custom-call | flops 5519360000 | bytes 15769600 | tf_op jit(solution)/shard_map/pallas_call | solution.py:82
  100.4 23.8 %shard_map.49.refs_5_ = f32[2000,1400]{1,0:T(8,128)} custom-call(s32[7]{0:T(128)} %stack.60.info_ref, bf16[352,2048]{1,0:T(8,128)(2,1)} %copy-done, bf16[352,2048]{1,0:T(8,128)(2,1)} %collective-permute-done.5.refs_4_.refs_1_, bf16[352,2048]{1,0:T(8,128)(2,1)} %collective-permute-done.refs_2_, bf16[352,2048]{1,0:T(8,128)(2,1)} %collective-permute-done.8.refs_4_.refs_3_, ...), custom_call_target="tpu_custom_call" | custom-call | flops 5734400 | bytes 11200 | tf_op jit(solution)/shard_map/pallas_call | solution.py:209
  124.2 1.9 %collective-permute-start.14 = (bf16[352,2048]{1,0:T(8,128)(2,1)}, bf16[352,2048]{1,0:T(8,128)(2,1)S(1)}, u32[]{:S(2)}, u32[]{:S(2)}) collective-permute-start(bf16[352,2048]{1,0:T(8,128)(2,1)} %collective-permute-done.7.refs_2_), channel_id=1, source_target_pairs={{0,1},{1,0},{6,7},{7,6},{8,9},{9,8},{14,15},{15,14},{16,17},{17,16... | collective-permute-start | bytes 4325384 | tf_op jit(solution)/shard_map/ppermute | solution.py:133
  126.8 2.8 %collective-permute-done.14.refs_3_ = bf16[352,2048]{1,0:T(8,128)(2,1)S(1)} collective-permute-done((bf16[352,2048]{1,0:T(8,128)(2,1)}, bf16[352,2048]{1,0:T(8,128)(2,1)S(1)}, u32[]{:S(2)}, u32[]{:S(2)}) %collective-permute-start.14) | collective-permute-done | bytes 1441824 | tf_op jit(solution)/shard_map/ppermute | solution.py:133
  130.7 14.6 %shard_map.50 = f32[2000,1400]{1,0:T(8,128)} custom-call(s32[3]{0:T(128)} %pad_add_fusion.info_ref, bf16[352,2048]{1,0:T(8,128)(2,1)} %copy-done.1, bf16[352,2048]{1,0:T(8,128)(2,1)} %copy-done.2, bf16[352,2048]{1,0:T(8,128)(2,1)} %collective-permute-done.7.refs_2_, bf16[352,2048]{1,0:T(8,128)(2,1)} %copy-done.3, ...), custom_call_target="tpu_custom_call", output_to_operand_aliasing={{}: (6, {})} | custom-call | flops 5734400 | bytes 11200 | tf_op jit(solution)/shard_map/pallas_call | solution.py:209
  (45 shorter events, 9.3 us)
Async XLA Ops:
  0.0 11.2 %copy-start.4 = (s32[1400]{0:T(1024)S(1)}, s32[1400]{0:T(1024)}, u32[]{:S(2)}) copy-start(s32[1400]{0:T(1024)} %param.6) | copy-start | bytes 16804
  1.5 16.8 %copy-start = (bf16[352,2048]{1,0:T(8,128)(2,1)}, bf16[352,2048]{1,0:T(8,128)(2,1)S(1)}, u32[]{:S(2)}) copy-start(bf16[352,2048]{1,0:T(8,128)(2,1)S(1)} %pad.8.refs_0_) | copy-start | bytes 4325380
  1.5 57.7 %collective-permute-start.5 = (bf16[352,2048]{1,0:T(8,128)(2,1)S(1)}, bf16[352,2048]{1,0:T(8,128)(2,1)}, u32[]{:S(2)}, u32[]{:S(2)}) collective-permute-start(bf16[352,2048]{1,0:T(8,128)(2,1)S(1)} %pad.8.refs_0_), channel_id=1, source_target_pairs={{0,1},{1,0},{2,3},{3,2},{4,5},{5,4},{6,7},{7,6},{8,9},{9,8},{10,11... | collective-permute-start | bytes 4325384 | tf_op jit(solution)/shard_map/ppermute | solution.py:133
  2.0 27.0 %collective-permute-start.1 = (bf16[352,2048]{1,0:T(8,128)(2,1)S(1)}, bf16[352,2048]{1,0:T(8,128)(2,1)}, u32[]{:S(2)}, u32[]{:S(2)}) collective-permute-start(bf16[352,2048]{1,0:T(8,128)(2,1)S(1)} %pad.8.refs_0_), channel_id=1, source_target_pairs={{2,4},{3,5},{4,2},{5,3},{10,12},{11,13},{12,10},{13,11},{18,20},{1... | collective-permute-start | bytes 4325384 | tf_op jit(solution)/shard_map/ppermute | solution.py:129
  3.8 36.4 %collective-permute-start = (bf16[352,2048]{1,0:T(8,128)(2,1)S(1)}, bf16[352,2048]{1,0:T(8,128)(2,1)}, u32[]{:S(2)}, u32[]{:S(2)}) collective-permute-start(bf16[352,2048]{1,0:T(8,128)(2,1)S(1)} %pad.8.refs_0_), channel_id=1, source_target_pairs={{0,2},{1,3},{2,0},{3,1},{4,6},{5,7},{6,4},{7,5},{8,10},{9,11},{10,... | collective-permute-start | bytes 4325384 | tf_op jit(solution)/shard_map/ppermute | solution.py:129
  8.2 45.3 %collective-permute-start.4 = (bf16[700,1400]{1,0:T(8,128)(2,1)}, bf16[700,1400]{1,0:T(8,128)(2,1)}, u32[]{:S(2)}, u32[]{:S(2)}) collective-permute-start(bf16[700,1400]{1,0:T(8,128)(2,1)} %refs_0_.1), channel_id=1, source_target_pairs={{0,16},{8,24},{16,0},{24,8},{1,17},{9,25},{17,1},{25,9},{2,18},{10... | collective-permute-start | bytes 5880008 | tf_op jit(solution)/shard_map/ppermute | solution.py:107
  9.7 46.6 %collective-permute-start.3 = (bf16[700,1400]{1,0:T(8,128)(2,1)}, bf16[700,1400]{1,0:T(8,128)(2,1)}, u32[]{:S(2)}, u32[]{:S(2)}) collective-permute-start(bf16[700,1400]{1,0:T(8,128)(2,1)} %refs_0_.1), channel_id=1, source_target_pairs={{0,8},{8,0},{16,24},{24,16},{1,9},{9,1},{17,25},{25,17},{2,10},{10... | collective-permute-start | bytes 5880008 | tf_op jit(solution)/shard_map/ppermute | solution.py:107
  40.2 38.3 %collective-permute-start.2 = (bf16[352,2048]{1,0:T(8,128)(2,1)}, bf16[352,2048]{1,0:T(8,128)(2,1)S(1)}, u32[]{:S(2)}, u32[]{:S(2)}) collective-permute-start(bf16[352,2048]{1,0:T(8,128)(2,1)} %collective-permute-done.refs_2_), channel_id=1, source_target_pairs={{2,4},{3,5},{4,2},{5,3},{10,12},{11,13},{12,10},{13,11},{18,20},{1... | collective-permute-start | bytes 4325384 | tf_op jit(solution)/shard_map/ppermute | solution.py:129
  41.0 39.5 %collective-permute-start.10 = (bf16[352,2048]{1,0:T(8,128)(2,1)}, bf16[352,2048]{1,0:T(8,128)(2,1)}, u32[]{:S(2)}, u32[]{:S(2)}) collective-permute-start(bf16[352,2048]{1,0:T(8,128)(2,1)} %collective-permute-done.1.refs_4_), channel_id=1, source_target_pairs={{2,0},{3,1},{4,6},{5,7},{10,8},{11,9},{12,14},{13,15},{18,16},{19,... | collective-permute-start | bytes 4325384 | tf_op jit(solution)/shard_map/ppermute | solution.py:129
  54.8 28.8 %collective-permute-start.12 = (bf16[352,1400]{1,0:T(8,128)(2,1)S(1)}, bf16[352,1400]{1,0:T(8,128)(2,1)}, u32[]{:S(2)}, u32[]{:S(2)}) collective-permute-start(bf16[352,1400]{1,0:T(8,128)(2,1)S(1)} %slice.12), channel_id=1, source_target_pairs={{0,8},{8,0},{16,24},{24,16},{1,9},{9,1},{17,25},{25,17},{2,10},{10... | collective-permute-start | bytes 2956808 | tf_op jit(solution)/shard_map/ppermute | solution.py:107
  57.6 23.6 %collective-permute-start.13 = (bf16[348,1400]{1,0:T(8,128)(2,1)S(1)}, bf16[348,1400]{1,0:T(8,128)(2,1)}, u32[]{:S(2)}, u32[]{:S(2)}) collective-permute-start(bf16[348,1400]{1,0:T(8,128)(2,1)S(1)} %slice.13), channel_id=1, source_target_pairs={{0,16},{8,24},{16,0},{24,8},{1,17},{9,25},{17,1},{25,9},{2,18},{10... | collective-permute-start | bytes 2923208 | tf_op jit(solution)/shard_map/ppermute | solution.py:107
  78.6 21.8 %copy-start.1 = (bf16[352,2048]{1,0:T(8,128)(2,1)}, bf16[352,2048]{1,0:T(8,128)(2,1)S(1)}, u32[]{:S(2)}) copy-start(bf16[352,2048]{1,0:T(8,128)(2,1)S(1)} %collective-permute-done.2.refs_0_) | copy-start | bytes 4325380
  78.6 7.9 %collective-permute-start.8 = (bf16[352,2048]{1,0:T(8,128)(2,1)}, bf16[352,2048]{1,0:T(8,128)(2,1)}, u32[]{:S(2)}, u32[]{:S(2)}) collective-permute-start(bf16[352,2048]{1,0:T(8,128)(2,1)} %collective-permute-done.refs_2_), channel_id=1, source_target_pairs={{0,1},{1,0},{2,3},{3,2},{4,5},{5,4},{6,7},{7,6},{8,9},{9,8},{10,11... | collective-permute-start | bytes 4325384 | tf_op jit(solution)/shard_map/ppermute | solution.py:133
  78.6 7.8 %collective-permute-start.9 = (bf16[352,2048]{1,0:T(8,128)(2,1)}, bf16[352,2048]{1,0:T(8,128)(2,1)}, u32[]{:S(2)}, u32[]{:S(2)}) collective-permute-start(bf16[352,2048]{1,0:T(8,128)(2,1)} %collective-permute-done.1.refs_4_), channel_id=1, source_target_pairs={{2,3},{3,2},{4,5},{5,4},{10,11},{11,10},{12,13},{13,12},{18,19},{1... | collective-permute-start | bytes 4325384 | tf_op jit(solution)/shard_map/ppermute | solution.py:133
  80.4 6.0 %collective-permute-start.6 = (bf16[352,2048]{1,0:T(8,128)(2,1)S(1)}, bf16[352,2048]{1,0:T(8,128)(2,1)S(1)}, u32[]{:S(2)}, u32[]{:S(2)}) collective-permute-start(bf16[352,2048]{1,0:T(8,128)(2,1)S(1)} %collective-permute-done.2.refs_0_), channel_id=1, source_target_pairs={{2,3},{3,2},{4,5},{5,4},{10,11},{11,10},{12,13},{13,12},{18,19},{1... | collective-permute-start | bytes 4325384 | tf_op jit(solution)/shard_map/ppermute | solution.py:133
  81.2 19.2 %collective-permute-start.11 = (bf16[352,2048]{1,0:T(8,128)(2,1)}, bf16[352,2048]{1,0:T(8,128)(2,1)}, u32[]{:S(2)}, u32[]{:S(2)}) collective-permute-start(bf16[352,2048]{1,0:T(8,128)(2,1)} %collective-permute-done.10.refs_6_), channel_id=1, source_target_pairs={{0,1},{1,0},{6,7},{7,6},{8,9},{9,8},{14,15},{15,14},{16,17},{17,16... | collective-permute-start | bytes 4325384 | tf_op jit(solution)/shard_map/ppermute | solution.py:133
  83.6 40.6 %collective-permute-start.7 = (bf16[352,2048]{1,0:T(8,128)(2,1)S(1)}, bf16[352,2048]{1,0:T(8,128)(2,1)}, u32[]{:S(2)}, u32[]{:S(2)}) collective-permute-start(bf16[352,2048]{1,0:T(8,128)(2,1)S(1)} %collective-permute-done.2.refs_0_), channel_id=1, source_target_pairs={{2,0},{3,1},{4,6},{5,7},{10,8},{11,9},{12,14},{13,15},{18,16},{19,... | collective-permute-start | bytes 4325384 | tf_op jit(solution)/shard_map/ppermute | solution.py:129
  86.5 1.2 copy-start.2
  124.2 5.3 %collective-permute-start.14 = (bf16[352,2048]{1,0:T(8,128)(2,1)}, bf16[352,2048]{1,0:T(8,128)(2,1)S(1)}, u32[]{:S(2)}, u32[]{:S(2)}) collective-permute-start(bf16[352,2048]{1,0:T(8,128)(2,1)} %collective-permute-done.7.refs_2_), channel_id=1, source_target_pairs={{0,1},{1,0},{6,7},{7,6},{8,9},{9,8},{14,15},{15,14},{16,17},{17,16... | collective-permute-start | bytes 4325384 | tf_op jit(solution)/shard_map/ppermute | solution.py:133
  129.6 1.1 copy-start.3

commit v7 on v6

--- a/solution.py
+++ b/solution.py
@@ -133,10 +133,14 @@
     return lax.ppermute(block, "col", [(z * CORES + core, z * CORES + 1 - core) for z in chips for core in range(CORES)])
 
 
-def product_kernel(slots, depth, info_ref, *refs):
-    out_ref, buffer, integrals, sems, sem_integrals = refs[-5:]
+def product_kernel(slots, chips, depth, halves, info_ref, *refs):
+    joined_ref, buffer, integrals, sems, sems_integrals = refs[-5:]
+    out_ref, far_ref = refs[-7:-5]
+    count = len(slots)
     n_arrays = CORES * sum(slots)
-    arrays, natural_ref, residual_ref = refs[:n_arrays], refs[n_arrays], refs[n_arrays + 1]
+    arrays = refs[:n_arrays]
+    natural_ref, residual_ref, pos_ref = refs[n_arrays : n_arrays + 3]
+    missing = refs[n_arrays + 3 : n_arrays + 3 + halves]
     core = info_ref[0]
     tile = residual_ref.shape[0]
     i = pl.program_id(0)
@@ -162,14 +166,13 @@
                     pl.when(info_ref[1 + 2 * s] == k)(start)
                 at += CORES
 
+    def copy_integrals(q):
+        return pltpu.make_async_copy(natural_ref.at[q], integrals.at[q], sems_integrals.at[q])
+
     @pl.when(i == 0)
     def _():
-        for s in range(len(slots)):
-            pltpu.make_async_copy(
-                natural_ref.at[info_ref[2 + 2 * s]],
-                integrals.at[pl.ds(CORES * depth * s, CORES * depth), :],
-                sem_integrals,
-            ).start()
+        for q in range(chips):
+            copy_integrals(q).start()
         fetch(0, 0)
 
     @pl.when(i + 1 < pl.num_programs(0))
@@ -178,12 +181,64 @@
 
     @pl.when(i == 0)
     def _():
-        pltpu.make_async_copy(integrals, integrals, sem_integrals).wait()
+        at = 0
+        for part in missing:
+            joined_ref[at : at + part.shape[0], :] = part[...]
+            at += part.shape[0]
+        for q in range(chips):
+            rows = joined_ref.shape[0]
+            picks = pos_ref[q] - info_ref[2 + 2 * count] == lax.broadcasted_iota(
+                jnp.int32, (pos_ref.shape[1], rows), 1
+            )
+            term = jnp.dot(picks.astype(jnp.bfloat16), joined_ref[...], preferred_element_type=jnp.float32)
+            copy_integrals(q).wait()
+            integrals[q] = integrals[q] + term.astype(integrals.dtype)
+        far_ref[...] = integrals[info_ref[1 + 2 * count]]
 
     now = lax.rem(i, 2)
     pltpu.make_async_copy(buffer.at[now], buffer.at[now], sems.at[now]).wait()
-    out_ref[...] = residual_ref[...] + lax.dot_general(
-        buffer[now], integrals[...], CONTRACT_FIRST, preferred_element_type=jnp.float32
+    total = residual_ref[...]
+    for s in range(count):
+        total += lax.dot_general(
+            buffer[now, CORES * depth * s : CORES * depth * (s + 1), :],
+            integrals[info_ref[2 + 2 * s]],
+            CONTRACT_FIRST,
+            preferred_element_type=jnp.float32,
+        )
+    out_ref[...] = total
+
+
+def last_kernel(mine, info_ref, *refs):
+    arrays, (far_ref, acc_ref, out_ref, buffer, sem) = refs[:-5], refs[-5:]
+    depth, tile = arrays[0].shape[0], acc_ref.shape[0]
+    i = pl.program_id(0)
+
+    def fetch(step, half):
+        lanes = pl.ds(pl.multiple_of(step * tile, tile), tile)
+        for k in range(mine):
+
+            @pl.when(info_ref[1] == k)
+            def _(k=k):
+                for other in range(CORES):
+                    place = jnp.where(info_ref[0] == other, 0, depth)
+                    pltpu.make_async_copy(
+                        arrays[CORES * k + other].at[:, lanes],
+                        buffer.at[half, pl.ds(pl.multiple_of(place, 16), depth), :],
+                        sem.at[half],
+                    ).start()
+
+    @pl.when(i == 0)
+    def _():
+        fetch(0, 0)
+
+    @pl.when(i + 1 < pl.num_programs(0))
+    def _():
+        fetch(i + 1, lax.rem(i + 1, 2))
+
+    now = lax.rem(i, 2)
+    pltpu.make_async_copy(buffer.at[now], buffer.at[now], sem.at[now]).wait()
+    out_ref[...] = acc_ref[...] + lax.dot_general(
+        buffer[now], far_ref[...], CONTRACT_FIRST, preferred_element_type=jnp.float32
     )
 
 
@@ -195,35 +250,62 @@
     )
 
 
-def add_product(info, slots, natural, acc, in_place, token):
+def add_product(info, slots, natural, pos, missing, acc, before):
     tile = TILE
     depth, lanes = slots[0][0][0].shape
-    tiles = lanes // tile
-    columns = natural.shape[2]
+    chips, chip_rows, columns = natural.shape
     arrays = [a for slot in slots for pair in slot for a in pair]
     anywhere = pl.BlockSpec(memory_space=pl.ANY)
     block = pl.BlockSpec((tile, columns), lambda i, *_: (i, 0))
-    operands = [info, *arrays, natural, acc, token]
-    aliases = {len(operands) - 2: 0} if in_place else {}
     rows = CORES * depth * len(slots)
+
+    def once(shape):
+        return pl.BlockSpec(shape, lambda i, *_: (0,) * len(shape), pipeline_mode=pl.Buffered(1))
+
     return pl.pallas_call(
-        functools.partial(product_kernel, tuple(len(slot) for slot in slots), depth),
+        functools.partial(product_kernel, tuple(len(slot) for slot in slots), chips, depth, len(missing)),
         grid_spec=pltpu.PrefetchScalarGridSpec(
             num_scalar_prefetch=1,
-            grid=(tiles,),
-            in_specs=[anywhere] * (len(arrays) + 1) + [block, anywhere],
-            out_specs=block,
+            grid=(lanes // tile,),
+            in_specs=[anywhere] * (len(arrays) + 1) + [block, once(pos.shape)] + [once(part.shape) for part in missing] + [anywhere] * len(before),
+            out_specs=[block, pl.BlockSpec((chip_rows, columns), lambda i, *_: (0, 0))],
             scratch_shapes=[
+                pltpu.VMEM((sum(part.shape[0] for part in missing), columns), natural.dtype),
                 pltpu.VMEM((2, rows, tile), natural.dtype),
-                pltpu.VMEM((rows, columns), natural.dtype),
+                pltpu.VMEM(natural.shape, natural.dtype),
                 pltpu.SemaphoreType.DMA((2,)),
-                pltpu.SemaphoreType.DMA,
+                pltpu.SemaphoreType.DMA((chips,)),
             ],
         ),
+        out_shape=[
+            jax.ShapeDtypeStruct(acc.shape, acc.dtype),
+            jax.ShapeDtypeStruct((chip_rows, columns), natural.dtype),
+        ],
+        compiler_params=pltpu.CompilerParams(vmem_limit_bytes=VMEM_BYTES),
+        cost_estimate=product_cost(lanes, rows, columns),
+    )(info, *arrays, natural, acc, pos, *missing, *before)
+
+
+def add_last(info, slot, far, acc):
+    tile = TILE
+    depth, lanes = slot[0][0].shape
+    arrays = [a for pair in slot for a in pair]
+    block = pl.BlockSpec((tile, far.shape[1]), lambda i, *_: (i, 0))
+    operands = [info, *arrays, far, acc]
+    return pl.pallas_call(
+        functools.partial(last_kernel, len(slot)),
+        grid_spec=pltpu.PrefetchScalarGridSpec(
+            num_scalar_prefetch=1,
+            grid=(lanes // tile,),
+            in_specs=[pl.BlockSpec(memory_space=pl.ANY)] * len(arrays)
+            + [pl.BlockSpec(far.shape, lambda i, *_: (0, 0), pipeline_mode=pl.Buffered(1)), block],
+            out_specs=block,
+            scratch_shapes=[pltpu.VMEM((2, CORES * depth, tile), far.dtype), pltpu.SemaphoreType.DMA((2,))],
+        ),
         out_shape=jax.ShapeDtypeStruct(acc.shape, acc.dtype),
-        input_output_aliases=aliases,
+        input_output_aliases={len(operands) - 1: 0},
         compiler_params=pltpu.CompilerParams(vmem_limit_bytes=VMEM_BYTES),
-        cost_estimate=product_cost(tiles * tile, rows, columns),
+        cost_estimate=product_cost(lanes, CORES * depth, far.shape[1]),
     )(*operands)
 
 
@@ -261,8 +343,9 @@
         a, b = (a, swap_cores(a, range(chips))), (b, swap_cores(b, inner))
         e = send_chips(d, outward)
         d, c = (d, swap_cores(d, inner)), (c, swap_cores(c, ends))
-    for distance in far:
-        natural, token = permuted([distance], natural, [token] + ([a[1], b[1], d[1]] if line else []))
+    for distance in far[:-1]:
+        natural, token = permuted([distance], natural, [token])
+    missing, missing_at = got[far[-1]], (lax.axis_index("row") ^ far[-1]) * stored_rows
 
     core, chip = lax.axis_index("col") % CORES, lax.axis_index("col") // CORES
     if line:
@@ -278,14 +361,16 @@
         blocks = [a] + [send_chips(whole, [(z, z ^ n) for z in range(chips)]) for n in range(2, chips)]
         slots = [[(whole, swapped)]] + [[(block, swap_cores(block, range(chips)))] for block in blocks]
         info = [core] + [number for distance in range(chips) for number in (0, chip ^ distance)]
-    info = [jnp.asarray(number, jnp.int32) for number in info]
-    early = 1 + 2 * len(slots)
-    acc = add_product(jnp.stack(info[:early]), slots, natural, residual_in, False, token)
-    if line:
-        e, acc = lax.optimization_barrier((e, acc))
-        last = [[d, (e, swap_cores(e, ends))]]
-        acc = add_product(jnp.stack([core, *info[early:]]), last, natural, acc, True, token)
-    return acc
+    info = [jnp.asarray(number, jnp.int32) for number in [*info, missing_at]]
+    if not line:
+        return add_product(jnp.stack([*info[:-1], info[0], info[-1]]), slots, natural, pos, missing, residual_in, [token])[0]
+    choice, far_chip = info[-3], info[-2]
+    acc, far_rows = add_product(
+        jnp.stack([*info[:-3], far_chip, info[-1]]), slots, natural, pos, missing, residual_in, [token, d[1]]
+    )
+    e, acc = lax.optimization_barrier((e, acc))
+    e = (e, swap_cores(e, ends))
+    return add_last(jnp.stack([core, choice]), [d, e], far_rows, acc)
 
 
 def solution(mesh):

time: 146 us -> 142 us (0.973)
  waiting for transfers between devices: 24.6 us -> 30.9 us
  Pallas kernels: 81.2 us -> 75.8 us
  starting transfers between devices: 23.3 us -> 20.5 us
    pallas_call x0 -> x1, Pallas kernels: none -> 14.3 us  [add_last(): pl.pallas_call(functools.partial(last_kernel, len(slot)), grid_spec=pltpu...]
    pallas_call x3 -> x2, Pallas kernels: 42.8 us -> 30.1 us  [add_permuted(): pl.pallas_call(functools.partial(permute_kernel, groups, previous is not...]
    pallas_call x2 -> x1, Pallas kernels: 38.4 us -> 31.4 us  [add_product(): pl.pallas_call(functools.partial(product_kernel, tuple((len(slot) for slo...]
    ppermute x4, waiting for transfers between devices: 10.5 us -> 14.7 us  [send(): return lax.ppermute(array, 'row', [(i, i ^ bit) for i in range(size)])]
  transfers between devices with their start and end apart: 15 -> 15, of which waited for: 3 -> 5; matrix products, arithmetic and copies ran while one was open for 8% -> 8% of each run, Pallas kernels for 46% -> 43%
where the time goes in v7:
time: 142 us
  Pallas kernels  75.8 us (53%)
  waiting for transfers between devices  30.9 us (22%)
  starting transfers between devices  20.5 us (14%)
  local copies, waits for them, and re-layouts  8.17 us (6%)
  other arithmetic  5.99 us (4%)
    pallas_call x1, Pallas kernels, add_product(): pl.pallas_call(functools.partial(product_kernel, tuple((len(slot) for slo...  31.4 us
    pallas_call x2, Pallas kernels, add_permuted(): pl.pallas_call(functools.partial(permute_kernel, groups, previous is not...  30.1 us
    ppermute x4, waiting for transfers between devices, send(): return lax.ppermute(array, 'row', [(i, i ^ bit) for i in range(size)])  14.7 us
    pallas_call x1, Pallas kernels, add_last(): pl.pallas_call(functools.partial(last_kernel, len(slot)), grid_spec=pltpu...  14.3 us
    ppermute x5, waiting for transfers between devices, send_chips(): lax.ppermute(block, 'col', [(z * CORES + core, to * CORES + core) for z,...  12.5 us
    ppermute x5, starting transfers between devices, send_chips(): lax.ppermute(block, 'col', [(z * CORES + core, to * CORES + core) for z,...  8.43 us
    ppermute x6, starting transfers between devices, swap_cores(): lax.ppermute(block, 'col', [(z * CORES + core, z * CORES + 1 - core) for...  6.89 us
    ppermute x4, starting transfers between devices, send(): return lax.ppermute(array, 'row', [(i, i ^ bit) for i in range(size)])  5.2 us
  transfers between devices with their start and end apart: 15, of which 5 were waited for; matrix products, arithmetic and copies ran while one was open for 8% of the time, Pallas kernels for 43%

profile of v7, /device:TPU:0, one launch (start us, length us, event | category | flops | bytes accessed | tf_op | source)
XLA Modules:
  0.0 141.8 jit_solution(15971703967286441593)
XLA Ops:
  0.0 1.5 %pad.8.refs_0_ = bf16[352,2048]{1,0:T(8,128)(2,1)S(1)} pad(bf16[350,2000]{1,0:T(8,128)(2,1)} %bitcast.12, bf16[]{:T(256)} %constant.42.clone.1), padding=0_2x0_48 | pad | bytes 2841794 | tf_op jit(solution)/shard_map/jit(_pad)/pad | solution.py:319
  1.5 3.1 %collective-permute-start = (bf16[352,2048]{1,0:T(8,128)(2,1)S(1)}, bf16[352,2048]{1,0:T(8,128)(2,1)}, u32[]{:S(2)}, u32[]{:S(2)}) collective-permute-start(bf16[352,2048]{1,0:T(8,128)(2,1)S(1)} %pad.8.refs_0_), channel_id=1, source_target_pairs={{0,2},{1,3},{2,0},{3,1},{4,6},{5,7},{6,4},{7,5},{8,10},{9,11},{10,... | collective-permute-start | bytes 4325384 | tf_op jit(solution)/shard_map/ppermute | solution.py:129
  4.6 1.8 %collective-permute-start.1 = (bf16[352,2048]{1,0:T(8,128)(2,1)S(1)}, bf16[352,2048]{1,0:T(8,128)(2,1)}, u32[]{:S(2)}, u32[]{:S(2)}) collective-permute-start(bf16[352,2048]{1,0:T(8,128)(2,1)S(1)} %pad.8.refs_0_), channel_id=1, source_target_pairs={{2,4},{3,5},{4,2},{5,3},{10,12},{11,13},{12,10},{13,11},{18,20},{1... | collective-permute-start | bytes 4325384 | tf_op jit(solution)/shard_map/ppermute | solution.py:129
  6.4 1.5 %collective-permute-start.3 = (bf16[700,1400]{1,0:T(8,128)(2,1)}, bf16[700,1400]{1,0:T(8,128)(2,1)}, u32[]{:S(2)}, u32[]{:S(2)}) collective-permute-start(bf16[700,1400]{1,0:T(8,128)(2,1)} %refs_0_.1), channel_id=1, source_target_pairs={{0,8},{8,0},{16,24},{24,16},{1,9},{9,1},{17,25},{25,17},{2,10},{10... | collective-permute-start | bytes 5880008 | tf_op jit(solution)/shard_map/ppermute | solution.py:107
  7.9 1.5 %collective-permute-start.4 = (bf16[700,1400]{1,0:T(8,128)(2,1)}, bf16[700,1400]{1,0:T(8,128)(2,1)}, u32[]{:S(2)}, u32[]{:S(2)}) collective-permute-start(bf16[700,1400]{1,0:T(8,128)(2,1)} %refs_0_.1), channel_id=1, source_target_pairs={{0,16},{8,24},{16,0},{24,8},{1,17},{9,25},{17,1},{25,9},{2,18},{10... | collective-permute-start | bytes 5880008 | tf_op jit(solution)/shard_map/ppermute | solution.py:107
  10.0 3.4 %convert_reduce_fusion = s32[4,704]{1,0:T(4,128)S(1)} fusion(s32[4,704]{1,0:T(4,128)S(1)} %lt.46, s32[2800]{0:T(1024)S(1)} %iota_add_fusion), kind=kLoop, calls=%fused_computation | loop fusion | flops 23651584 | bytes 33728 | tf_op jit(solution)/shard_map/reduce_sum | solution.py:29
  13.9 1.4 lt.50
  15.3 1.3 broadcast_select_fusion.pos_ref.refs_10_
  16.6 10.7 %shard_map.46 = (bf16[4,704,1400]{2,1,0:T(8,128)(2,1)}, f32[8,128]{1,0:T(8,128)}) custom-call(s32[1]{0:T(128)} %bitcast.3.base_ref, s32[4,704,1]{2,1,0:T(8,128)} %broadcast_select_fusion.pos_ref.refs_10_, bf16[700,1400]{1,0:T(8,128)(2,1)} %refs_0_.1), custom_call_target="tpu_custom_call" | custom-call | flops 5519360000 | bytes 15769600 | tf_op jit(solution)/shard_map/pallas_call | solution.py:82
  27.3 9.0 %collective-permute-done.refs_2_ = bf16[352,2048]{1,0:T(8,128)(2,1)} collective-permute-done((bf16[352,2048]{1,0:T(8,128)(2,1)S(1)}, bf16[352,2048]{1,0:T(8,128)(2,1)}, u32[]{:S(2)}, u32[]{:S(2)}) %collective-permute-start) | collective-permute-done | bytes 1441824 | tf_op jit(solution)/shard_map/ppermute | solution.py:129
  37.0 1.3 collective-permute-start.10
  38.9 14.6 %collective-permute-done.4.refs_1_ = bf16[700,1400]{1,0:T(8,128)(2,1)} collective-permute-done((bf16[700,1400]{1,0:T(8,128)(2,1)}, bf16[700,1400]{1,0:T(8,128)(2,1)}, u32[]{:S(2)}, u32[]{:S(2)}) %collective-permute-start.4) | collective-permute-done | bytes 1960032 | tf_op jit(solution)/shard_map/ppermute | solution.py:107
  53.5 1.3 slice.12
  55.4 1.3 slice.13
  56.7 1.6 %collective-permute-start.13 = (bf16[348,1400]{1,0:T(8,128)(2,1)S(1)}, bf16[348,1400]{1,0:T(8,128)(2,1)}, u32[]{:S(2)}, u32[]{:S(2)}) collective-permute-start(bf16[348,1400]{1,0:T(8,128)(2,1)S(1)} %slice.13), channel_id=1, source_target_pairs={{0,16},{8,24},{16,0},{24,8},{1,17},{9,25},{17,1},{25,9},{2,18},{10... | collective-permute-start | bytes 2923208 | tf_op jit(solution)/shard_map/ppermute | solution.py:107
  58.3 19.3 %shard_map.47 = (bf16[4,704,1400]{2,1,0:T(8,128)(2,1)}, f32[8,128]{1,0:T(8,128)}) custom-call(s32[2]{0:T(128)} %pad_add_fusion.1.base_ref, s32[4,704,1]{2,1,0:T(8,128)} %broadcast_select_fusion.pos_ref.refs_10_, bf16[700,1400]{1,0:T(8,128)(2,1)} %collective-permute-done.3.refs_0_, ...), custom_call_target="tpu_custom_call", output_to_operand_aliasing={{0}: (4, {})} | custom-call | flops 11038720000 | bytes 15769600 | tf_op jit(solution)/shard_map/pallas_call | solution.py:82
  78.5 1.8 %collective-permute-start.9 = (bf16[352,2048]{1,0:T(8,128)(2,1)}, bf16[352,2048]{1,0:T(8,128)(2,1)}, u32[]{:S(2)}, u32[]{:S(2)}) collective-permute-start(bf16[352,2048]{1,0:T(8,128)(2,1)} %collective-permute-done.1.refs_4_), channel_id=1, source_target_pairs={{2,3},{3,2},{4,5},{5,4},{10,11},{11,10},{12,13},{13,12},{18,19},{1... | collective-permute-start | bytes 4325384 | tf_op jit(solution)/shard_map/ppermute | solution.py:133
  80.3 2.4 %collective-permute-start.11 = (bf16[352,2048]{1,0:T(8,128)(2,1)}, bf16[352,2048]{1,0:T(8,128)(2,1)}, u32[]{:S(2)}, u32[]{:S(2)}) collective-permute-start(bf16[352,2048]{1,0:T(8,128)(2,1)} %collective-permute-done.10.refs_6_), channel_id=1, source_target_pairs={{0,1},{1,0},{6,7},{7,6},{8,9},{9,8},{14,15},{15,14},{16,17},{17,16... | collective-permute-start | bytes 4325384 | tf_op jit(solution)/shard_map/ppermute | solution.py:133
  82.7 1.5 %collective-permute-start.7 = (bf16[352,2048]{1,0:T(8,128)(2,1)S(1)}, bf16[352,2048]{1,0:T(8,128)(2,1)}, u32[]{:S(2)}, u32[]{:S(2)}) collective-permute-start(bf16[352,2048]{1,0:T(8,128)(2,1)S(1)} %collective-permute-done.2.refs_0_), channel_id=1, source_target_pairs={{2,0},{3,1},{4,6},{5,7},{10,8},{11,9},{12,14},{13,15},{18,16},{19,... | collective-permute-start | bytes 4325384 | tf_op jit(solution)/shard_map/ppermute | solution.py:129
  85.9 31.4 %shard_map.48 = (f32[2000,1400]{1,0:T(8,128)}, bf16[704,1400]{1,0:T(8,128)(2,1)}) custom-call(s32[9]{0:T(128)} %stack.57.info_ref, bf16[352,2048]{1,0:T(8,128)(2,1)} %copy-done.1, bf16[352,2048]{1,0:T(8,128)(2,1)} %collective-permute-done.5.refs_4_.refs_1_, bf16[352,2048]{1,0:T(8,128)(2,1)} %collective-permute-done.refs_2_, ...), custom_call_target="tpu_custom_call" | custom-call | flops 5734400 | bytes 11200 | tf_op jit(solution)/shard_map/pallas_call | solution.py:265
  117.4 3.4 %collective-permute-done.7.refs_2_ = bf16[352,2048]{1,0:T(8,128)(2,1)} collective-permute-done((bf16[352,2048]{1,0:T(8,128)(2,1)S(1)}, bf16[352,2048]{1,0:T(8,128)(2,1)}, u32[]{:S(2)}, u32[]{:S(2)}) %collective-permute-start.7) | collective-permute-done | bytes 1441824 | tf_op jit(solution)/shard_map/ppermute | solution.py:129
  120.9 1.9 %collective-permute-start.14 = (bf16[352,2048]{1,0:T(8,128)(2,1)}, bf16[352,2048]{1,0:T(8,128)(2,1)S(1)}, u32[]{:S(2)}, u32[]{:S(2)}) collective-permute-start(bf16[352,2048]{1,0:T(8,128)(2,1)} %collective-permute-done.7.refs_2_), channel_id=1, source_target_pairs={{0,1},{1,0},{6,7},{7,6},{8,9},{9,8},{14,15},{15,14},{16,17},{17,16... | collective-permute-start | bytes 4325384 | tf_op jit(solution)/shard_map/ppermute | solution.py:133
  123.4 2.8 %collective-permute-done.14.refs_3_ = bf16[352,2048]{1,0:T(8,128)(2,1)S(1)} collective-permute-done((bf16[352,2048]{1,0:T(8,128)(2,1)}, bf16[352,2048]{1,0:T(8,128)(2,1)S(1)}, u32[]{:S(2)}, u32[]{:S(2)}) %collective-permute-start.14) | collective-permute-done | bytes 1441824 | tf_op jit(solution)/shard_map/ppermute | solution.py:133
  127.3 14.3 %shard_map.49 = f32[2000,1400]{1,0:T(8,128)} custom-call(s32[2]{0:T(128)} %pad_add_fusion.info_ref, bf16[352,2048]{1,0:T(8,128)(2,1)} %copy-done.2, bf16[352,2048]{1,0:T(8,128)(2,1)} %copy-done, bf16[352,2048]{1,0:T(8,128)(2,1)} %collective-permute-done.7.refs_2_, bf16[352,2048]{1,0:T(8,128)(2,1)} %copy-done.3, ...), custom_call_target="tpu_custom_call", output_to_operand_aliasing={{}: (6, {})} | custom-call | flops 5734400 | bytes 11200 | tf_op jit(solution)/shard_map/pallas_call | solution.py:295
  (43 shorter events, 7.3 us)
Async XLA Ops:
  0.0 9.4 %copy-start.4 = (s32[1400]{0:T(1024)S(1)}, s32[1400]{0:T(1024)}, u32[]{:S(2)}) copy-start(s32[1400]{0:T(1024)} %param.6) | copy-start | bytes 16804
  1.5 15.1 %copy-start.1 = (bf16[352,2048]{1,0:T(8,128)(2,1)}, bf16[352,2048]{1,0:T(8,128)(2,1)S(1)}, u32[]{:S(2)}) copy-start(bf16[352,2048]{1,0:T(8,128)(2,1)S(1)} %pad.8.refs_0_) | copy-start | bytes 4325380
  1.5 34.8 %collective-permute-start = (bf16[352,2048]{1,0:T(8,128)(2,1)S(1)}, bf16[352,2048]{1,0:T(8,128)(2,1)}, u32[]{:S(2)}, u32[]{:S(2)}) collective-permute-start(bf16[352,2048]{1,0:T(8,128)(2,1)S(1)} %pad.8.refs_0_), channel_id=1, source_target_pairs={{0,2},{1,3},{2,0},{3,1},{4,6},{5,7},{6,4},{7,5},{8,10},{9,11},{10,... | collective-permute-start | bytes 4325384 | tf_op jit(solution)/shard_map/ppermute | solution.py:129
  4.6 31.7 %collective-permute-start.1 = (bf16[352,2048]{1,0:T(8,128)(2,1)S(1)}, bf16[352,2048]{1,0:T(8,128)(2,1)}, u32[]{:S(2)}, u32[]{:S(2)}) collective-permute-start(bf16[352,2048]{1,0:T(8,128)(2,1)S(1)} %pad.8.refs_0_), channel_id=1, source_target_pairs={{2,4},{3,5},{4,2},{5,3},{10,12},{11,13},{12,10},{13,11},{18,20},{1... | collective-permute-start | bytes 4325384 | tf_op jit(solution)/shard_map/ppermute | solution.py:129
  6.4 51.9 %collective-permute-start.5 = (bf16[352,2048]{1,0:T(8,128)(2,1)S(1)}, bf16[352,2048]{1,0:T(8,128)(2,1)}, u32[]{:S(2)}, u32[]{:S(2)}) collective-permute-start(bf16[352,2048]{1,0:T(8,128)(2,1)S(1)} %pad.8.refs_0_), channel_id=1, source_target_pairs={{0,1},{1,0},{2,3},{3,2},{4,5},{5,4},{6,7},{7,6},{8,9},{9,8},{10,11... | collective-permute-start | bytes 4325384 | tf_op jit(solution)/shard_map/ppermute | solution.py:133
  6.4 49.0 %collective-permute-start.3 = (bf16[700,1400]{1,0:T(8,128)(2,1)}, bf16[700,1400]{1,0:T(8,128)(2,1)}, u32[]{:S(2)}, u32[]{:S(2)}) collective-permute-start(bf16[700,1400]{1,0:T(8,128)(2,1)} %refs_0_.1), channel_id=1, source_target_pairs={{0,8},{8,0},{16,24},{24,16},{1,9},{9,1},{17,25},{25,17},{2,10},{10... | collective-permute-start | bytes 5880008 | tf_op jit(solution)/shard_map/ppermute | solution.py:107
  7.9 45.6 %collective-permute-start.4 = (bf16[700,1400]{1,0:T(8,128)(2,1)}, bf16[700,1400]{1,0:T(8,128)(2,1)}, u32[]{:S(2)}, u32[]{:S(2)}) collective-permute-start(bf16[700,1400]{1,0:T(8,128)(2,1)} %refs_0_.1), channel_id=1, source_target_pairs={{0,16},{8,24},{16,0},{24,8},{1,17},{9,25},{17,1},{25,9},{2,18},{10... | collective-permute-start | bytes 5880008 | tf_op jit(solution)/shard_map/ppermute | solution.py:107
  36.3 41.4 %collective-permute-start.2 = (bf16[352,2048]{1,0:T(8,128)(2,1)}, bf16[352,2048]{1,0:T(8,128)(2,1)S(1)}, u32[]{:S(2)}, u32[]{:S(2)}) collective-permute-start(bf16[352,2048]{1,0:T(8,128)(2,1)} %collective-permute-done.refs_2_), channel_id=1, source_target_pairs={{2,4},{3,5},{4,2},{5,3},{10,12},{11,13},{12,10},{13,11},{18,20},{1... | collective-permute-start | bytes 4325384 | tf_op jit(solution)/shard_map/ppermute | solution.py:129
  37.0 41.5 %collective-permute-start.10 = (bf16[352,2048]{1,0:T(8,128)(2,1)}, bf16[352,2048]{1,0:T(8,128)(2,1)}, u32[]{:S(2)}, u32[]{:S(2)}) collective-permute-start(bf16[352,2048]{1,0:T(8,128)(2,1)} %collective-permute-done.1.refs_4_), channel_id=1, source_target_pairs={{2,0},{3,1},{4,6},{5,7},{10,8},{11,9},{12,14},{13,15},{18,16},{19,... | collective-permute-start | bytes 4325384 | tf_op jit(solution)/shard_map/ppermute | solution.py:129
  54.8 27.8 %collective-permute-start.12 = (bf16[352,1400]{1,0:T(8,128)(2,1)S(1)}, bf16[352,1400]{1,0:T(8,128)(2,1)}, u32[]{:S(2)}, u32[]{:S(2)}) collective-permute-start(bf16[352,1400]{1,0:T(8,128)(2,1)S(1)} %slice.12), channel_id=1, source_target_pairs={{0,8},{8,0},{16,24},{24,16},{1,9},{9,1},{17,25},{25,17},{2,10},{10... | collective-permute-start | bytes 2956808 | tf_op jit(solution)/shard_map/ppermute | solution.py:107
  56.7 23.6 %collective-permute-start.13 = (bf16[348,1400]{1,0:T(8,128)(2,1)S(1)}, bf16[348,1400]{1,0:T(8,128)(2,1)}, u32[]{:S(2)}, u32[]{:S(2)}) collective-permute-start(bf16[348,1400]{1,0:T(8,128)(2,1)S(1)} %slice.13), channel_id=1, source_target_pairs={{0,16},{8,24},{16,0},{24,8},{1,17},{9,25},{17,1},{25,9},{2,18},{10... | collective-permute-start | bytes 2923208 | tf_op jit(solution)/shard_map/ppermute | solution.py:107
  77.7 39.7 %copy-start.2 = (bf16[352,2048]{1,0:T(8,128)(2,1)}, bf16[352,2048]{1,0:T(8,128)(2,1)S(1)}, u32[]{:S(2)}) copy-start(bf16[352,2048]{1,0:T(8,128)(2,1)S(1)} %collective-permute-done.2.refs_0_) | copy-start | bytes 4325380
  77.7 7.2 %collective-permute-start.6 = (bf16[352,2048]{1,0:T(8,128)(2,1)S(1)}, bf16[352,2048]{1,0:T(8,128)(2,1)S(1)}, u32[]{:S(2)}, u32[]{:S(2)}) collective-permute-start(bf16[352,2048]{1,0:T(8,128)(2,1)S(1)} %collective-permute-done.2.refs_0_), channel_id=1, source_target_pairs={{2,3},{3,2},{4,5},{5,4},{10,11},{11,10},{12,13},{13,12},{18,19},{1... | collective-permute-start | bytes 4325384 | tf_op jit(solution)/shard_map/ppermute | solution.py:133
  78.4 6.4 %collective-permute-start.8 = (bf16[352,2048]{1,0:T(8,128)(2,1)}, bf16[352,2048]{1,0:T(8,128)(2,1)}, u32[]{:S(2)}, u32[]{:S(2)}) collective-permute-start(bf16[352,2048]{1,0:T(8,128)(2,1)} %collective-permute-done.refs_2_), channel_id=1, source_target_pairs={{0,1},{1,0},{2,3},{3,2},{4,5},{5,4},{6,7},{7,6},{8,9},{9,8},{10,11... | collective-permute-start | bytes 4325384 | tf_op jit(solution)/shard_map/ppermute | solution.py:133
  78.5 6.3 %collective-permute-start.9 = (bf16[352,2048]{1,0:T(8,128)(2,1)}, bf16[352,2048]{1,0:T(8,128)(2,1)}, u32[]{:S(2)}, u32[]{:S(2)}) collective-permute-start(bf16[352,2048]{1,0:T(8,128)(2,1)} %collective-permute-done.1.refs_4_), channel_id=1, source_target_pairs={{2,3},{3,2},{4,5},{5,4},{10,11},{11,10},{12,13},{13,12},{18,19},{1... | collective-permute-start | bytes 4325384 | tf_op jit(solution)/shard_map/ppermute | solution.py:133
  80.3 5.6 %collective-permute-start.11 = (bf16[352,2048]{1,0:T(8,128)(2,1)}, bf16[352,2048]{1,0:T(8,128)(2,1)}, u32[]{:S(2)}, u32[]{:S(2)}) collective-permute-start(bf16[352,2048]{1,0:T(8,128)(2,1)} %collective-permute-done.10.refs_6_), channel_id=1, source_target_pairs={{0,1},{1,0},{6,7},{7,6},{8,9},{9,8},{14,15},{15,14},{16,17},{17,16... | collective-permute-start | bytes 4325384 | tf_op jit(solution)/shard_map/ppermute | solution.py:133
  82.7 38.2 %collective-permute-start.7 = (bf16[352,2048]{1,0:T(8,128)(2,1)S(1)}, bf16[352,2048]{1,0:T(8,128)(2,1)}, u32[]{:S(2)}, u32[]{:S(2)}) collective-permute-start(bf16[352,2048]{1,0:T(8,128)(2,1)S(1)} %collective-permute-done.2.refs_0_), channel_id=1, source_target_pairs={{2,0},{3,1},{4,6},{5,7},{10,8},{11,9},{12,14},{13,15},{18,16},{19,... | collective-permute-start | bytes 4325384 | tf_op jit(solution)/shard_map/ppermute | solution.py:129
  84.8 1.1 copy-start
  120.9 5.3 %collective-permute-start.14 = (bf16[352,2048]{1,0:T(8,128)(2,1)}, bf16[352,2048]{1,0:T(8,128)(2,1)S(1)}, u32[]{:S(2)}, u32[]{:S(2)}) collective-permute-start(bf16[352,2048]{1,0:T(8,128)(2,1)} %collective-permute-done.7.refs_2_), channel_id=1, source_target_pairs={{0,1},{1,0},{6,7},{7,6},{8,9},{9,8},{14,15},{15,14},{16,17},{17,16... | collective-permute-start | bytes 4325384 | tf_op jit(solution)/shard_map/ppermute | solution.py:133
  126.2 1.1 copy-start.3

commit v8 on v7

--- a/solution.py
+++ b/solution.py
@@ -217,7 +217,7 @@
         lanes = pl.ds(pl.multiple_of(step * tile, tile), tile)
         for k in range(mine):
 
-            @pl.when(info_ref[1] == k)
+            @pl.when(info_ref[info_ref.shape[0] - 1] == k)
             def _(k=k):
                 for other in range(CORES):
                     place = jnp.where(info_ref[0] == other, 0, depth)
@@ -251,7 +251,7 @@
 
 
 def add_product(info, slots, natural, pos, missing, acc, before):
-    tile = TILE
+    tile = TILE // 2
     depth, lanes = slots[0][0][0].shape
     chips, chip_rows, columns = natural.shape
     arrays = [a for slot in slots for pair in slot for a in pair]
@@ -365,12 +365,13 @@
     if not line:
         return add_product(jnp.stack([*info[:-1], info[0], info[-1]]), slots, natural, pos, missing, residual_in, [token])[0]
     choice, far_chip = info[-3], info[-2]
+    info = jnp.stack([*info[:-3], far_chip, info[-1], choice])
     acc, far_rows = add_product(
-        jnp.stack([*info[:-3], far_chip, info[-1]]), slots, natural, pos, missing, residual_in, [token, d[1]]
+        info, slots, natural, pos, missing, residual_in, [token, d[1]]
     )
     e, acc = lax.optimization_barrier((e, acc))
     e = (e, swap_cores(e, ends))
-    return add_last(jnp.stack([core, choice]), [d, e], far_rows, acc)
+    return add_last(info, [d, e], far_rows, acc)
 
 
 def solution(mesh):

time: 142 us -> 142 us (level)
  no operation moved by 1% of the time
where the time goes in v8:
time: 142 us
  Pallas kernels  75.5 us (53%)
  waiting for transfers between devices  31.8 us (22%)
  starting transfers between devices  20.5 us (14%)
  local copies, waits for them, and re-layouts  8.26 us (6%)
  other arithmetic  5.36 us (4%)
    pallas_call x1, Pallas kernels, add_product(): pl.pallas_call(functools.partial(product_kernel, tuple((len(slot) for slo...  31.1 us
    pallas_call x2, Pallas kernels, add_permuted(): pl.pallas_call(functools.partial(permute_kernel, groups, previous is not...  30.1 us
    ppermute x4, waiting for transfers between devices, send(): return lax.ppermute(array, 'row', [(i, i ^ bit) for i in range(size)])  14.7 us
    pallas_call x1, Pallas kernels, add_last(): pl.pallas_call(functools.partial(last_kernel, len(slot)), grid_spec=pltpu...  14.3 us
    ppermute x5, waiting for transfers between devices, send_chips(): lax.ppermute(block, 'col', [(z * CORES + core, to * CORES + core) for z,...  12.8 us
    ppermute x5, starting transfers between devices, send_chips(): lax.ppermute(block, 'col', [(z * CORES + core, to * CORES + core) for z,...  8.43 us
    ppermute x6, starting transfers between devices, swap_cores(): lax.ppermute(block, 'col', [(z * CORES + core, z * CORES + 1 - core) for...  6.89 us
    ppermute x4, starting transfers between devices, send(): return lax.ppermute(array, 'row', [(i, i ^ bit) for i in range(size)])  5.2 us
  transfers between devices with their start and end apart: 15, of which 5 were waited for; matrix products, arithmetic and copies ran while one was open for 8% of the time, Pallas kernels for 43%

profile of v8, /device:TPU:0, one launch (start us, length us, event | category | flops | bytes accessed | tf_op | source)
XLA Modules:
  0.0 141.7 jit_solution(11057964321196010346)
XLA Ops:
  0.0 1.5 %pad.8.refs_0_ = bf16[352,2048]{1,0:T(8,128)(2,1)S(1)} pad(bf16[350,2000]{1,0:T(8,128)(2,1)} %bitcast.12, bf16[]{:T(256)} %constant.45.clone.1), padding=0_2x0_48 | pad | bytes 2841794 | tf_op jit(solution)/shard_map/jit(_pad)/pad | solution.py:319
  1.5 3.1 %collective-permute-start = (bf16[352,2048]{1,0:T(8,128)(2,1)S(1)}, bf16[352,2048]{1,0:T(8,128)(2,1)}, u32[]{:S(2)}, u32[]{:S(2)}) collective-permute-start(bf16[352,2048]{1,0:T(8,128)(2,1)S(1)} %pad.8.refs_0_), channel_id=1, source_target_pairs={{0,2},{1,3},{2,0},{3,1},{4,6},{5,7},{6,4},{7,5},{8,10},{9,11},{10,... | collective-permute-start | bytes 4325384 | tf_op jit(solution)/shard_map/ppermute | solution.py:129
  4.6 1.8 %collective-permute-start.1 = (bf16[352,2048]{1,0:T(8,128)(2,1)S(1)}, bf16[352,2048]{1,0:T(8,128)(2,1)}, u32[]{:S(2)}, u32[]{:S(2)}) collective-permute-start(bf16[352,2048]{1,0:T(8,128)(2,1)S(1)} %pad.8.refs_0_), channel_id=1, source_target_pairs={{2,4},{3,5},{4,2},{5,3},{10,12},{11,13},{12,10},{13,11},{18,20},{1... | collective-permute-start | bytes 4325384 | tf_op jit(solution)/shard_map/ppermute | solution.py:129
  6.4 1.5 %collective-permute-start.3 = (bf16[700,1400]{1,0:T(8,128)(2,1)}, bf16[700,1400]{1,0:T(8,128)(2,1)}, u32[]{:S(2)}, u32[]{:S(2)}) collective-permute-start(bf16[700,1400]{1,0:T(8,128)(2,1)} %refs_0_.1), channel_id=1, source_target_pairs={{0,8},{8,0},{16,24},{24,16},{1,9},{9,1},{17,25},{25,17},{2,10},{10... | collective-permute-start | bytes 5880008 | tf_op jit(solution)/shard_map/ppermute | solution.py:107
  7.9 1.5 %collective-permute-start.4 = (bf16[700,1400]{1,0:T(8,128)(2,1)}, bf16[700,1400]{1,0:T(8,128)(2,1)}, u32[]{:S(2)}, u32[]{:S(2)}) collective-permute-start(bf16[700,1400]{1,0:T(8,128)(2,1)} %refs_0_.1), channel_id=1, source_target_pairs={{0,16},{8,24},{16,0},{24,8},{1,17},{9,25},{17,1},{25,9},{2,18},{10... | collective-permute-start | bytes 5880008 | tf_op jit(solution)/shard_map/ppermute | solution.py:107
  10.0 3.4 %convert_reduce_fusion = s32[4,704]{1,0:T(4,128)S(1)} fusion(s32[4,704]{1,0:T(4,128)S(1)} %lt.47, s32[2800]{0:T(1024)S(1)} %iota_add_fusion), kind=kLoop, calls=%fused_computation | loop fusion | flops 23651584 | bytes 33728 | tf_op jit(solution)/shard_map/reduce_sum | solution.py:29
  13.9 1.4 lt.50
  15.3 1.3 broadcast_select_fusion.pos_ref.refs_10_
  16.6 10.7 %shard_map.46 = (bf16[4,704,1400]{2,1,0:T(8,128)(2,1)}, f32[8,128]{1,0:T(8,128)}) custom-call(s32[1]{0:T(128)} %bitcast.8.base_ref, s32[4,704,1]{2,1,0:T(8,128)} %broadcast_select_fusion.pos_ref.refs_10_, bf16[700,1400]{1,0:T(8,128)(2,1)} %refs_0_.1), custom_call_target="tpu_custom_call" | custom-call | flops 5519360000 | bytes 15769600 | tf_op jit(solution)/shard_map/pallas_call | solution.py:82
  27.3 9.0 %collective-permute-done.refs_2_ = bf16[352,2048]{1,0:T(8,128)(2,1)} collective-permute-done((bf16[352,2048]{1,0:T(8,128)(2,1)S(1)}, bf16[352,2048]{1,0:T(8,128)(2,1)}, u32[]{:S(2)}, u32[]{:S(2)}) %collective-permute-start) | collective-permute-done | bytes 1441824 | tf_op jit(solution)/shard_map/ppermute | solution.py:129
  37.0 1.3 collective-permute-start.10
  38.9 14.6 %collective-permute-done.4.refs_1_ = bf16[700,1400]{1,0:T(8,128)(2,1)} collective-permute-done((bf16[700,1400]{1,0:T(8,128)(2,1)}, bf16[700,1400]{1,0:T(8,128)(2,1)}, u32[]{:S(2)}, u32[]{:S(2)}) %collective-permute-start.4) | collective-permute-done | bytes 1960032 | tf_op jit(solution)/shard_map/ppermute | solution.py:107
  53.5 1.3 slice.12
  55.4 1.3 slice.13
  56.7 1.6 %collective-permute-start.13 = (bf16[348,1400]{1,0:T(8,128)(2,1)S(1)}, bf16[348,1400]{1,0:T(8,128)(2,1)}, u32[]{:S(2)}, u32[]{:S(2)}) collective-permute-start(bf16[348,1400]{1,0:T(8,128)(2,1)S(1)} %slice.13), channel_id=1, source_target_pairs={{0,16},{8,24},{16,0},{24,8},{1,17},{9,25},{17,1},{25,9},{2,18},{10... | collective-permute-start | bytes 2923208 | tf_op jit(solution)/shard_map/ppermute | solution.py:107
  58.3 19.3 %shard_map.47 = (bf16[4,704,1400]{2,1,0:T(8,128)(2,1)}, f32[8,128]{1,0:T(8,128)}) custom-call(s32[2]{0:T(128)} %pad_add_fusion.base_ref, s32[4,704,1]{2,1,0:T(8,128)} %broadcast_select_fusion.pos_ref.refs_10_, bf16[700,1400]{1,0:T(8,128)(2,1)} %collective-permute-done.3.refs_0_, ...), custom_call_target="tpu_custom_call", output_to_operand_aliasing={{0}: (4, {})} | custom-call | flops 11038720000 | bytes 15769600 | tf_op jit(solution)/shard_map/pallas_call | solution.py:82
  78.5 1.8 %collective-permute-start.9 = (bf16[352,2048]{1,0:T(8,128)(2,1)}, bf16[352,2048]{1,0:T(8,128)(2,1)}, u32[]{:S(2)}, u32[]{:S(2)}) collective-permute-start(bf16[352,2048]{1,0:T(8,128)(2,1)} %collective-permute-done.1.refs_4_), channel_id=1, source_target_pairs={{2,3},{3,2},{4,5},{5,4},{10,11},{11,10},{12,13},{13,12},{18,19},{1... | collective-permute-start | bytes 4325384 | tf_op jit(solution)/shard_map/ppermute | solution.py:133
  80.3 2.4 %collective-permute-start.11 = (bf16[352,2048]{1,0:T(8,128)(2,1)}, bf16[352,2048]{1,0:T(8,128)(2,1)}, u32[]{:S(2)}, u32[]{:S(2)}) collective-permute-start(bf16[352,2048]{1,0:T(8,128)(2,1)} %collective-permute-done.10.refs_6_), channel_id=1, source_target_pairs={{0,1},{1,0},{6,7},{7,6},{8,9},{9,8},{14,15},{15,14},{16,17},{17,16... | collective-permute-start | bytes 4325384 | tf_op jit(solution)/shard_map/ppermute | solution.py:133
  82.7 1.5 %collective-permute-start.7 = (bf16[352,2048]{1,0:T(8,128)(2,1)S(1)}, bf16[352,2048]{1,0:T(8,128)(2,1)}, u32[]{:S(2)}, u32[]{:S(2)}) collective-permute-start(bf16[352,2048]{1,0:T(8,128)(2,1)S(1)} %collective-permute-done.2.refs_0_), channel_id=1, source_target_pairs={{2,0},{3,1},{4,6},{5,7},{10,8},{11,9},{12,14},{13,15},{18,16},{19,... | collective-permute-start | bytes 4325384 | tf_op jit(solution)/shard_map/ppermute | solution.py:129
  86.0 31.1 %shard_map.48 = (f32[2000,1400]{1,0:T(8,128)}, bf16[704,1400]{1,0:T(8,128)(2,1)}) custom-call(s32[10]{0:T(128)} %stack.48.info_ref, bf16[352,2048]{1,0:T(8,128)(2,1)} %copy-done.1, bf16[352,2048]{1,0:T(8,128)(2,1)} %collective-permute-done.5.refs_4_.refs_1_, bf16[352,2048]{1,0:T(8,128)(2,1)} %collective-permute-done.refs_2_, ...), custom_call_target="tpu_custom_call" | custom-call | flops 5734400 | bytes 11200 | tf_op jit(solution)/shard_map/pallas_call | solution.py:265
  117.1 3.8 %collective-permute-done.7.refs_2_ = bf16[352,2048]{1,0:T(8,128)(2,1)} collective-permute-done((bf16[352,2048]{1,0:T(8,128)(2,1)S(1)}, bf16[352,2048]{1,0:T(8,128)(2,1)}, u32[]{:S(2)}, u32[]{:S(2)}) %collective-permute-start.7) | collective-permute-done | bytes 1441824 | tf_op jit(solution)/shard_map/ppermute | solution.py:129
  120.9 1.9 %collective-permute-start.14 = (bf16[352,2048]{1,0:T(8,128)(2,1)}, bf16[352,2048]{1,0:T(8,128)(2,1)S(1)}, u32[]{:S(2)}, u32[]{:S(2)}) collective-permute-start(bf16[352,2048]{1,0:T(8,128)(2,1)} %collective-permute-done.7.refs_2_), channel_id=1, source_target_pairs={{0,1},{1,0},{6,7},{7,6},{8,9},{9,8},{14,15},{15,14},{16,17},{17,16... | collective-permute-start | bytes 4325384 | tf_op jit(solution)/shard_map/ppermute | solution.py:133
  122.8 3.4 %collective-permute-done.14.refs_3_ = bf16[352,2048]{1,0:T(8,128)(2,1)S(1)} collective-permute-done((bf16[352,2048]{1,0:T(8,128)(2,1)}, bf16[352,2048]{1,0:T(8,128)(2,1)S(1)}, u32[]{:S(2)}, u32[]{:S(2)}) %collective-permute-start.14) | collective-permute-done | bytes 1441824 | tf_op jit(solution)/shard_map/ppermute | solution.py:133
  127.3 14.3 %shard_map.49 = f32[2000,1400]{1,0:T(8,128)} custom-call(s32[10]{0:T(128)} %stack.48.info_ref, bf16[352,2048]{1,0:T(8,128)(2,1)} %copy-done.2, bf16[352,2048]{1,0:T(8,128)(2,1)} %copy-done, bf16[352,2048]{1,0:T(8,128)(2,1)} %collective-permute-done.7.refs_2_, bf16[352,2048]{1,0:T(8,128)(2,1)} %copy-done.3, ...), custom_call_target="tpu_custom_call", output_to_operand_aliasing={{}: (6, {})} | custom-call | flops 5734400 | bytes 11200 | tf_op jit(solution)/shard_map/pallas_call | solution.py:295
  (42 shorter events, 6.7 us)
Async XLA Ops:
  0.0 9.4 %copy-start.4 = (s32[1400]{0:T(1024)S(1)}, s32[1400]{0:T(1024)}, u32[]{:S(2)}) copy-start(s32[1400]{0:T(1024)} %param.6) | copy-start | bytes 16804
  1.5 15.1 %copy-start.1 = (bf16[352,2048]{1,0:T(8,128)(2,1)}, bf16[352,2048]{1,0:T(8,128)(2,1)S(1)}, u32[]{:S(2)}) copy-start(bf16[352,2048]{1,0:T(8,128)(2,1)S(1)} %pad.8.refs_0_) | copy-start | bytes 4325380
  1.5 34.8 %collective-permute-start = (bf16[352,2048]{1,0:T(8,128)(2,1)S(1)}, bf16[352,2048]{1,0:T(8,128)(2,1)}, u32[]{:S(2)}, u32[]{:S(2)}) collective-permute-start(bf16[352,2048]{1,0:T(8,128)(2,1)S(1)} %pad.8.refs_0_), channel_id=1, source_target_pairs={{0,2},{1,3},{2,0},{3,1},{4,6},{5,7},{6,4},{7,5},{8,10},{9,11},{10,... | collective-permute-start | bytes 4325384 | tf_op jit(solution)/shard_map/ppermute | solution.py:129
  4.6 31.7 %collective-permute-start.1 = (bf16[352,2048]{1,0:T(8,128)(2,1)S(1)}, bf16[352,2048]{1,0:T(8,128)(2,1)}, u32[]{:S(2)}, u32[]{:S(2)}) collective-permute-start(bf16[352,2048]{1,0:T(8,128)(2,1)S(1)} %pad.8.refs_0_), channel_id=1, source_target_pairs={{2,4},{3,5},{4,2},{5,3},{10,12},{11,13},{12,10},{13,11},{18,20},{1... | collective-permute-start | bytes 4325384 | tf_op jit(solution)/shard_map/ppermute | solution.py:129
  6.4 51.9 %collective-permute-start.5 = (bf16[352,2048]{1,0:T(8,128)(2,1)S(1)}, bf16[352,2048]{1,0:T(8,128)(2,1)}, u32[]{:S(2)}, u32[]{:S(2)}) collective-permute-start(bf16[352,2048]{1,0:T(8,128)(2,1)S(1)} %pad.8.refs_0_), channel_id=1, source_target_pairs={{0,1},{1,0},{2,3},{3,2},{4,5},{5,4},{6,7},{7,6},{8,9},{9,8},{10,11... | collective-permute-start | bytes 4325384 | tf_op jit(solution)/shard_map/ppermute | solution.py:133
  6.4 49.0 %collective-permute-start.3 = (bf16[700,1400]{1,0:T(8,128)(2,1)}, bf16[700,1400]{1,0:T(8,128)(2,1)}, u32[]{:S(2)}, u32[]{:S(2)}) collective-permute-start(bf16[700,1400]{1,0:T(8,128)(2,1)} %refs_0_.1), channel_id=1, source_target_pairs={{0,8},{8,0},{16,24},{24,16},{1,9},{9,1},{17,25},{25,17},{2,10},{10... | collective-permute-start | bytes 5880008 | tf_op jit(solution)/shard_map/ppermute | solution.py:107
  7.9 45.6 %collective-permute-start.4 = (bf16[700,1400]{1,0:T(8,128)(2,1)}, bf16[700,1400]{1,0:T(8,128)(2,1)}, u32[]{:S(2)}, u32[]{:S(2)}) collective-permute-start(bf16[700,1400]{1,0:T(8,128)(2,1)} %refs_0_.1), channel_id=1, source_target_pairs={{0,16},{8,24},{16,0},{24,8},{1,17},{9,25},{17,1},{25,9},{2,18},{10... | collective-permute-start | bytes 5880008 | tf_op jit(solution)/shard_map/ppermute | solution.py:107
  36.3 41.4 %collective-permute-start.2 = (bf16[352,2048]{1,0:T(8,128)(2,1)}, bf16[352,2048]{1,0:T(8,128)(2,1)S(1)}, u32[]{:S(2)}, u32[]{:S(2)}) collective-permute-start(bf16[352,2048]{1,0:T(8,128)(2,1)} %collective-permute-done.refs_2_), channel_id=1, source_target_pairs={{2,4},{3,5},{4,2},{5,3},{10,12},{11,13},{12,10},{13,11},{18,20},{1... | collective-permute-start | bytes 4325384 | tf_op jit(solution)/shard_map/ppermute | solution.py:129
  37.0 41.5 %collective-permute-start.10 = (bf16[352,2048]{1,0:T(8,128)(2,1)}, bf16[352,2048]{1,0:T(8,128)(2,1)}, u32[]{:S(2)}, u32[]{:S(2)}) collective-permute-start(bf16[352,2048]{1,0:T(8,128)(2,1)} %collective-permute-done.1.refs_4_), channel_id=1, source_target_pairs={{2,0},{3,1},{4,6},{5,7},{10,8},{11,9},{12,14},{13,15},{18,16},{19,... | collective-permute-start | bytes 4325384 | tf_op jit(solution)/shard_map/ppermute | solution.py:129
  54.8 27.8 %collective-permute-start.12 = (bf16[352,1400]{1,0:T(8,128)(2,1)S(1)}, bf16[352,1400]{1,0:T(8,128)(2,1)}, u32[]{:S(2)}, u32[]{:S(2)}) collective-permute-start(bf16[352,1400]{1,0:T(8,128)(2,1)S(1)} %slice.12), channel_id=1, source_target_pairs={{0,8},{8,0},{16,24},{24,16},{1,9},{9,1},{17,25},{25,17},{2,10},{10... | collective-permute-start | bytes 2956808 | tf_op jit(solution)/shard_map/ppermute | solution.py:107
  56.7 23.6 %collective-permute-start.13 = (bf16[348,1400]{1,0:T(8,128)(2,1)S(1)}, bf16[348,1400]{1,0:T(8,128)(2,1)}, u32[]{:S(2)}, u32[]{:S(2)}) collective-permute-start(bf16[348,1400]{1,0:T(8,128)(2,1)S(1)} %slice.13), channel_id=1, source_target_pairs={{0,16},{8,24},{16,0},{24,8},{1,17},{9,25},{17,1},{25,9},{2,18},{10... | collective-permute-start | bytes 2923208 | tf_op jit(solution)/shard_map/ppermute | solution.py:107
  77.7 39.4 %copy-start.2 = (bf16[352,2048]{1,0:T(8,128)(2,1)}, bf16[352,2048]{1,0:T(8,128)(2,1)S(1)}, u32[]{:S(2)}) copy-start(bf16[352,2048]{1,0:T(8,128)(2,1)S(1)} %collective-permute-done.2.refs_0_) | copy-start | bytes 4325380
  77.7 7.2 %collective-permute-start.6 = (bf16[352,2048]{1,0:T(8,128)(2,1)S(1)}, bf16[352,2048]{1,0:T(8,128)(2,1)S(1)}, u32[]{:S(2)}, u32[]{:S(2)}) collective-permute-start(bf16[352,2048]{1,0:T(8,128)(2,1)S(1)} %collective-permute-done.2.refs_0_), channel_id=1, source_target_pairs={{2,3},{3,2},{4,5},{5,4},{10,11},{11,10},{12,13},{13,12},{18,19},{1... | collective-permute-start | bytes 4325384 | tf_op jit(solution)/shard_map/ppermute | solution.py:133
  78.4 6.5 %collective-permute-start.8 = (bf16[352,2048]{1,0:T(8,128)(2,1)}, bf16[352,2048]{1,0:T(8,128)(2,1)}, u32[]{:S(2)}, u32[]{:S(2)}) collective-permute-start(bf16[352,2048]{1,0:T(8,128)(2,1)} %collective-permute-done.refs_2_), channel_id=1, source_target_pairs={{0,1},{1,0},{2,3},{3,2},{4,5},{5,4},{6,7},{7,6},{8,9},{9,8},{10,11... | collective-permute-start | bytes 4325384 | tf_op jit(solution)/shard_map/ppermute | solution.py:133
  78.5 6.4 %collective-permute-start.9 = (bf16[352,2048]{1,0:T(8,128)(2,1)}, bf16[352,2048]{1,0:T(8,128)(2,1)}, u32[]{:S(2)}, u32[]{:S(2)}) collective-permute-start(bf16[352,2048]{1,0:T(8,128)(2,1)} %collective-permute-done.1.refs_4_), channel_id=1, source_target_pairs={{2,3},{3,2},{4,5},{5,4},{10,11},{11,10},{12,13},{13,12},{18,19},{1... | collective-permute-start | bytes 4325384 | tf_op jit(solution)/shard_map/ppermute | solution.py:133
  80.3 5.6 %collective-permute-start.11 = (bf16[352,2048]{1,0:T(8,128)(2,1)}, bf16[352,2048]{1,0:T(8,128)(2,1)}, u32[]{:S(2)}, u32[]{:S(2)}) collective-permute-start(bf16[352,2048]{1,0:T(8,128)(2,1)} %collective-permute-done.10.refs_6_), channel_id=1, source_target_pairs={{0,1},{1,0},{6,7},{7,6},{8,9},{9,8},{14,15},{15,14},{16,17},{17,16... | collective-permute-start | bytes 4325384 | tf_op jit(solution)/shard_map/ppermute | solution.py:133
  82.7 38.2 %collective-permute-start.7 = (bf16[352,2048]{1,0:T(8,128)(2,1)S(1)}, bf16[352,2048]{1,0:T(8,128)(2,1)}, u32[]{:S(2)}, u32[]{:S(2)}) collective-permute-start(bf16[352,2048]{1,0:T(8,128)(2,1)S(1)} %collective-permute-done.2.refs_0_), channel_id=1, source_target_pairs={{2,0},{3,1},{4,6},{5,7},{10,8},{11,9},{12,14},{13,15},{18,16},{19,... | collective-permute-start | bytes 4325384 | tf_op jit(solution)/shard_map/ppermute | solution.py:129
  84.9 1.1 copy-start
  120.9 5.3 %collective-permute-start.14 = (bf16[352,2048]{1,0:T(8,128)(2,1)}, bf16[352,2048]{1,0:T(8,128)(2,1)S(1)}, u32[]{:S(2)}, u32[]{:S(2)}) collective-permute-start(bf16[352,2048]{1,0:T(8,128)(2,1)} %collective-permute-done.7.refs_2_), channel_id=1, source_target_pairs={{0,1},{1,0},{6,7},{7,6},{8,9},{9,8},{14,15},{15,14},{16,17},{17,16... | collective-permute-start | bytes 4325384 | tf_op jit(solution)/shard_map/ppermute | solution.py:133
  126.2 1.1 copy-start.3
